TPU v7x, 32 devices: a whole 2x2x4 slice. The times are simulated.
32 devices in a mesh: replica: 8 (over y, x, core), shard: 4 (over z).
Axes of the slice: x: 2, y: 2, z: 4, core: 2. Of those that a mesh axis runs over, the one named last changes fastest.
Arguments:
- tokens: bfloat16 [6144, 2048], P(('replica', 'shard')), may hold values from -6 to 6
- cotangent: bfloat16 [6144, 2048], P(('replica', 'shard')), may hold values from -6 to 6
- qkv_weight: bfloat16 [2048, 6144], P('shard'), may hold values from -0.125 to 0.125
- qkv_bias: bfloat16 [6144], P('shard'), may hold values from -3 to 3
- out_weight: bfloat16 [2048, 2048], P('shard'), may hold values from -1 to 1
- gate_up_weight: bfloat16 [2048, 11264], P('shard'), may hold values from -0.125 to 0.125
- down_weight: bfloat16 [5632, 2048], P('shard'), may hold values from -0.078125 to 0.078125
- norm1_gain: bfloat16 [2048], P('shard'), may hold values from 0.5 to 1.5
- norm1_shift: bfloat16 [2048], P('shard'), may hold values from -1 to 1
- norm2_gain: bfloat16 [2048], P('shard'), may hold values from 0.5 to 1.5
- norm2_shift: bfloat16 [2048], P('shard'), may hold values from -1 to 1
- seq_lengths: int32 [8, 3], P('replica'), may hold values from 1 to 766, as said below
Outputs:
- mixed: bfloat16 [6144, 2048], P(('replica', 'shard'))
- input_grad: float32 [6144, 2048], P(('replica', 'shard'))
- qkv_weight_grad: float32 [2048, 6144], P('shard')
- qkv_bias_grad: float32 [6144], P('shard')
- out_weight_grad: float32 [2048, 2048], P('shard')
- gate_up_weight_grad: float32 [2048, 11264], P('shard')
- down_weight_grad: float32 [5632, 2048], P('shard')
- norm1_gain_grad: float32 [2048], P('shard')
- norm1_shift_grad: float32 [2048], P('shard')
- norm2_gain_grad: float32 [2048], P('shard')
- norm2_shift_grad: float32 [2048], P('shard')
Inputs may be any that keep to these rules, and one draw needn't show every extreme that they name: `seq_lengths`: each row lists the lengths of the 3 sequences of one group of 768 tokens; they sum to 768 and one of them is longer than 384.
All inputs are finite; a program needn't handle non-finite values.
Results may differ from a plain program's by a relative error of at most 0.02.
Values may be sent and summed in bfloat16 or wider, within the bound.
A program may use at most 512 MiB of HBM per device.

v0:
```python
import jax
import jax.numpy as jnp
from jax import lax
from jax.sharding import PartitionSpec as P

D = 2048
FF = 5632
HEADS = 32
HEAD_DIM = 64
ROT_DIM = 16


norm_eps = 1e-05
masked_score = -1000000000.0


def layer_norm(values, norm_gain, norm_shift):
    centered = values - jnp.mean(values, axis=-1, keepdims=True)
    spread = jnp.mean(centered * centered, axis=-1, keepdims=True)
    return centered * lax.rsqrt(spread + norm_eps) * norm_gain + norm_shift


def group_layout(lengths, token_index):
    seq_ends = jnp.cumsum(lengths)
    passed = (token_index[:, None] >= seq_ends[None, :]).astype(jnp.int32)
    segment = jnp.sum(passed, axis=1)
    position = token_index - jnp.sum(passed * lengths[None, :], axis=1)
    return (segment, position)


def rope_tables(position):
    half_rot = ROT_DIM // 2
    frequency = jnp.exp(
        -jnp.log(10000.0) * (2.0 * jnp.arange(half_rot, dtype=jnp.float32) / ROT_DIM)
    )
    angles = position.astype(jnp.float32)[:, None] * frequency[None, :]
    return (jnp.cos(angles), jnp.sin(angles))


def rotate(heads, cosine, sine_value):
    half_rot = ROT_DIM // 2
    first = heads[..., :half_rot]
    second = heads[..., half_rot:ROT_DIM]
    cos_wide = cosine[:, None, :]
    sin_wide = sine_value[:, None, :]
    return jnp.concatenate(
        [
            first * cos_wide - second * sin_wide,
            second * cos_wide + first * sin_wide,
            heads[..., ROT_DIM:],
        ],
        axis=-1,
    )


def head_block():
    return 8


def split_heads(array):
    return jnp.moveaxis(
        array.reshape(array.shape[0], HEADS // head_block(), head_block(), HEAD_DIM), 1, 0
    )


def join_heads(array):
    return jnp.moveaxis(array, 0, 1).reshape(array.shape[1], D)


def contract_last(left, right):
    return lax.dot_general(
        left, right, (((1,), (1,)), ((), ())), preferred_element_type=jnp.float32
    )


def contract_first(left, right):
    return lax.dot_general(
        left, right, (((0,), (0,)), ((), ())), preferred_element_type=jnp.float32
    )


def weight_term(left, right):
    return contract_first(left, right)


def block_scores(query, key_group, visible):
    scores = jnp.einsum(
        "qhd,khd->hqk", query, key_group, preferred_element_type=jnp.float32
    ) * HEAD_DIM ** (-0.5)
    return jnp.where(visible[None], scores, masked_score)


def attend(query, key_group, value_group, visible):
    scores = block_scores(query, key_group, visible)
    top = jnp.max(scores, axis=-1, keepdims=True)
    weights = jnp.exp(scores - top)
    totals = jnp.sum(weights, axis=-1, keepdims=True)
    probs = weights / totals
    context = jnp.einsum(
        "hqk,khd->qhd", probs.astype(jnp.bfloat16), value_group, preferred_element_type=jnp.float32
    )
    return (context, top, totals)


def attend_back(query, key_group, value_group, top, totals, d_context, visible):
    scores = block_scores(query, key_group, visible)
    probs = jnp.exp(scores - top) / totals
    d_probs = jnp.einsum("qhd,khd->hqk", d_context, value_group, preferred_element_type=jnp.float32)
    inner = jnp.sum(probs * d_probs, axis=-1, keepdims=True)
    d_scores = (probs * (d_probs - inner)).astype(jnp.bfloat16)
    scale = HEAD_DIM ** (-0.5)
    d_query = (
        jnp.einsum("hqk,khd->qhd", d_scores, key_group, preferred_element_type=jnp.float32) * scale
    )
    d_key = jnp.einsum("hqk,qhd->khd", d_scores, query, preferred_element_type=jnp.float32) * scale
    d_value = jnp.einsum(
        "hqk,qhd->khd", probs.astype(jnp.bfloat16), d_context, preferred_element_type=jnp.float32
    )
    return (d_query, d_key, d_value)


def swiglu(gate_up):
    return jax.nn.silu(gate_up[:, :FF]) * gate_up[:, FF:]


def on_device(
    tokens,
    cotangent,
    qkv_weight,
    qkv_bias,
    out_weight,
    gate_up_weight,
    down_weight,
    norm1_gain,
    norm1_shift,
    norm2_gain,
    norm2_shift,
    seq_lengths,
):
    gathered = (
        lax.all_gather(qkv_weight, "shard", axis=0, tiled=True),
        lax.all_gather(out_weight, "shard", axis=0, tiled=True),
        lax.all_gather(gate_up_weight, "shard", axis=0, tiled=True),
        lax.all_gather(down_weight, "shard", axis=0, tiled=True),
        lax.all_gather(qkv_bias, "shard", axis=0, tiled=True),
        lax.all_gather(norm1_gain, "shard", axis=0, tiled=True),
        lax.all_gather(norm1_shift, "shard", axis=0, tiled=True),
        lax.all_gather(norm2_gain, "shard", axis=0, tiled=True),
        lax.all_gather(norm2_shift, "shard", axis=0, tiled=True),
    )
    weight_qkv, weight_out, weight_gate_up, weight_down = (
        gathered[0],
        gathered[1],
        gathered[2],
        gathered[3],
    )
    bias_full = gathered[4].astype(jnp.float32)
    gain_one = gathered[5].astype(jnp.float32)
    shift_one = gathered[6].astype(jnp.float32)
    gain_two = gathered[7].astype(jnp.float32)
    shift_two = gathered[8].astype(jnp.float32)
    row_count = tokens.shape[0]
    group_rows = row_count * lax.axis_size("shard")
    local_index = lax.axis_index("shard") * row_count + jnp.arange(row_count, dtype=jnp.int32)
    key_index = jnp.arange(group_rows, dtype=jnp.int32)
    lengths = seq_lengths[0]
    local_segment, local_position = group_layout(lengths, local_index)
    key_segment, key_position = group_layout(lengths, key_index)
    visible = (key_index[None, :] <= local_index[:, None]) & (
        key_segment[None, :] == local_segment[:, None]
    )
    cosine, sine_value = rope_tables(local_position)
    inputs = tokens.astype(jnp.float32)
    normed, norm_one_pull = jax.vjp(layer_norm, inputs, gain_one, shift_one)
    normed_low = normed.astype(jnp.bfloat16)
    projected = jnp.dot(normed_low, weight_qkv, preferred_element_type=jnp.float32) + bias_full
    query_low = (
        rotate(projected[:, :D].reshape(row_count, HEADS, HEAD_DIM), cosine, sine_value)
        .astype(jnp.bfloat16)
        .reshape(row_count, D)
    )
    key_low = (
        rotate(projected[:, D : 2 * D].reshape(row_count, HEADS, HEAD_DIM), cosine, sine_value)
        .astype(jnp.bfloat16)
        .reshape(row_count, D)
    )
    value_low = projected[:, 2 * D :].astype(jnp.bfloat16)
    key_group, value_group = (
        lax.all_gather(key_low, "shard", axis=0, tiled=True),
        lax.all_gather(value_low, "shard", axis=0, tiled=True),
    )
    query_blocks = split_heads(query_low)
    key_blocks = split_heads(key_group)
    value_blocks = split_heads(value_group)

    def forward_block(pieces):
        return attend(pieces[0], pieces[1], pieces[2], visible)

    context, tops, totals = lax.map(forward_block, (query_blocks, key_blocks, value_blocks))
    attended = join_heads(context).astype(jnp.bfloat16)
    middle = inputs + jnp.dot(attended, weight_out, preferred_element_type=jnp.float32)
    normed_two, norm_two_pull = jax.vjp(layer_norm, middle, gain_two, shift_two)
    normed_two_low = normed_two.astype(jnp.bfloat16)
    gate_up = jnp.dot(normed_two_low, weight_gate_up, preferred_element_type=jnp.float32)
    hidden, swiglu_pull = jax.vjp(swiglu, gate_up)
    hidden_low = hidden.astype(jnp.bfloat16)
    mixed = (middle + jnp.dot(hidden_low, weight_down, preferred_element_type=jnp.float32)).astype(
        jnp.bfloat16
    )
    again = (
        lax.all_gather(qkv_weight, "shard", axis=0, tiled=True),
        lax.all_gather(out_weight, "shard", axis=0, tiled=True),
        lax.all_gather(gate_up_weight, "shard", axis=0, tiled=True),
        lax.all_gather(down_weight, "shard", axis=0, tiled=True),
        lax.all_gather(qkv_bias, "shard", axis=0, tiled=True),
        lax.all_gather(norm1_gain, "shard", axis=0, tiled=True),
        lax.all_gather(norm1_shift, "shard", axis=0, tiled=True),
        lax.all_gather(norm2_gain, "shard", axis=0, tiled=True),
        lax.all_gather(norm2_shift, "shard", axis=0, tiled=True),
    )
    back_qkv, back_out, back_gate_up, back_down = (again[0], again[1], again[2], again[3])
    upstream = cotangent.astype(jnp.float32)
    down_term = lax.psum_scatter(
        weight_term(hidden_low, cotangent).astype(jnp.bfloat16),
        "shard",
        scatter_dimension=0,
        tiled=True,
    )
    d_hidden = contract_last(cotangent, back_down)
    d_gate_up_low = swiglu_pull(d_hidden)[0].astype(jnp.bfloat16)
    gate_up_term = lax.psum_scatter(
        weight_term(normed_two_low, d_gate_up_low).astype(jnp.bfloat16),
        "shard",
        scatter_dimension=0,
        tiled=True,
    )
    d_normed_two = contract_last(d_gate_up_low, back_gate_up)
    d_middle_norm, d_gain_two, d_shift_two = norm_two_pull(d_normed_two)
    d_middle = upstream + d_middle_norm
    d_middle_low = d_middle.astype(jnp.bfloat16)
    out_term = lax.psum_scatter(
        weight_term(attended, d_middle_low).astype(jnp.bfloat16),
        "shard",
        scatter_dimension=0,
        tiled=True,
    )
    d_context_low = contract_last(d_middle_low, back_out).astype(jnp.bfloat16)

    def backward_block(pieces):
        return attend_back(
            pieces[0], pieces[1], pieces[2], pieces[3], pieces[4], pieces[5], visible
        )

    d_query, d_key, d_value = lax.map(
        backward_block,
        (query_blocks, key_blocks, value_blocks, tops, totals, split_heads(d_context_low)),
    )
    key_value_terms = jnp.concatenate([join_heads(d_key), join_heads(d_value)], axis=1)
    key_value_own = lax.psum_scatter(
        key_value_terms.astype(jnp.bfloat16), "shard", scatter_dimension=0, tiled=True
    ).astype(jnp.float32)
    d_query_flat = rotate(
        join_heads(d_query).reshape(row_count, HEADS, HEAD_DIM), cosine, -sine_value
    ).reshape(row_count, D)
    d_key_flat = rotate(
        key_value_own[:, :D].reshape(row_count, HEADS, HEAD_DIM), cosine, -sine_value
    ).reshape(row_count, D)
    d_projected_low = jnp.concatenate(
        [d_query_flat, d_key_flat, key_value_own[:, D:]], axis=1
    ).astype(jnp.bfloat16)
    qkv_term = lax.psum_scatter(
        weight_term(normed_low, d_projected_low).astype(jnp.bfloat16),
        "shard",
        scatter_dimension=0,
        tiled=True,
    )
    d_normed = contract_last(d_projected_low, back_qkv)
    d_input_norm, d_gain_one, d_shift_one = norm_one_pull(d_normed)
    input_grad = d_middle + d_input_norm
    bias_local = jnp.sum(d_projected_low.astype(jnp.float32), axis=0)
    vector_own = (
        lax.psum_scatter(
            bias_local.astype(jnp.bfloat16), "shard", scatter_dimension=0, tiled=True
        ).astype(jnp.float32),
        lax.psum_scatter(
            d_gain_one.astype(jnp.bfloat16), "shard", scatter_dimension=0, tiled=True
        ).astype(jnp.float32),
        lax.psum_scatter(
            d_shift_one.astype(jnp.bfloat16), "shard", scatter_dimension=0, tiled=True
        ).astype(jnp.float32),
        lax.psum_scatter(
            d_gain_two.astype(jnp.bfloat16), "shard", scatter_dimension=0, tiled=True
        ).astype(jnp.float32),
        lax.psum_scatter(
            d_shift_two.astype(jnp.bfloat16), "shard", scatter_dimension=0, tiled=True
        ).astype(jnp.float32),
    )
    summed = (
        lax.psum(qkv_term, "replica").astype(jnp.float32),
        lax.psum(vector_own[0].astype(jnp.bfloat16), "replica").astype(jnp.float32),
        lax.psum(out_term, "replica").astype(jnp.float32),
        lax.psum(gate_up_term, "replica").astype(jnp.float32),
        lax.psum(down_term, "replica").astype(jnp.float32),
        lax.psum(vector_own[1].astype(jnp.bfloat16), "replica").astype(jnp.float32),
        lax.psum(vector_own[2].astype(jnp.bfloat16), "replica").astype(jnp.float32),
        lax.psum(vector_own[3].astype(jnp.bfloat16), "replica").astype(jnp.float32),
        lax.psum(vector_own[4].astype(jnp.bfloat16), "replica").astype(jnp.float32),
    )
    return (
        mixed,
        input_grad,
        summed[0],
        summed[1],
        summed[2],
        summed[3],
        summed[4],
        summed[5],
        summed[6],
        summed[7],
        summed[8],
    )


def solution(mesh):
    placed = (
        P(("replica", "shard"), None),
        P(("replica", "shard"), None),
        P("shard", None),
        P("shard"),
        P("shard", None),
        P("shard", None),
        P("shard", None),
        P("shard"),
        P("shard"),
        P("shard"),
        P("shard"),
        P("replica", None),
    )
    return jax.shard_map(
        on_device,
        mesh=mesh,
        in_specs=placed,
        out_specs=(
            P(("replica", "shard"), None),
            P(("replica", "shard"), None),
            P("shard", None),
            P("shard"),
            P("shard", None),
            P("shard", None),
            P("shard", None),
            P("shard"),
            P("shard"),
            P("shard"),
            P("shard"),
        ),
        check_vma=False,
    )
```

profile of v0, /device:TPU:9, one launch (start us, length us, event | category | flops | bytes accessed | tf_op | source)
XLA Modules:
  0.0 4171.4 jit_solution(2266054848997949200)
XLA Ops:
  27.9 37.7 all-gather
  66.8 366.6 %all-gather.12.cloned.1.call-done = bf16[2048,6144]{1,0:T(8,128)(2,1)} async-done(((bf16[512,6144]{1,0:T(8,128)(2,1)}), bf16[2048,6144]{1,0:T(8,128)(2,1)}) %all-gather.12.cloned.1.call-update) | async-done | bytes 25165840 | tf_op jit(solution)/shard_map/all_gather | solution.py:141
  485.8 24.2 all-gather.14.cloned.1.call-done
  514.7 59.7 %all-gather.16.cloned.1.call-done = bf16[768,2048]{1,0:T(8,128)(2,1)} async-done(((bf16[192,2048]{1,0:T(8,128)(2,1)}), bf16[768,2048]{1,0:T(8,128)(2,1)}) %all-gather.16.cloned.1.call-update) | async-done | bytes 3145744 | tf_op jit(solution)/shard_map/all_gather | solution.py:189
  577.5 28.3 while.32
  605.8 117.9 %all-gather.18.cloned.1.call-done = bf16[2048,2048]{1,0:T(8,128)(2,1)} async-done(((bf16[512,2048]{1,0:T(8,128)(2,1)}), bf16[2048,2048]{1,0:T(8,128)(2,1)}) %all-gather.18.cloned.1.call-update) | async-done | bytes 8388624 | tf_op jit(solution)/shard_map/all_gather | solution.py:142
  729.8 761.4 %all-gather.20.cloned.1.call-done = bf16[2048,11264]{1,0:T(8,128)(2,1)} async-done(((bf16[512,11264]{1,0:T(8,128)(2,1)}), bf16[2048,11264]{1,0:T(8,128)(2,1)}) %all-gather.20.cloned.1.call-update) | async-done | bytes 46137360 | tf_op jit(solution)/shard_map/all_gather | solution.py:143
  1491.1 24.7 fusion.78
  1515.8 366.2 %all-gather.22.cloned.1.call-done = bf16[5632,2048]{1,0:T(8,128)(2,1)} async-done(((bf16[1408,2048]{1,0:T(8,128)(2,1)}), bf16[5632,2048]{1,0:T(8,128)(2,1)}) %all-gather.22.cloned.1.call-update) | async-done | bytes 23068688 | tf_op jit(solution)/shard_map/all_gather | solution.py:144
  1882.0 18.3 fusion.65
  1900.3 24.2 multiply_reduce_fusion.1
  1937.5 43.0 %while.33 = (s32[]{:T(128)}, f32[4,192,8,64]{1,3,2,0:T(8,128)}, bf16[4,768,8,64]{1,3,2,0:T(8,128)(2,1)}, bf16[4,768,8,64]{1,3,2,0:T(8,128)(2,1)}, bf16[4,768,8,6...) while((s32[]{:T(128)}, f32[4,192,8,64]{1,3,2,0:T(8,128)}, ...), condition=%wide.region_16.17_spmd.clone.clone, body=%wide.region_14.16_spmd.clone.sunk.clone | while | flops 767703552 | bytes 108885816 | solution.py:254
  2019.2 87.8 %reduce-scatter.16.cloned.1.call-done = bf16[192,4096]{1,0:T(8,128)(2,1)} async-done(((bf16[768,4096]{1,0:T(8,128)(2,1)}), bf16[192,4096]{1,0:T(8,128)(2,1)}) %reduce-scatter.16.cloned.1.call-update) | async-done | bytes 1572880
  2118.6 14.6 convolution_convert_fusion.2
  2133.8 22.5 convolution_convert_fusion
  2156.4 98.2 %reduce-scatter.10.cloned.1.call-done = bf16[512,2048]{1,0:T(8,128)(2,1)} async-done(((bf16[2048,2048]{1,0:T(8,128)(2,1)}), bf16[512,2048]{1,0:T(8,128)(2,1)}) %reduce-scatter.10.cloned.1.call-update) | async-done | bytes 2097168 | tf_op jit(solution)/shard_map/reduce_scatter | solution.py:241
  2254.7 384.3 %reduce-scatter.14.cloned.1.call-done = bf16[1408,2048]{1,0:T(8,128)(2,1)} async-done(((bf16[5632,2048]{1,0:T(8,128)(2,1)}), bf16[1408,2048]{1,0:T(8,128)(2,1)}) %reduce-scatter.14.cloned.1.call-update) | async-done | bytes 5767184 | tf_op jit(solution)/shard_map/reduce_scatter | solution.py:223
  2639.0 418.6 %reduce-scatter.8.cloned.1.call-done = bf16[512,6144]{1,0:T(8,128)(2,1)} async-done(((bf16[2048,6144]{1,0:T(8,128)(2,1)}), bf16[512,6144]{1,0:T(8,128)(2,1)}) %reduce-scatter.8.cloned.1.call-update) | async-done | bytes 6291472 | tf_op jit(solution)/shard_map/reduce_scatter | solution.py:271
  3057.6 754.8 %reduce-scatter.12.cloned.1.call-done = bf16[512,11264]{1,0:T(8,128)(2,1)} async-done(((bf16[2048,11264]{1,0:T(8,128)(2,1)}), bf16[512,11264]{1,0:T(8,128)(2,1)}) %reduce-scatter.12.cloned.1.call-update) | async-done | bytes 11534352 | tf_op jit(solution)/shard_map/reduce_scatter | solution.py:231
  3814.9 13.7 fusion.51
  3828.7 14.7 fusion.79
  3846.8 16.6 all-reduce.9
  3863.9 16.0 all-reduce.7
  3886.7 250.5 %all-reduce.12.cloned.1.call-done = (bf16[512,6144]{1,0:T(8,128)(2,1)}, bf16[512,2048]{1,0:T(8,128)(2,1)}, bf16[512,11264]{1,0:T(8,128)(2,1)}, bf16[1408,2048]{1,0:T(8,128)(2,1)}) async-done(((bf16[512,6144]{1,0:T(8,128)(2,1)}, bf16[512,2048]{1,0:T(8,128)(2,1)}, bf16[512,11264]{1,0:T(8,128)(2,1)}, bf16[1408,2048]{1,0:T(8,128)(2,1)}), (bf16[512,6144]{1,0:T(8,128)(2,1)}, bf16[512,2048]{1,0:T(8,128)(2,1)}, ...) | async-done | bytes 25690128 | tf_op jit(solution)/shard_map/psum | solution.py:299
  (311 shorter events, 261.2 us)
Async XLA Ops:
  7.2 20.7 copy-start.43
  7.2 58.4 %copy-start.2 = (bf16[192,2048]{1,0:T(8,128)(2,1)S(1)}, bf16[192,2048]{1,0:T(8,128)(2,1)}, u32[]{:S(2)}) copy-start(bf16[192,2048]{1,0:T(8,128)(2,1)} %param.16) | copy-start | bytes 2359300
  7.2 426.2 %all-gather.12.cloned.1.call-start = ((), (), s32[]{:S(2)}) async-start(), calls=%async_computation.5 | async-start | bytes 31457280 | tf_op jit(solution)/shard_map/all_gather | solution.py:141
  8.0 502.1 %all-gather.14.cloned.1.call-start = ((), (), s32[]{:S(2)}) async-start(), calls=%async_computation.6 | async-start | bytes 3932160 | tf_op jit(solution)/shard_map/all_gather | solution.py:190
  27.9 416.5 %copy-start.26 = (f32[4,1,512]{2,1,0:T(1,128)}, f32[4,1,512]{2,1,0:T(1,128)S(1)}, u32[]{:S(2)}) copy-start(f32[4,1,512]{2,1,0:T(1,128)S(1)} %convert_element_type.186) | copy-start | bytes 24580
  65.6 378.7 %copy-start.24 = (f32[4,1,512]{2,1,0:T(1,128)}, f32[4,1,512]{2,1,0:T(1,128)S(1)}, u32[]{:S(2)}) copy-start(f32[4,1,512]{2,1,0:T(1,128)S(1)} %convert_element_type.185) | copy-start | bytes 24580
  65.8 378.5 %copy-start.28 = (f32[192]{0:T(256)}, f32[192]{0:T(256)S(1)}, u32[]{:S(2)}) copy-start(f32[192]{0:T(256)S(1)} %broadcast_multiply_fusion.1) | copy-start | bytes 2308
  66.8 377.6 %copy-start.30 = (f32[192]{0:T(256)}, f32[192]{0:T(256)S(1)}, u32[]{:S(2)}) copy-start(f32[192]{0:T(256)S(1)} %fusion.69) | copy-start | bytes 2308
  447.6 126.8 %all-gather.16.cloned.1.call-start = ((), (), s32[]{:S(2)}) async-start(), calls=%async_computation.7 | async-start | bytes 3932160 | tf_op jit(solution)/shard_map/all_gather | solution.py:189
  458.7 265.0 %all-gather.18.cloned.1.call-start = ((), (), s32[]{:S(2)}) async-start(), calls=%async_computation.8 | async-start | bytes 10485760 | tf_op jit(solution)/shard_map/all_gather | solution.py:142
  459.3 1031.9 %all-gather.20.cloned.1.call-start = ((), (), s32[]{:S(2)}) async-start(), calls=%async_computation.9 | async-start | bytes 57671680 | tf_op jit(solution)/shard_map/all_gather | solution.py:143
  459.9 1422.1 %all-gather.22.cloned.1.call-start = ((), (), s32[]{:S(2)}) async-start(), calls=%async_computation.10 | async-start | bytes 28835840 | tf_op jit(solution)/shard_map/all_gather | solution.py:144
  460.5 1646.5 %reduce-scatter.16.cloned.1.call-start = ((), (), s32[]{:S(2)}) async-start(), calls=%async_computation.15 | async-start | bytes 7864320
  471.1 1020.1 %copy-start.22 = (f32[4,1,512]{2,1,0:T(1,128)}, f32[4,1,512]{2,1,0:T(1,128)S(1)}, u32[]{:S(2)}) copy-start(f32[4,1,512]{2,1,0:T(1,128)S(1)} %convert_element_type.189) | copy-start | bytes 24580
  605.8 117.9 %copy-start = (bf16[4,768,8,64]{1,3,2,0:T(8,128)(2,1)}, bf16[4,768,8,64]{1,3,2,0:T(8,128)(2,1)S(1)}, u32[]{:S(2)}) copy-start(bf16[4,768,8,64]{1,3,2,0:T(8,128)(2,1)S(1)} %get-tuple-element.594) | copy-start | bytes 9437188
  1491.1 390.9 %copy-start.13 = (bf16[192,2048]{1,0:T(8,128)(2,1)S(1)}, bf16[192,2048]{1,0:T(8,128)(2,1)}, u32[]{:S(2)}) copy-start(bf16[192,2048]{1,0:T(8,128)(2,1)} %param.17) | copy-start | bytes 2359300
  1995.0 259.6 %reduce-scatter.10.cloned.1.call-start = ((), (), s32[]{:S(2)}) async-start(), calls=%async_computation.12 | async-start | bytes 10485760 | tf_op jit(solution)/shard_map/reduce_scatter | solution.py:241
  2003.1 635.9 %reduce-scatter.14.cloned.1.call-start = ((), (), s32[]{:S(2)}) async-start(), calls=%async_computation.14 | async-start | bytes 28835840 | tf_op jit(solution)/shard_map/reduce_scatter | solution.py:223
  2016.7 1040.8 %reduce-scatter.8.cloned.1.call-start = ((), (), s32[]{:S(2)}) async-start(), calls=%async_computation.11 | async-start | bytes 31457280 | tf_op jit(solution)/shard_map/reduce_scatter | solution.py:271
  2133.2 1679.2 %reduce-scatter.12.cloned.1.call-start = ((), (), s32[]{:S(2)}) async-start(), calls=%async_computation.13 | async-start | bytes 57671680 | tf_op jit(solution)/shard_map/reduce_scatter | solution.py:231
  2156.4 1980.9 %all-reduce.12.cloned.1.call-start = ((), (), s32[]{:S(2)}) async-start(), calls=%async_computation.16 | async-start | bytes 51380224 | tf_op jit(solution)/shard_map/psum | solution.py:299
  3828.7 14.8 copy-start.38
  3843.4 39.3 copy-start.8
  3843.4 39.3 copy-start.36
  (62 other events, 208.8 us)
Sparse Core Ops, SparseCore 0:
  9.6 423.6 all-gather.11
  447.7 62.3 all-gather.13
  512.2 62.0 all-gather.15
  575.8 147.9 all-gather.17
  725.1 765.9 all-gather.19
  1492.6 389.3 all-gather.21
  1995.2 111.7 reduce-scatter.15
  2109.9 144.6 reduce-scatter.9
  2257.6 381.3 reduce-scatter.13
  2641.3 416.1 reduce-scatter.7
  3059.9 752.4 reduce-scatter.11
  3817.1 320.0 all-reduce.11
where the time goes:
time: 4180 us; the launch traced here: 4170 us
  waiting for transfers between devices  3690 us (88%)
  matrix products  223 us (5%)
  blocking collectives  111 us (3%)
  other arithmetic  64.7 us (2%)
  local copies, waits for them, and re-layouts  61.8 us (1%)
    all_gather x1, waiting for transfers between devices, on_device(): lax.all_gather(gate_up_weight, 'shard', axis=0, tiled=True)  761 us
    reduce_scatter x1, waiting for transfers between devices, on_device(): lax.psum_scatter(weight_term(normed_two_low, d_gate_up_low).astype(jnp.bf...  755 us
    reduce_scatter x1, waiting for transfers between devices, on_device(): lax.psum_scatter(weight_term(normed_low, d_projected_low).astype(jnp.bflo...  419 us
    reduce_scatter x1, waiting for transfers between devices, on_device(): lax.psum_scatter(weight_term(hidden_low, cotangent).astype(jnp.bfloat16),...  384 us
    all_gather x1, waiting for transfers between devices, on_device(): lax.all_gather(qkv_weight, 'shard', axis=0, tiled=True)  367 us
    all_gather x1, waiting for transfers between devices, on_device(): lax.all_gather(down_weight, 'shard', axis=0, tiled=True)  366 us
    psum x1, waiting for transfers between devices, on_device(): lax.psum(qkv_term, 'replica').astype(jnp.float32)  251 us
    all_gather x1, waiting for transfers between devices, on_device(): lax.all_gather(out_weight, 'shard', axis=0, tiled=True)  118 us
  transfers between devices with their start and end apart: 12, of which 12 were waited for; matrix products, arithmetic and copies ran while one was open for 5% of the time, Pallas kernels for 0%

commit v1 on v0

v1 whole, which is shorter than its diff:
```python
import jax
import jax.numpy as jnp
from jax import lax
from jax.sharding import PartitionSpec as P

D = 2048
FF = 5632
HEADS = 32
HEAD_DIM = 64
ROT_DIM = 16


norm_eps = 1e-05
masked_score = -1000000000.0


def layer_norm(values, norm_gain, norm_shift):
    centered = values - jnp.mean(values, axis=-1, keepdims=True)
    spread = jnp.mean(centered * centered, axis=-1, keepdims=True)
    return centered * lax.rsqrt(spread + norm_eps) * norm_gain + norm_shift


def group_layout(lengths, token_index):
    seq_ends = jnp.cumsum(lengths)
    passed = (token_index[:, None] >= seq_ends[None, :]).astype(jnp.int32)
    segment = jnp.sum(passed, axis=1)
    position = token_index - jnp.sum(passed * lengths[None, :], axis=1)
    return (segment, position)


def rope_tables(position):
    half_rot = ROT_DIM // 2
    frequency = jnp.exp(
        -jnp.log(10000.0) * (2.0 * jnp.arange(half_rot, dtype=jnp.float32) / ROT_DIM)
    )
    angles = position.astype(jnp.float32)[:, None] * frequency[None, :]
    return (jnp.cos(angles), jnp.sin(angles))


def rotate(heads, cosine, sine_value):
    half_rot = ROT_DIM // 2
    first = heads[..., :half_rot]
    second = heads[..., half_rot:ROT_DIM]
    cos_wide = cosine[:, None, :]
    sin_wide = sine_value[:, None, :]
    return jnp.concatenate(
        [
            first * cos_wide - second * sin_wide,
            second * cos_wide + first * sin_wide,
            heads[..., ROT_DIM:],
        ],
        axis=-1,
    )


def contract_last(left, right):
    return lax.dot_general(
        left, right, (((1,), (1,)), ((), ())), preferred_element_type=jnp.float32
    )


def contract_first(left, right):
    return lax.dot_general(
        left, right, (((0,), (0,)), ((), ())), preferred_element_type=jnp.float32
    )


def spread_rows(rows, columns):
    shards = lax.axis_size("shard")
    copies = lax.axis_size("replica")
    own = rows.shape[0] // copies
    start = lax.axis_index("replica") * own
    piece = lax.dynamic_slice_in_dim(rows, start, own, axis=0)
    piece = piece.reshape(own, columns, shards, -1).transpose(2, 0, 1, 3)
    piece = piece.reshape(shards, own, -1)
    moved = lax.all_to_all(piece, "shard", split_axis=0, concat_axis=0, tiled=True)
    full = lax.all_gather(moved, "replica", axis=0, tiled=False)
    return full.transpose(1, 0, 2, 3).reshape(shards * copies * own, -1)


def gather_rows(rows):
    copies = lax.axis_size("replica")
    own = rows.shape[0] // copies
    start = lax.axis_index("replica") * own
    piece = lax.dynamic_slice_in_dim(rows, start, own, axis=0)
    moved = lax.all_gather(piece, "shard", axis=0, tiled=False)
    full = lax.all_gather(moved, "replica", axis=0, tiled=False)
    return full.transpose(1, 0, 2, 3).reshape(-1, rows.shape[1])


def own_rows(features):
    copies = lax.axis_size("replica")
    shards = lax.axis_size("shard")
    count = features.shape[0]
    return (
        features.reshape(count, shards, copies, -1).transpose(0, 2, 1, 3).reshape(count, -1)
    )


def sum_columns(features, slopes, columns):
    shards = lax.axis_size("shard")
    copies = lax.axis_size("replica")
    term = contract_first(own_rows(features), slopes).astype(jnp.bfloat16)
    part = lax.psum_scatter(term, "replica", scatter_dimension=0, tiled=True)
    own = part.shape[0] // shards
    moved = lax.all_to_all(
        part.reshape(shards, own, -1), "shard", split_axis=0, concat_axis=0, tiled=True
    )
    moved = moved.reshape(shards, own, columns, -1).transpose(1, 2, 0, 3).reshape(own, -1)
    return lax.all_gather(moved, "replica", axis=0, tiled=True).astype(jnp.float32)


def block_scores(query, keys, visible):
    scores = (
        jnp.einsum("qhd,khd->hqk", query, keys, preferred_element_type=jnp.float32)
        * HEAD_DIM ** (-0.5)
    )
    return jnp.where(visible[None], scores, masked_score)


def attend(query, keys, values, visible):
    scores = block_scores(query, keys, visible)
    top = jnp.max(scores, axis=-1, keepdims=True)
    weights = jnp.exp(scores - top)
    totals = jnp.sum(weights, axis=-1, keepdims=True)
    probs = weights / totals
    context = jnp.einsum(
        "hqk,khd->qhd", probs.astype(jnp.bfloat16), values, preferred_element_type=jnp.float32
    )
    return (context, top, totals)


def attend_back(query, keys, values, top, totals, d_context, visible):
    scores = block_scores(query, keys, visible)
    probs = jnp.exp(scores - top) / totals
    d_probs = jnp.einsum("qhd,khd->hqk", d_context, values, preferred_element_type=jnp.float32)
    inner = jnp.sum(probs * d_probs, axis=-1, keepdims=True)
    d_scores = (probs * (d_probs - inner)).astype(jnp.bfloat16)
    scale = HEAD_DIM ** (-0.5)
    d_query = (
        jnp.einsum("hqk,khd->qhd", d_scores, keys, preferred_element_type=jnp.float32) * scale
    )
    d_key = jnp.einsum("hqk,qhd->khd", d_scores, query, preferred_element_type=jnp.float32) * scale
    d_value = jnp.einsum(
        "hqk,qhd->khd", probs.astype(jnp.bfloat16), d_context, preferred_element_type=jnp.float32
    )
    return (d_query, d_key, d_value)


def swiglu(gate_up):
    half = gate_up.shape[1] // 2
    return jax.nn.silu(gate_up[:, :half]) * gate_up[:, half:]


def norm_stats(values):
    mean = jnp.mean(values, axis=-1, keepdims=True)
    centered = values - mean
    inverse = lax.rsqrt(jnp.mean(centered * centered, axis=-1, keepdims=True) + norm_eps)
    return centered * inverse, inverse


def norm_back(slope, unit, inverse, gain):
    scaled = slope * gain
    return inverse * (
        scaled
        - jnp.mean(scaled, axis=-1, keepdims=True)
        - unit * jnp.mean(scaled * unit, axis=-1, keepdims=True)
    )


def on_device(
    tokens,
    cotangent,
    qkv_weight,
    qkv_bias,
    out_weight,
    gate_up_weight,
    down_weight,
    norm1_gain,
    norm1_shift,
    norm2_gain,
    norm2_shift,
    seq_lengths,
):
    shards = lax.axis_size("shard")
    here = lax.axis_index("shard")
    row_count = tokens.shape[0]
    group_rows = row_count * shards
    width = D // shards
    local_heads = HEADS // shards
    f32 = jnp.float32
    low = jnp.bfloat16

    vectors = jnp.concatenate([qkv_bias, norm1_gain, norm1_shift, norm2_gain, norm2_shift])
    vectors = lax.all_gather(vectors, "shard", axis=0, tiled=False).astype(f32)
    bias_rows = qkv_bias.shape[0]
    bias_full = vectors[:, :bias_rows].reshape(3, shards, width)
    bias = lax.dynamic_index_in_dim(bias_full, here, axis=1, keepdims=False).reshape(3 * width)
    gain_one, shift_one, gain_two, shift_two = (
        vectors[:, bias_rows + i * width : bias_rows + (i + 1) * width].reshape(D)
        for i in range(4)
    )

    group_tokens = lax.all_gather(tokens, "shard", axis=0, tiled=True)
    weight_qkv = spread_rows(qkv_weight, 3)
    weight_out = gather_rows(out_weight)
    weight_gate_up = spread_rows(gate_up_weight, 2)
    group_cotangent = lax.all_gather(cotangent, "shard", axis=0, tiled=True)

    index = jnp.arange(group_rows, dtype=jnp.int32)
    segment, position = group_layout(seq_lengths[0], index)
    visible = (index[None, :] <= index[:, None]) & (segment[None, :] == segment[:, None])
    cosine, sine_value = rope_tables(position)

    def local(array):
        return lax.dynamic_slice_in_dim(array, here * row_count, row_count, axis=0)

    inputs = group_tokens.astype(f32)
    unit_one, inverse_one = norm_stats(inputs)
    normed_low = (unit_one * gain_one + shift_one).astype(low)
    projected = jnp.dot(normed_low, weight_qkv, preferred_element_type=f32) + bias
    projected = projected.reshape(group_rows, 3, local_heads, HEAD_DIM)
    query = rotate(projected[:, 0], cosine, sine_value).astype(low)
    keys = rotate(projected[:, 1], cosine, sine_value).astype(low)
    values = projected[:, 2].astype(low)
    context, tops, totals = attend(query, keys, values, visible)
    attended = context.reshape(group_rows, width).astype(low)
    attended_full = lax.all_gather(attended, "shard", axis=1, tiled=True)
    middle = inputs + jnp.dot(attended_full, weight_out, preferred_element_type=f32)
    unit_two, inverse_two = norm_stats(middle)
    normed_two_low = (unit_two * gain_two + shift_two).astype(low)
    gate_up = jnp.dot(normed_two_low, weight_gate_up, preferred_element_type=f32)
    hidden, swiglu_pull = jax.vjp(swiglu, gate_up)
    hidden_low = hidden.astype(low)
    down_part = jnp.dot(hidden_low, down_weight, preferred_element_type=f32).astype(low)
    down_own = lax.psum_scatter(down_part, "shard", scatter_dimension=0, tiled=True)
    mixed = (local(middle) + down_own.astype(f32)).astype(low)

    d_hidden = contract_last(group_cotangent, down_weight)
    down_grad = lax.psum(
        contract_first(hidden_low, group_cotangent).astype(low), "replica"
    ).astype(f32)
    d_gate_up_low = swiglu_pull(d_hidden)[0].astype(low)
    d_normed_two_part = contract_last(d_gate_up_low, weight_gate_up).astype(low)
    gate_up_grad = sum_columns(normed_two_low, d_gate_up_low, 2)
    d_normed_two = lax.psum_scatter(
        d_normed_two_part, "shard", scatter_dimension=0, tiled=True
    ).astype(f32)
    unit_two_own = local(unit_two)
    d_middle = cotangent.astype(f32) + norm_back(
        d_normed_two, unit_two_own, local(inverse_two), gain_two
    )
    d_gain_two = jnp.sum(d_normed_two * unit_two_own, axis=0)
    d_shift_two = jnp.sum(d_normed_two, axis=0)
    d_middle_low = d_middle.astype(low)
    d_attended_own = contract_last(d_middle_low, weight_out).astype(low)
    d_attended = lax.all_to_all(
        d_attended_own, "shard", split_axis=1, concat_axis=0, tiled=True
    ).reshape(group_rows, local_heads, HEAD_DIM)
    d_middle_columns = lax.all_to_all(
        d_middle_low, "shard", split_axis=1, concat_axis=0, tiled=True
    )
    out_grad = sum_columns(attended_full, d_middle_columns, 1)
    d_query, d_key, d_value = attend_back(
        query, keys, values, tops, totals, d_attended, visible
    )
    d_projected = jnp.stack(
        [rotate(d_query, cosine, -sine_value), rotate(d_key, cosine, -sine_value), d_value], axis=1
    )
    d_projected_low = d_projected.astype(low).reshape(group_rows, 3 * width)
    d_normed_part = contract_last(d_projected_low, weight_qkv).astype(low)
    qkv_grad = sum_columns(normed_low, d_projected_low, 3)
    d_normed = lax.psum_scatter(
        d_normed_part, "shard", scatter_dimension=0, tiled=True
    ).astype(f32)
    unit_one_own = local(unit_one)
    input_grad = d_middle + norm_back(d_normed, unit_one_own, local(inverse_one), gain_one)
    d_gain_one = jnp.sum(d_normed * unit_one_own, axis=0)
    d_shift_one = jnp.sum(d_normed, axis=0)

    bias_part = jnp.sum(d_projected_low.astype(f32), axis=0).reshape(3, 1, width)
    bias_wide = lax.dynamic_update_slice(
        jnp.zeros((3, shards, width), f32), bias_part, (0, here, 0)
    ).reshape(shards, 3 * width)
    small = jnp.concatenate(
        [bias_wide]
        + [v.reshape(shards, width) for v in (d_gain_one, d_shift_one, d_gain_two, d_shift_two)],
        axis=1,
    )
    small = lax.psum(small, ("replica", "shard"))
    small = lax.dynamic_index_in_dim(small, here, axis=0, keepdims=False)
    return (
        mixed,
        input_grad,
        qkv_grad,
        small[:bias_rows],
        out_grad,
        gate_up_grad,
        down_grad,
    ) + tuple(small[bias_rows + i * width : bias_rows + (i + 1) * width] for i in range(4))


def solution(mesh):
    placed = (
        P(("replica", "shard"), None),
        P(("replica", "shard"), None),
        P("shard", None),
        P("shard"),
        P("shard", None),
        P("shard", None),
        P("shard", None),
        P("shard"),
        P("shard"),
        P("shard"),
        P("shard"),
        P("replica", None),
    )
    return jax.shard_map(
        on_device,
        mesh=mesh,
        in_specs=placed,
        out_specs=(
            P(("replica", "shard"), None),
            P(("replica", "shard"), None),
            P("shard", None),
            P("shard"),
            P("shard", None),
            P("shard", None),
            P("shard", None),
            P("shard"),
            P("shard"),
            P("shard"),
            P("shard"),
        ),
        check_vma=False,
    )
```

time: 4180 us -> 1210 us (0.29)
  waiting for transfers between devices: 3690 us -> 620 us
  blocking collectives: 111 us -> 221 us
  matrix products: 223 us -> 169 us
    all_gather x6 -> x10, waiting for transfers between devices: 1700 us -> 286 us  [the longest x2 93.5 us: spread_rows(): full = lax.all_gather(moved, 'replica', axis=0, tiled=False)]
    reduce_scatter x4 -> x6, waiting for transfers between devices: 1660 us -> 267 us  [the longest x3 92.5 us: sum_columns(): part = lax.psum_scatter(term, 'replica', scatter_dimension=0, tiled=True)]
    psum x1, waiting for transfers between devices: 251 us -> 61.1 us  [on_device(): lax.psum(contract_first(hidden_low, group_cotangent).astype(low), 'replica')]
    all_to_all x0 -> x5, blocking collectives: none -> 169 us  [the longest x2 101 us: spread_rows(): lax.all_to_all(piece, 'shard', split_axis=0, concat_axis=0, tiled=True)]
    unnamed x13 -> x17, waiting for transfers between devices: 90.2 us -> 1.64 us
    all_gather x5 -> x1, blocking collectives: 78.8 us -> 12 us  [on_device(): vectors = lax.all_gather(vectors, 'shard', axis=0, tiled=False).astype(f32)]
    dot_general x24 -> x7, matrix products: 96.6 us -> 62.8 us  [the longest x1 13 us: attend_back(): jnp.einsum('qhd,khd->hqk', d_context, values, preferred_element_type=jnp....]
  transfers between devices with their start and end apart: 12 -> 19, of which waited for: 12 -> 15; matrix products, arithmetic and copies ran while one was open for 5% -> 21% of each run, Pallas kernels for 0% -> 0%
where the time goes in v1:
time: 1210 us; the launch traced here: 1200 us
  waiting for transfers between devices  620 us (51%)
  blocking collectives  221 us (18%)
  matrix products  169 us (14%)
  local copies, waits for them, and re-layouts  84.2 us (7%)
  other arithmetic  78 us (6%)
  between operations  15.4 us (1%)
  starting transfers between devices  12.6 us (1%)
    all_to_all x2, blocking collectives, spread_rows(): lax.all_to_all(piece, 'shard', split_axis=0, concat_axis=0, tiled=True)  101 us
    all_gather x2, waiting for transfers between devices, spread_rows(): full = lax.all_gather(moved, 'replica', axis=0, tiled=False)  93.5 us
    reduce_scatter x3, waiting for transfers between devices, sum_columns(): part = lax.psum_scatter(term, 'replica', scatter_dimension=0, tiled=True)  92.5 us
    all_gather x3, waiting for transfers between devices, sum_columns(): lax.all_gather(moved, 'replica', axis=0, tiled=True).astype(jnp.float32)  87.7 us
    all_to_all x3, blocking collectives, sum_columns(): lax.all_to_all(part.reshape(shards, own, -1), 'shard', split_axis=0, conc...  68.2 us
    psum x1, waiting for transfers between devices, on_device(): lax.psum(contract_first(hidden_low, group_cotangent).astype(low), 'replica')  61.1 us
    reduce_scatter x1, waiting for transfers between devices, on_device(): lax.psum_scatter(d_normed_two_part, 'shard', scatter_dimension=0, tiled=T...  61 us
    reduce_scatter x1, waiting for transfers between devices, on_device(): lax.psum_scatter(d_normed_part, 'shard', scatter_dimension=0, tiled=True)  59.6 us
  transfers between devices with their start and end apart: 19, of which 15 were waited for; matrix products, arithmetic and copies ran while one was open for 21% of the time, Pallas kernels for 0%

profile of v1, /device:TPU:9, one launch (start us, length us, event | category | flops | bytes accessed | tf_op | source)
XLA Modules:
  0.0 1200.2 jit_solution(10549714155116851225)
XLA Ops:
  13.7 38.4 %all_to_all.60 = bf16[4,64,1536]{2,1,0:T(8,128)(2,1)} all-to-all(bf16[4,64,1536]{2,1,0:T(8,128)(2,1)S(1)} %reshape.371), channel_id=1, replica_groups=mesh['replica'=8,'shard'=4] {'shard'}, dimensions={0} | all-to-all | bytes 1572864 | tf_op jit(solution)/shard_map/all_to_all | solution.py:76
  68.2 49.3 %all-gather.17.cloned.1.call-done = bf16[768,2048]{1,0:T(8,128)(2,1)} async-done(((bf16[192,2048]{1,0:T(8,128)(2,1)}), bf16[768,2048]{1,0:T(8,128)(2,1)}) %all-gather.17.cloned.1.call-update) | async-done | bytes 3145744 | tf_op jit(solution)/shard_map/all_gather | solution.py:204
  125.8 40.7 %all-gather.29.cloned.1.call-done = bf16[32,64,1536]{2,1,0:T(8,128)(2,1)} async-done(((bf16[4,64,1536]{2,1,0:T(8,128)(2,1)}), bf16[32,64,1536]{2,1,0:T(8,128)(2,1)}) %all-gather.29.cloned.1.call-update) | async-done | bytes 6291472 | tf_op jit(solution)/shard_map/all_gather | solution.py:77
  214.4 62.5 %all_to_all.61 = bf16[4,64,2816]{2,1,0:T(8,128)(2,1)} all-to-all(bf16[4,64,2816]{2,1,0:T(8,128)(2,1)S(1)} %reshape.379), channel_id=1, replica_groups=mesh['replica'=8,'shard'=4] {'shard'}, dimensions={0} | all-to-all | bytes 2883584 | tf_op jit(solution)/shard_map/all_to_all | solution.py:76
  286.4 14.5 %all-gather.19.cloned.1.call-done = bf16[768,2048]{0,1:T(8,128)(2,1)} async-done(((bf16[768,512]{0,1:T(8,128)(2,1)}), bf16[768,2048]{0,1:T(8,128)(2,1)}) %all-gather.19.cloned.1.call-update) | async-done | bytes 3145744 | tf_op jit(solution)/shard_map/all_gather | solution.py:228
  319.3 52.8 %all-gather.35.cloned.1.call-done = bf16[32,64,2816]{2,1,0:T(8,128)(2,1)} async-done(((bf16[4,64,2816]{2,1,0:T(8,128)(2,1)}), bf16[32,64,2816]{2,1,0:T(8,128)(2,1)}) %all-gather.35.cloned.1.call-update) | async-done | bytes 11534352 | tf_op jit(solution)/shard_map/all_gather | solution.py:77
  394.3 39.9 %all-gather.21.cloned.1.call-done = bf16[768,2048]{1,0:T(8,128)(2,1)} async-done(((bf16[192,2048]{1,0:T(8,128)(2,1)}), bf16[768,2048]{1,0:T(8,128)(2,1)}) %all-gather.21.cloned.1.call-update) | async-done | bytes 3145744 | tf_op jit(solution)/shard_map/all_gather | solution.py:208
  434.3 13.2 %fusion.44 = (f32[768,1408]{1,0:T(8,128)S(1)}, f32[768,1408]{1,0:T(8,128)}, bf16[768,1408]{1,0:T(8,128)(2,1)}) fusion(f32[768,2816]{1,0:T(8,128)} %fusion.57, bf16[768,2048]{1,0:T(8,128)(2,1)} %all-gather.21.cloned.1.call-done, bf16[1408,2048]{1,0:T(8,128)(2,1)} %param.18), kind=kOutput, calls=%fused_computation.88 | convolution fusion | flops 4444323840 | bytes 28377088 | tf_op jit(solution)/shard_map/dot_general | solution.py:57
  449.5 14.9 %convolution_convert_fusion.4 = bf16[768,2048]{1,0:T(8,128)(2,1)} fusion(bf16[2048,2816]{1,0:T(8,128)(2,1)} %bitcast.137, f32[768,1408]{1,0:T(8,128)} %get-tuple-element.26, f32[768,1408]{1,0:T(8,128)S(1)} %get-tuple-element.25), kind=kOutput, calls=%fused_computation.38 | convolution fusion | flops 8864268288 | bytes 23330816 | tf_op jit(solution)/shard_map/dot_general | solution.py:57
  464.4 61.0 %reduce-scatter.9.cloned.1.call-done = bf16[192,2048]{1,0:T(8,128)(2,1)} async-done(((bf16[768,2048]{1,0:T(8,128)(2,1)}), bf16[192,2048]{1,0:T(8,128)(2,1)}) %reduce-scatter.9.cloned.1.call-update) | async-done | bytes 786448 | tf_op jit(solution)/shard_map/reduce_scatter | solution.py:246
  567.5 13.0 %multiply_reduce_fusion = (f32[8,768]{1,0:T(8,128)S(1)}, f32[8,768,768]{1,2,0:T(8,128)}) fusion(f32[8,768,768]{1,2,0:T(8,128)} %get-tuple-element.56, f32[8,768]{1,0:T(8,128)S(1)} %get-tuple-element.55, bf16[768,8,64]{0,2,1:T(8,128)(2,1)S(1)} %reshape.381, f32[768,3,8,64]{0,3,2,1:T(8,128)} %bitcast.132), kind=kOutput, calls=%fused_computation.2 | convolution fusion | flops 618129408 | bytes 39370752 | tf_op jit(solution)/shard_map/qhd,khd->hqk/dot_general | solution.py:136
  580.5 12.9 %multiply_convert_fusion = bf16[8,768,768]{1,2,0:T(8,128)(2,1)S(1)} fusion(f32[8,768,768]{1,2,0:T(8,128)} %get-tuple-element.60, f32[8,768]{1,0:T(8,128)S(1)} %get-tuple-element.59, f32[8,768,768]{1,2,0:T(8,128)} %get-tuple-element.56, f32[8,768]{1,0:T(8,128)S(1)} %get-tuple-element.55), kind=kLoop, calls=%fused_computation.1 | loop fusion | flops 18874368 | bytes 47235072 | tf_op jit(solution)/shard_map/convert_element_type | solution.py:138
  630.7 15.2 %convolution_convert_fusion = bf16[2048,2816]{1,0:T(8,128)(2,1)} fusion(bf16[768,2048]{0,1:T(8,128)(2,1)S(1)} %bitcast.152, f32[768,1408]{1,0:T(8,128)} %get-tuple-element.26, f32[768,1408]{1,0:T(8,128)} %copy-done.49), kind=kOutput, calls=%fused_computation.6 | convolution fusion | flops 8868462592 | bytes 23330816 | tf_op jit(solution)/shard_map/dot_general | solution.py:63
  686.4 26.7 %reduce-scatter.13.cloned.1.call-done = bf16[256,1536]{1,0:T(8,128)(2,1)} async-done(((bf16[2048,1536]{1,0:T(8,128)(2,1)}), bf16[256,1536]{1,0:T(8,128)(2,1)}) %reduce-scatter.13.cloned.1.call-update) | async-done | bytes 786448 | tf_op jit(solution)/shard_map/reduce_scatter | solution.py:104
  713.0 22.0 %all_to_all.63 = bf16[4,64,1536]{2,1,0:T(8,128)(2,1)S(1)} all-to-all(bf16[4,64,1536]{2,1,0:T(8,128)(2,1)} %bitcast.161), channel_id=1, replica_groups=mesh['replica'=8,'shard'=4] {'shard'}, dimensions={0} | all-to-all | bytes 1572864 | tf_op jit(solution)/shard_map/all_to_all | solution.py:106
  738.1 65.8 %reduce-scatter.17.cloned.1.call-done = bf16[256,2816]{1,0:T(8,128)(2,1)} async-done(((bf16[2048,2816]{1,0:T(8,128)(2,1)}), bf16[256,2816]{1,0:T(8,128)(2,1)}) %reduce-scatter.17.cloned.1.call-update) | async-done | bytes 1441808 | tf_op jit(solution)/shard_map/reduce_scatter | solution.py:104
  803.9 36.0 %all_to_all.64 = bf16[4,64,2816]{2,1,0:T(8,128)(2,1)S(1)} all-to-all(bf16[4,64,2816]{2,1,0:T(8,128)(2,1)} %bitcast.156), channel_id=1, replica_groups=mesh['replica'=8,'shard'=4] {'shard'}, dimensions={0} | all-to-all | bytes 2883584 | tf_op jit(solution)/shard_map/all_to_all | solution.py:106
  844.9 61.1 %all-reduce.4.cloned.1.call-done = bf16[1408,2048]{1,0:T(8,128)(2,1)} async-done(((bf16[1408,2048]{1,0:T(8,128)(2,1)}), bf16[1408,2048]{1,0:T(8,128)(2,1)}) %all-reduce.4.cloned.1.call-update) | async-done | bytes 5767184 | tf_op jit(solution)/shard_map/psum | solution.py:240
  914.7 54.3 %reduce-scatter.7.cloned.1.call-done = bf16[192,2048]{1,0:T(8,128)(2,1)} async-done(((bf16[768,2048]{1,0:T(8,128)(2,1)}), bf16[192,2048]{1,0:T(8,128)(2,1)}) %reduce-scatter.7.cloned.1.call-update) | async-done | bytes 786448 | tf_op jit(solution)/shard_map/reduce_scatter | solution.py:236
  971.9 59.6 %reduce-scatter.11.cloned.1.call-done = bf16[192,2048]{1,0:T(8,128)(2,1)} async-done(((bf16[768,2048]{1,0:T(8,128)(2,1)}), bf16[192,2048]{1,0:T(8,128)(2,1)}) %reduce-scatter.11.cloned.1.call-update) | async-done | bytes 786448 | tf_op jit(solution)/shard_map/reduce_scatter | solution.py:273
  1034.0 39.7 %psum.14 = f32[4,3584]{1,0:T(4,128)S(1)} all-reduce(f32[4,3584]{1,0:T(4,128)S(1)} %constant_dynamic-update-slice_fusion), channel_id=1, replica_groups=mesh['replica'=8,'shard'=4] {'replica','shard'}, use_global_device_ids=true, to_apply=%region_23.24 | all-reduce | flops 14336 | bytes 114688 | tf_op jit(solution)/shard_map/psum | solution.py:290
  1083.3 27.3 %all-gather.23.cloned.1.call-done = bf16[512,6144]{1,0:T(8,128)(2,1)} async-done(((bf16[64,6144]{1,0:T(8,128)(2,1)}), bf16[512,6144]{1,0:T(8,128)(2,1)}) %all-gather.23.cloned.1.call-update) | async-done | bytes 6291472 | tf_op jit(solution)/shard_map/all_gather | solution.py:110
  1119.8 60.4 %all-gather.27.cloned.1.call-done = bf16[512,11264]{1,0:T(8,128)(2,1)} async-done(((bf16[64,11264]{1,0:T(8,128)(2,1)}), bf16[512,11264]{1,0:T(8,128)(2,1)}) %all-gather.27.cloned.1.call-update) | async-done | bytes 11534352 | tf_op jit(solution)/shard_map/all_gather | solution.py:110
  1180.2 13.0 %convert_element_type.155 = f32[512,11264]{1,0:T(8,128)} convert(bf16[512,11264]{1,0:T(8,128)(2,1)} %all-gather.27.cloned.1.call-done) | non-fusion elementwise | flops 5767168 | bytes 34603008 | tf_op jit(solution)/shard_map/convert_element_type | solution.py:110
  (258 shorter events, 290.7 us)
Async XLA Ops:
  7.2 45.5 %all-gather.31.cloned.1.call-start = ((), (), s32[]{:S(2)}) async-start(), calls=%async_computation.27 | async-start | bytes 1310720 | tf_op jit(solution)/shard_map/all_gather | solution.py:86
  9.5 108.0 %all-gather.17.cloned.1.call-start = ((), (), s32[]{:S(2)}) async-start(), calls=%async_computation.13 | async-start | bytes 3932160 | tf_op jit(solution)/shard_map/all_gather | solution.py:204
  10.3 156.2 %all-gather.29.cloned.1.call-start = ((), (), s32[]{:S(2)}) async-start(), calls=%async_computation.26 | async-start | bytes 7077888 | tf_op jit(solution)/shard_map/all_gather | solution.py:77
  52.1 225.9 %all-gather.33.cloned.1.call-start = ((), (), s32[]{:S(2)}) async-start(), calls=%async_computation.28 | async-start | bytes 9437184 | tf_op jit(solution)/shard_map/all_gather | solution.py:87
  52.8 248.2 %all-gather.19.cloned.1.call-start = ((), (), s32[]{:S(2)}) async-start(), calls=%async_computation.14 | async-start | bytes 3932160 | tf_op jit(solution)/shard_map/all_gather | solution.py:228
  209.6 162.4 %all-gather.35.cloned.1.call-start = ((), (), s32[]{:S(2)}) async-start(), calls=%async_computation.29 | async-start | bytes 12976128 | tf_op jit(solution)/shard_map/all_gather | solution.py:77
  276.9 157.4 %all-gather.21.cloned.1.call-start = ((), (), s32[]{:S(2)}) async-start(), calls=%async_computation.16 | async-start | bytes 3932160 | tf_op jit(solution)/shard_map/all_gather | solution.py:208
  277.6 247.8 %reduce-scatter.9.cloned.1.call-start = ((), (), s32[]{:S(2)}) async-start(), calls=%async_computation.17 | async-start | bytes 3932160 | tf_op jit(solution)/shard_map/reduce_scatter | solution.py:246
  278.0 250.4 %copy-start.29 = (f32[1,4,4,128]{3,1,2,0:T(4,128)}, f32[1,4,4,128]{3,1,2,0:T(4,128)S(1)}, u32[]{:S(2)}) copy-start(f32[1,4,4,128]{3,1,2,0:T(4,128)S(1)} %copy.139) | copy-start | bytes 24580
  537.7 20.4 %all-to-all-start.2 = ((bf16[192,4,512]{2,0,1:T(8,128)(2,1)}), bf16[192,4,512]{2,0,1:T(8,128)(2,1)S(1)}, u32[]{:S(2)}, u32[]{:S(2)}) async-start(bf16[192,4,512]{2,0,1:T(8,128)(2,1)} %bitcast.128), calls=%async_computation.4 | async-start | bytes 1572864 | tf_op jit(solution)/shard_map/all_to_all | solution.py:257
  558.2 40.3 %all-to-all-start.4 = ((bf16[192,4,512]{2,0,1:T(8,128)(2,1)}), bf16[192,4,512]{2,0,1:T(8,128)(2,1)}, u32[]{:S(2)}, u32[]{:S(2)}) async-start(bf16[192,4,512]{2,0,1:T(8,128)(2,1)} %bitcast.127), calls=%async_computation.8 | async-start | bytes 1572864 | tf_op jit(solution)/shard_map/all_to_all | solution.py:260
  565.7 109.4 %reduce-scatter.15.cloned.1.call-start = ((), (), s32[]{:S(2)}) async-start(), calls=%async_computation.21 | async-start | bytes 2359296 | tf_op jit(solution)/shard_map/reduce_scatter | solution.py:104
  603.7 109.3 %reduce-scatter.13.cloned.1.call-start = ((), (), s32[]{:S(2)}) async-start(), calls=%async_computation.19 | async-start | bytes 7077888 | tf_op jit(solution)/shard_map/reduce_scatter | solution.py:104
  623.8 180.2 %reduce-scatter.17.cloned.1.call-start = ((), (), s32[]{:S(2)}) async-start(), calls=%async_computation.23 | async-start | bytes 12976128 | tf_op jit(solution)/shard_map/reduce_scatter | solution.py:104
  645.9 260.1 %all-reduce.4.cloned.1.call-start = ((), (), s32[]{:S(2)}) async-start(), calls=%async_computation.25 | async-start | bytes 11534336 | tf_op jit(solution)/shard_map/psum | solution.py:240
  655.8 313.2 %reduce-scatter.7.cloned.1.call-start = ((), (), s32[]{:S(2)}) async-start(), calls=%async_computation.15 | async-start | bytes 3932160 | tf_op jit(solution)/shard_map/reduce_scatter | solution.py:236
  665.3 366.3 %reduce-scatter.11.cloned.1.call-start = ((), (), s32[]{:S(2)}) async-start(), calls=%async_computation.18 | async-start | bytes 3932160 | tf_op jit(solution)/shard_map/reduce_scatter | solution.py:273
  675.0 404.2 %all-gather.25.cloned.1.call-start = ((), (), s32[]{:S(2)}) async-start(), calls=%async_computation.22 | async-start | bytes 2359296 | tf_op jit(solution)/shard_map/all_gather | solution.py:110
  686.3 424.3 %all-gather.23.cloned.1.call-start = ((), (), s32[]{:S(2)}) async-start(), calls=%async_computation.20 | async-start | bytes 7077888 | tf_op jit(solution)/shard_map/all_gather | solution.py:110
  738.0 442.1 %all-gather.27.cloned.1.call-start = ((), (), s32[]{:S(2)}) async-start(), calls=%async_computation.24 | async-start | bytes 12976128 | tf_op jit(solution)/shard_map/all_gather | solution.py:110
  844.9 186.7 %copy-start.32 = (f32[1,4,4,128]{3,1,2,0:T(4,128)S(1)}, f32[1,4,4,128]{3,1,2,0:T(4,128)}, u32[]{:S(2)}) copy-start(f32[1,4,4,128]{3,1,2,0:T(4,128)} %copy-done.31) | copy-start | bytes 24580
  914.6 160.3 %copy-start.38 = (f32[192]{0:T(256)S(1)}, f32[192]{0:T(256)}, u32[]{:S(2)}) copy-start(f32[192]{0:T(256)} %copy-done.37) | copy-start | bytes 2308
  914.7 160.3 %copy-start.40 = (f32[192]{0:T(256)S(1)}, f32[192]{0:T(256)}, u32[]{:S(2)}) copy-start(f32[192]{0:T(256)} %copy-done.39) | copy-start | bytes 2308
  914.7 160.3 %copy-start.42 = (f32[192]{0:T(256)S(1)}, f32[192]{0:T(256)}, u32[]{:S(2)}) copy-start(f32[192]{0:T(256)} %copy-done.41) | copy-start | bytes 2308
  (45 other events, 1414.4 us)
Sparse Core Ops, SparseCore 0:
  10.2 42.5 all-gather.30
  54.3 63.2 all-gather.16
  119.5 46.9 all-gather.28
  168.2 54.3 all-gather.32
  224.6 76.2 all-gather.18
  302.7 69.2 all-gather.34
  373.6 60.6 all-gather.20
  464.5 60.9 reduce-scatter.8
  603.8 43.1 reduce-scatter.14
  651.2 61.7 reduce-scatter.12
  717.1 86.7 reduce-scatter.16
  807.7 98.2 all-reduce.3
  909.0 60.0 reduce-scatter.6
  971.3 60.2 reduce-scatter.10
  1033.5 29.0 all-gather.24
  1065.0 45.5 all-gather.22
  1112.5 67.6 all-gather.26

commit v2 on v1

v2 whole, which is shorter than its diff:
```python
import functools

import jax
import jax.numpy as jnp
from jax import lax
from jax.experimental import pallas as pl
from jax.experimental.pallas import tpu as pltpu
from jax.sharding import PartitionSpec as P

D = 2048
FF = 5632
HEADS = 32
HEAD_DIM = 64
ROT_DIM = 16
MESH = pl.DeviceIdType.MESH


norm_eps = 1e-05
masked_score = -1000000000.0


def group_layout(lengths, token_index):
    seq_ends = jnp.cumsum(lengths)
    passed = (token_index[:, None] >= seq_ends[None, :]).astype(jnp.int32)
    segment = jnp.sum(passed, axis=1)
    position = token_index - jnp.sum(passed * lengths[None, :], axis=1)
    return (segment, position)


def rope_tables(position):
    half_rot = ROT_DIM // 2
    frequency = jnp.exp(
        -jnp.log(10000.0) * (2.0 * jnp.arange(half_rot, dtype=jnp.float32) / ROT_DIM)
    )
    angles = position.astype(jnp.float32)[:, None] * frequency[None, :]
    return (jnp.cos(angles), jnp.sin(angles))


def contract_last(left, right):
    return lax.dot_general(
        left, right, (((1,), (1,)), ((), ())), preferred_element_type=jnp.float32
    )


def aligned(value, unit):
    return pl.multiple_of(value * unit, unit)


def greet(partners, count):
    barrier = pltpu.get_barrier_semaphore()
    for there, device in partners:
        @pl.when(there)
        def _():
            pl.semaphore_signal(barrier, inc=1, device_id=device, device_id_type=MESH)
    pl.semaphore_wait(barrier, count)


def greet_line(z, shards):
    count = (z + shards - 1) // shards + (2 * shards - 2 - z) // shards
    greet([(z >= 1, {"shard": z - 1}), (z + 1 < shards, {"shard": z + 1})], count)


def remote(source, target, send, recv, device):
    return pltpu.make_async_remote_copy(
        src_ref=source, dst_ref=target, send_sem=send, recv_sem=recv,
        device_id=device, device_id_type=MESH,
    )


def start_kernel(shards, tokens, vectors, weight, cosine, minus, plus,
                 all_tokens, all_vectors, normed, qkv, kept_weight,
                 x_buf, v_buf, w_buf, n_buf, out_buf,
                 x_send, x_recv, v_send, v_recv, w_send, w_recv, xy_send, xy_recv, c_send, c_recv, loc):
    z = lax.axis_index("shard")
    r = lax.axis_index("replica")
    rows = tokens.shape[0]
    depth = weight.shape[0]
    share = depth // 8
    half = share // 2
    width = w_buf.shape[1] // 3
    core, x, y = r % 2, (r // 2) % 2, r // 4
    xr, yr, cr = r + 2 - 4 * x, r + 4 - 8 * y, r + 1 - 2 * core
    dr = 4 * (1 - y) + 2 * (1 - x) + core
    true = z >= 0
    greet(
        [((z != o), {"shard": o}) for o in range(shards)]
        + [(true, {"replica": d}) for d in (xr, yr, cr)],
        shards + 2,
    )

    def w_rows(owner, replica):
        return pl.ds(aligned(owner * 8 + replica, share), share)

    def vec_copy(o):
        return remote(vectors, v_buf.at[z], v_send.at[o], v_recv.at[z], {"shard": o})

    def w_copy(o, part):
        return remote(
            weight.at[pl.ds(aligned(r, share), share), pl.ds(aligned(part * shards + o, width), width)],
            w_buf.at[w_rows(z, r), pl.ds(part * width, width)],
            w_send.at[o, part], w_recv.at[z, part], {"shard": o},
        )

    def w_arrival(o, part):
        block = w_buf.at[w_rows(o, r), pl.ds(part * width, width)]
        return remote(block, block, w_send.at[o, part], w_recv.at[o, part], {"shard": o})

    def v_arrival(o):
        return remote(vectors, v_buf.at[o], v_send.at[o], v_recv.at[o], {"shard": o})

    def x_copy(way, step):
        target = z + 1 if way == 0 else z - 1
        chunk = z - step if way == 0 else z + step
        source = tokens if step == 0 else x_buf.at[chunk]
        return remote(source, x_buf.at[chunk], x_send.at[way, step], x_recv.at[way, step], {"shard": target})

    def x_sends(way, step):
        if way == 0:
            return (z + 1 < shards) & (z - step >= 0)
        return (z >= 1) & (z + step < shards)

    def x_gets(way, step):
        return (z - step >= 1) if way == 0 else (z + step + 1 < shards)

    for o in range(shards):
        @pl.when(z != o)
        def _():
            vec_copy(o).start()
            for part in range(3):
                w_copy(o, part).start()
    for way in (0, 1):
        @pl.when(x_sends(way, 0))
        def _():
            x_copy(way, 0).start()
    own_x = pltpu.make_async_copy(tokens, x_buf.at[z], loc.at[0])
    own_x.start()
    own_v = pltpu.make_async_copy(vectors, v_buf.at[z], loc.at[1])
    own_v.start()
    own_w = [
        pltpu.make_async_copy(
            weight.at[pl.ds(aligned(r, share), share), pl.ds(aligned(part * shards + z, width), width)],
            w_buf.at[w_rows(z, r), pl.ds(part * width, width)], loc.at[2 + part],
        )
        for part in range(3)
    ]
    for copy in own_w:
        copy.start()

    def to_x(o):
        block = w_buf.at[w_rows(o, r)]
        return remote(block, block, xy_send.at[0, o], xy_recv.at[0, o], {"replica": xr})

    def to_y(o):
        block = w_buf.at[w_rows(o, r)]
        return remote(block, block, xy_send.at[1, o], xy_recv.at[1, o], {"replica": yr})

    def on_to_y(o):
        block = w_buf.at[pl.ds(aligned((o * 8 + xr) * 2, half), half)]
        return remote(block, block, xy_send.at[2, o], xy_recv.at[2, o], {"replica": yr})

    def on_to_x(o):
        block = w_buf.at[pl.ds(aligned((o * 8 + yr) * 2 + 1, half), half)]
        return remote(block, block, xy_send.at[3, o], xy_recv.at[3, o], {"replica": xr})

    def to_core(o, kind):
        whose = (r, xr, yr, dr)[kind]
        block = w_buf.at[w_rows(o, whose)]
        return remote(block, block, c_send.at[kind, o], c_recv.at[kind, o], {"replica": cr})

    for copy in own_w:
        copy.wait()
    for step in range(shards):
        for o in range(shards):
            @pl.when((z - o == step) | (o - z == step))
            def _():
                if step > 0:
                    for part in range(3):
                        w_arrival(o, part).wait_recv()
                to_x(o).start()
                to_y(o).start()
                to_core(o, 0).start()
        if step + 1 < shards:
            for way in (0, 1):
                @pl.when(x_gets(way, step))
                def _():
                    x_copy(way, step).wait_recv()
                @pl.when(x_sends(way, step + 1))
                def _():
                    x_copy(way, step + 1).start()
    for o in range(shards):
        to_x(o).wait_recv()
        on_to_y(o).start()
        to_core(o, 1).start()
        to_y(o).wait_recv()
        on_to_x(o).start()
        to_core(o, 2).start()
    own_x.wait()
    own_v.wait()
    for o in range(shards):
        @pl.when(z != o)
        def _():
            v_arrival(o).wait_recv()

    keep_x = pltpu.make_async_copy(x_buf, all_tokens, loc.at[5])
    keep_x.start()
    keep_v = pltpu.make_async_copy(v_buf, all_vectors, loc.at[6])
    keep_v.start()
    gain = jnp.concatenate([v_buf[o, 3:4, :] for o in range(shards)], axis=1)
    shift = jnp.concatenate([v_buf[o, 4:5, :] for o in range(shards)], axis=1)
    for o in range(shards):
        @pl.loop(0, rows, step=32)
        def _(at):
            block = pl.ds(pl.multiple_of(at, 32), 32)
            values = x_buf[o, block, :].astype(jnp.float32)
            centered = values - jnp.mean(values, axis=-1, keepdims=True)
            spread = jnp.mean(centered * centered, axis=-1, keepdims=True)
            out = centered * lax.rsqrt(spread + norm_eps) * gain + shift
            n_buf[pl.ds(pl.multiple_of(o * rows + at, 32), 32), :] = out.astype(jnp.bfloat16)
    keep_n = pltpu.make_async_copy(n_buf, normed, loc.at[7])
    keep_n.start()

    for o in range(shards):
        on_to_y(o).wait_recv()
        on_to_x(o).wait_recv()
        to_core(o, 3).start()
    for o in range(shards):
        for kind in range(4):
            to_core(o, kind).wait_recv()
    keep_w = pltpu.make_async_copy(w_buf, kept_weight, loc.at[8])
    keep_w.start()

    tile = 256
    per_part = width // tile

    @pl.loop(0, 3 * per_part)
    def _(t):
        columns = pl.ds(aligned(t, tile), tile)
        bias_row = bias_piece(v_buf, z, t, tile, shards, per_part)
        value = jnp.dot(n_buf[...], w_buf[:, columns], preferred_element_type=jnp.float32) + bias_row

        @pl.when(t < 2 * per_part)
        def _():
            wide = jnp.concatenate([cosine[...]] * (tile // 128), axis=1)
            wide_minus = jnp.concatenate([minus[...]] * (tile // 128), axis=1)
            wide_plus = jnp.concatenate([plus[...]] * (tile // 128), axis=1)
            turned = value * wide + pltpu.roll(value, tile - 8, 1) * wide_minus + pltpu.roll(value, 8, 1) * wide_plus
            out_buf[:, columns] = turned.astype(jnp.bfloat16)

        @pl.when(t >= 2 * per_part)
        def _():
            out_buf[:, columns] = value.astype(jnp.bfloat16)
    keep_q = pltpu.make_async_copy(out_buf, qkv, loc.at[9])
    keep_q.start()

    for o in range(shards):
        @pl.when(z != o)
        def _():
            vec_copy(o).wait_send()
            for part in range(3):
                w_copy(o, part).wait_send()
        to_x(o).wait_send()
        to_y(o).wait_send()
        on_to_y(o).wait_send()
        on_to_x(o).wait_send()
        for kind in range(4):
            to_core(o, kind).wait_send()
    for step in range(shards - 1):
        for way in (0, 1):
            @pl.when(x_sends(way, step))
            def _():
                x_copy(way, step).wait_send()
    for copy in (keep_x, keep_v, keep_n, keep_w, keep_q):
        copy.wait()


def bias_piece(v_buf, z, t, tile, shards, per_part):
    part = t // per_part
    at = t % per_part
    flat = part * shards + z
    return v_buf[flat // 3, pl.ds(flat % 3, 1), pl.ds(aligned(at, tile), tile)]


def start_call(shards, tokens, vectors, weight, cosine, minus, plus):
    rows = tokens.shape[0]
    group = rows * shards
    depth = weight.shape[0]
    width = weight.shape[1] // shards
    any_ = pl.BlockSpec(memory_space=pl.ANY)
    vm = pl.BlockSpec(memory_space=pltpu.VMEM)
    low = jnp.bfloat16
    dma = pltpu.SemaphoreType.DMA
    return pl.pallas_call(
        functools.partial(start_kernel, shards),
        out_shape=[
            jax.ShapeDtypeStruct((shards, rows, D), low),
            jax.ShapeDtypeStruct((shards,) + vectors.shape, vectors.dtype),
            jax.ShapeDtypeStruct((group, D), low),
            jax.ShapeDtypeStruct((group, width), low),
            jax.ShapeDtypeStruct((depth * shards, width), low),
        ],
        in_specs=[any_, any_, any_, vm, vm, vm],
        out_specs=[any_] * 5,
        scratch_shapes=[
            pltpu.VMEM((shards, rows, D), low),
            pltpu.VMEM((shards,) + vectors.shape, vectors.dtype),
            pltpu.VMEM((depth * shards, width), low),
            pltpu.VMEM((group, D), low),
            pltpu.VMEM((group, width), low),
            dma((2, shards)), dma((2, shards)),
            dma((shards,)), dma((shards,)),
            dma((shards, 3)), dma((shards, 3)),
            dma((4, shards)), dma((4, shards)),
            dma((4, shards)), dma((4, shards)),
            dma((10,)),
        ],
        compiler_params=pltpu.CompilerParams(
            collective_id=1, has_side_effects=True, vmem_limit_bytes=48 * 2**20
        ),
        name="start",
        cost_estimate=pl.CostEstimate(flops=2 * group * D * width, bytes_accessed=150 * 10**6, transcendentals=0),
    )(tokens, vectors, weight, cosine, minus, plus)


def head_mask(even, rows):
    lane = lax.broadcasted_iota(jnp.int32, (rows, 128), 1)
    return (lane < HEAD_DIM) if even else (lane >= HEAD_DIM)


def only(values, keep):
    return jnp.where(keep, values.astype(jnp.float32), 0.0).astype(jnp.bfloat16)


def block_visible(at, rows, seg_rows, seg_columns):
    count = at + rows
    row = lax.broadcasted_iota(jnp.int32, (rows, count), 0) + at
    column = lax.broadcasted_iota(jnp.int32, (rows, count), 1)
    return (column <= row) & (seg_rows[at : at + rows, :1] == seg_columns[:1, :count])


def line_sends(z, shards, way, step):
    if way == 0:
        return (z + 1 < shards) & (z - step >= 0)
    return (z >= 1) & (z + step < shards)


def line_gets(z, shards, way, step):
    return (z - step >= 1) if way == 0 else (z + step + 1 < shards)


def attend_kernel(shards, rows, qkv, seg_rows, seg_columns, attended, stats,
                  a_buf, a_send, a_recv, loc):
    z = lax.axis_index("shard")
    width = qkv.shape[1] // 3
    group = qkv.shape[0]
    pairs = width // 128
    greet_line(z, shards)

    def a_copy(way, step, block):
        target = z + 1 if way == 0 else z - 1
        owner = z - step if way == 0 else z + step
        piece = a_buf.at[owner, pl.ds(block * rows, rows)]
        return remote(piece, piece, a_send.at[way, step, block], a_recv.at[way, step, block], {"shard": target})

    scale = HEAD_DIM ** (-0.5)
    blocks = group // rows
    for block in range(blocks):
        at = block * rows
        count = at + rows
        seen = block_visible(at, rows, seg_rows, seg_columns)
        for pair in range(pairs):
            lanes = slice(128 * pair, 128 * pair + 128)
            query = qkv[at:count, lanes]
            keys = qkv[:count, width + 128 * pair : width + 128 * pair + 128]
            values = qkv[:count, 2 * width + 128 * pair : 2 * width + 128 * pair + 128]
            results = []
            for odd in (0, 1):
                keep = head_mask(odd == 0, rows)
                scores = contract_last(only(query, keep), keys) * scale
                scores = jnp.where(seen, scores, masked_score)
                top = jnp.max(scores, axis=-1, keepdims=True)
                weights = jnp.exp(scores - top)
                total = jnp.sum(weights, axis=-1, keepdims=True)
                probs = (weights * (1.0 / total)).astype(jnp.bfloat16)
                results.append(jnp.dot(probs, values, preferred_element_type=jnp.float32))
                head = 2 * pair + odd
                stats[at:count, head : head + 1] = top
                stats[at:count, 64 + head : 65 + head] = 1.0 / total
            merged = jnp.where(head_mask(True, rows), results[0], results[1])
            a_buf[z, at:count, lanes] = merged.astype(jnp.bfloat16)
        for way in (0, 1):
            @pl.when(line_sends(z, shards, way, 0))
            def _():
                a_copy(way, 0, block).start()
    for step in range(shards - 1):
        for block in range(blocks):
            for way in (0, 1):
                @pl.when(line_gets(z, shards, way, step))
                def _():
                    a_copy(way, step, block).wait_recv()
                if step + 1 < shards - 1:
                    @pl.when(line_sends(z, shards, way, step + 1))
                    def _():
                        a_copy(way, step + 1, block).start()
    keep_a = [pltpu.make_async_copy(a_buf.at[o], attended.at[:, pl.ds(o * width, width)], loc.at[o]) for o in range(shards)]
    for copy in keep_a:
        copy.start()
    for step in range(shards - 1):
        for block in range(blocks):
            for way in (0, 1):
                @pl.when(line_sends(z, shards, way, step))
                def _():
                    a_copy(way, step, block).wait_send()
    for copy in keep_a:
        copy.wait()


def attend_call(shards, rows, qkv, seg_rows, seg_columns):
    group = qkv.shape[0]
    width = qkv.shape[1] // 3
    blocks = group // rows
    vm = pl.BlockSpec(memory_space=pltpu.VMEM)
    any_ = pl.BlockSpec(memory_space=pl.ANY)
    dma = pltpu.SemaphoreType.DMA
    return pl.pallas_call(
        functools.partial(attend_kernel, shards, rows),
        out_shape=[
            jax.ShapeDtypeStruct((group, shards * width), jnp.bfloat16),
            jax.ShapeDtypeStruct((group, 128), jnp.float32),
        ],
        in_specs=[vm, vm, vm],
        out_specs=[any_, vm],
        scratch_shapes=[
            pltpu.VMEM((shards, group, width), jnp.bfloat16),
            dma((2, shards - 1, blocks)), dma((2, shards - 1, blocks)), dma((shards,)),
        ],
        compiler_params=pltpu.CompilerParams(
            collective_id=2, has_side_effects=True, vmem_limit_bytes=48 * 2**20
        ),
        name="attend",
        cost_estimate=pl.CostEstimate(flops=10**9, bytes_accessed=150 * 10**6, transcendentals=0),
    )(qkv, seg_rows, seg_columns)


def attend_back_kernel(rows, qkv, d_attended, stats, seg_rows, seg_columns, cosine, minus, plus,
                       d_qkv, bias_grad, d_keys, d_values):
    width = qkv.shape[1] // 3
    group = qkv.shape[0]
    blocks = group // rows
    pairs = width // 128
    scale = HEAD_DIM ** (-0.5)

    def turned(value, at, count):
        return (value * cosine[at:count, :] - pltpu.roll(value, 120, 1) * minus[at:count, :]
                - pltpu.roll(value, 8, 1) * plus[at:count, :])

    for block in reversed(range(blocks)):
        at = block * rows
        count = at + rows
        seen = block_visible(at, rows, seg_rows, seg_columns)
        for pair in range(pairs):
            lanes = slice(128 * pair, 128 * pair + 128)
            query = qkv[at:count, lanes]
            keys = qkv[:count, width + 128 * pair : width + 128 * pair + 128]
            values = qkv[:count, 2 * width + 128 * pair : 2 * width + 128 * pair + 128]
            slope = d_attended[at:count, lanes]
            d_query, d_key, d_value = [], [], []
            for odd in (0, 1):
                keep = head_mask(odd == 0, rows)
                head = 2 * pair + odd
                own_query = only(query, keep)
                own_slope = only(slope, keep)
                scores = contract_last(own_query, keys) * scale
                scores = jnp.where(seen, scores, masked_score)
                probs = jnp.exp(scores - stats[at:count, head : head + 1]) * stats[at:count, 64 + head : 65 + head]
                d_probs = contract_last(own_slope, values)
                inner = jnp.sum(probs * d_probs, axis=-1, keepdims=True)
                d_scores = (probs * (d_probs - inner)).astype(jnp.bfloat16)
                d_query.append(jnp.dot(d_scores, keys, preferred_element_type=jnp.float32))
                d_key.append(contract_first(d_scores, own_query))
                d_value.append(contract_first(probs.astype(jnp.bfloat16), own_slope))
            keep = head_mask(True, rows)
            d_q = jnp.where(keep, d_query[0], d_query[1]) * scale
            d_q = turned(d_q, at, count).astype(jnp.bfloat16)
            d_qkv[at:count, lanes] = d_q
            d_k = (d_key[0] + d_key[1]) * scale
            d_v = d_value[0] + d_value[1]
            if block == blocks - 1:
                d_keys[:, lanes] = d_k
                d_values[:, lanes] = d_v
            else:
                d_keys[:count, lanes] += d_k
                d_values[:count, lanes] += d_v
            k_out = turned(d_keys[at:count, lanes], at, count).astype(jnp.bfloat16)
            d_qkv[at:count, width + 128 * pair : width + 128 * pair + 128] = k_out
            v_out = d_values[at:count, lanes].astype(jnp.bfloat16)
            d_qkv[at:count, 2 * width + 128 * pair : 2 * width + 128 * pair + 128] = v_out
    for part in range(3 * pairs):
        lanes = slice(128 * part, 128 * part + 128)
        bias_grad[:, lanes] = jnp.broadcast_to(
            jnp.sum(d_qkv[:, lanes].astype(jnp.float32), axis=0, keepdims=True), (8, 128))


def contract_first(left, right):
    return lax.dot_general(
        left, right, (((0,), (0,)), ((), ())), preferred_element_type=jnp.float32
    )


def attend_back_call(rows, qkv, d_attended, stats, seg_rows, seg_columns, cosine, minus, plus):
    group = qkv.shape[0]
    width = qkv.shape[1] // 3
    vm = pl.BlockSpec(memory_space=pltpu.VMEM)
    return pl.pallas_call(
        functools.partial(attend_back_kernel, rows),
        out_shape=[
            jax.ShapeDtypeStruct((group, 3 * width), jnp.bfloat16),
            jax.ShapeDtypeStruct((8, 3 * width), jnp.float32),
        ],
        in_specs=[vm] * 8,
        out_specs=[vm, vm],
        scratch_shapes=[pltpu.VMEM((group, width), jnp.float32), pltpu.VMEM((group, width), jnp.float32)],
        compiler_params=pltpu.CompilerParams(vmem_limit_bytes=48 * 2**20),
        name="attend_back",
        cost_estimate=pl.CostEstimate(flops=3 * 10**9, bytes_accessed=100 * 10**6, transcendentals=0),
    )(qkv, d_attended, stats, seg_rows, seg_columns, cosine, minus, plus)


def scatter_kernel(shards, cuts, parts, total, own, got, load, send, recv):
    z = lax.axis_index("shard")
    rows = parts.shape[1]
    step_rows = rows // cuts
    greet_line(z, shards)

    def piece(cut):
        return pl.ds(cut * step_rows, step_rows)

    def moved(way, block, cut):
        target = z + 1 if way == 0 else z - 1
        place = got.at[way, block, piece(cut)]
        return remote(place, place, send.at[way, block, cut], recv.at[way, block, cut], {"shard": target})

    loads = [pltpu.make_async_copy(parts.at[j], own.at[j], load.at[j]) for j in range(shards)]
    for copy in loads:
        copy.start()
    for copy in loads:
        copy.wait()
    for far in range(shards - 1):
        for cut in range(cuts):
            for way in (0, 1):
                block = shards - 1 - far if way == 0 else far
                sends = z < block if way == 0 else z > block
                first = z == 0 if way == 0 else z == shards - 1

                @pl.when(sends)
                def _():
                    @pl.when(first)
                    def _():
                        got[way, block, piece(cut)] = own[block, piece(cut)]

                    @pl.when(jnp.logical_not(first))
                    def _():
                        moved(way, block, cut).wait_recv()
                        got[way, block, piece(cut)] = (
                            got[way, block, piece(cut)].astype(jnp.float32)
                            + own[block, piece(cut)].astype(jnp.float32)
                        ).astype(got.dtype)
                    moved(way, block, cut).start()
    total[...] = own[z].astype(jnp.float32)
    for way in (0, 1):
        @pl.when(z >= 1 if way == 0 else z + 1 < shards)
        def _():
            for cut in range(cuts):
                moved(way, z, cut).wait_recv()
            total[...] += got[way, z].astype(jnp.float32)
    for far in range(shards - 1):
        for cut in range(cuts):
            for way in (0, 1):
                block = shards - 1 - far if way == 0 else far

                @pl.when(z < block if way == 0 else z > block)
                def _():
                    moved(way, block, cut).wait_send()


def scatter_call(shards, parts, number):
    _, rows, columns = parts.shape
    cuts = 3
    dma = pltpu.SemaphoreType.DMA
    return pl.pallas_call(
        functools.partial(scatter_kernel, shards, cuts),
        out_shape=jax.ShapeDtypeStruct((rows, columns), jnp.float32),
        in_specs=[pl.BlockSpec(memory_space=pl.ANY)],
        out_specs=pl.BlockSpec(memory_space=pltpu.VMEM),
        scratch_shapes=[
            pltpu.VMEM(parts.shape, parts.dtype),
            pltpu.VMEM((2,) + parts.shape, parts.dtype),
            dma((shards,)), dma((2, shards, cuts)), dma((2, shards, cuts)),
        ],
        compiler_params=pltpu.CompilerParams(
            collective_id=number, has_side_effects=True, vmem_limit_bytes=32 * 2**20
        ),
        name="scatter",
        cost_estimate=pl.CostEstimate(flops=0, bytes_accessed=200 * 10**6, transcendentals=0),
    )(parts)


def exchange_kernel(shards, first, second, first_out, second_out, send, recv, loc):
    z = lax.axis_index("shard")
    width = first.shape[1] // shards
    greet([((z != o), {"shard": o}) for o in range(shards)], shards - 1)
    arrays = ((first, first_out), (second, second_out))

    def move(k, o):
        source, target = arrays[k]
        return remote(source.at[:, pl.ds(o * width, width)], target.at[z], send.at[k, o], recv.at[k, z], {"shard": o})

    def arrival(k, o):
        source, target = arrays[k]
        return remote(target.at[o], target.at[o], send.at[k, o], recv.at[k, o], {"shard": o})

    for k in (0, 1):
        for o in range(shards):
            @pl.when(z != o)
            def _():
                move(k, o).start()

            @pl.when(z == o)
            def _():
                source, target = arrays[k]
                pltpu.make_async_copy(source.at[:, pl.ds(o * width, width)], target.at[o], loc.at[k]).start()
    for k in (0, 1):
        for o in range(shards):
            @pl.when(z != o)
            def _():
                arrival(k, o).wait_recv()
                move(k, o).wait_send()

            @pl.when(z == o)
            def _():
                source, target = arrays[k]
                pltpu.make_async_copy(source.at[:, pl.ds(o * width, width)], target.at[o], loc.at[k]).wait()


def exchange_call(shards, first, second):
    rows, columns = first.shape
    shape = jax.ShapeDtypeStruct((shards, rows, columns // shards), first.dtype)
    any_ = pl.BlockSpec(memory_space=pl.ANY)
    dma = pltpu.SemaphoreType.DMA
    return pl.pallas_call(
        functools.partial(exchange_kernel, shards),
        out_shape=[shape, shape],
        in_specs=[any_, any_],
        out_specs=[any_, any_],
        scratch_shapes=[dma((2, shards)), dma((2, shards)), dma((2,))],
        compiler_params=pltpu.CompilerParams(collective_id=5, has_side_effects=True),
        name="exchange",
        cost_estimate=pl.CostEstimate(flops=0, bytes_accessed=100 * 10**6, transcendentals=0),
    )(first, second)


def swap_pieces(pieces):
    shards = lax.axis_size("shard")
    here = lax.axis_index("shard")
    out = pieces
    for k in range(1, shards):
        partner = jnp.bitwise_xor(here, k)
        piece = lax.dynamic_index_in_dim(pieces, partner, axis=0, keepdims=True)
        piece = lax.ppermute(piece, "shard", [(i, i ^ k) for i in range(shards)])
        out = lax.dynamic_update_slice_in_dim(out, piece, partner, axis=0)
    return out


def own_share(rows):
    own = rows.shape[0] // lax.axis_size("replica")
    return lax.dynamic_slice_in_dim(rows, lax.axis_index("replica") * own, own, axis=0)


def spread_rows(rows, columns):
    shards = lax.axis_size("shard")
    piece = own_share(rows)
    own = piece.shape[0]
    piece = piece.reshape(own, columns, shards, -1).transpose(2, 0, 1, 3).reshape(shards, own, -1)
    full = lax.all_gather(swap_pieces(piece), "replica", axis=0, tiled=False)
    return full.transpose(1, 0, 2, 3).reshape(rows.shape[0] * shards, -1)


def gather_rows(rows):
    shards = lax.axis_size("shard")
    piece = own_share(rows)
    moved = swap_pieces(jnp.broadcast_to(piece[None], (shards,) + piece.shape))
    full = lax.all_gather(moved, "replica", axis=0, tiled=False)
    return full.transpose(1, 0, 2, 3).reshape(rows.shape[0] * shards, -1)


def own_rows(features):
    copies = lax.axis_size("replica")
    shards = lax.axis_size("shard")
    count = features.shape[0]
    return (
        features.reshape(count, shards, copies, -1).transpose(0, 2, 1, 3).reshape(count, -1)
    )


def sum_columns(features, slopes, columns):
    shards = lax.axis_size("shard")
    term = contract_first(own_rows(features), slopes).astype(jnp.bfloat16)
    part = lax.psum_scatter(term, "replica", scatter_dimension=0, tiled=True)
    own = part.shape[0] // shards
    moved = swap_pieces(part.reshape(shards, own, -1))
    moved = moved.reshape(shards, own, columns, -1).transpose(1, 2, 0, 3).reshape(own, -1)
    return lax.all_gather(moved, "replica", axis=0, tiled=True).astype(jnp.float32)


def swiglu(gate_up):
    half = gate_up.shape[1] // 2
    return jax.nn.silu(gate_up[:, :half]) * gate_up[:, half:]


def norm_stats(values):
    mean = jnp.mean(values, axis=-1, keepdims=True)
    centered = values - mean
    inverse = lax.rsqrt(jnp.mean(centered * centered, axis=-1, keepdims=True) + norm_eps)
    return centered * inverse, inverse


def norm_back(slope, unit, inverse, gain):
    scaled = slope * gain
    return inverse * (
        scaled
        - jnp.mean(scaled, axis=-1, keepdims=True)
        - unit * jnp.mean(scaled * unit, axis=-1, keepdims=True)
    )


def start_plain(tokens, vectors, qkv_weight, cosine, minus, plus):
    shards = lax.axis_size("shard")
    here = lax.axis_index("shard")
    all_tokens = lax.all_gather(tokens, "shard", axis=0, tiled=False)
    all_vectors = lax.all_gather(vectors, "shard", axis=0, tiled=False)
    weight = spread_rows(qkv_weight, 3)
    width = D // shards
    gain, shift = (all_vectors[:, 3 + i].reshape(D) for i in (0, 1))
    unit, _ = norm_stats(all_tokens.reshape(-1, D).astype(jnp.float32))
    normed = (unit * gain + shift).astype(jnp.bfloat16)
    bias = all_vectors[:, :3].reshape(3, shards, width)
    bias = lax.dynamic_index_in_dim(bias, here, axis=1, keepdims=False).reshape(3 * width)
    value = jnp.dot(normed, weight, preferred_element_type=jnp.float32) + bias
    turned = value[:, : 2 * width]
    wide = [jnp.tile(t, (1, 2 * width // 128)) for t in (cosine, minus, plus)]
    turned = (
        turned * wide[0] + jnp.roll(turned, -8, 1) * wide[1] + jnp.roll(turned, 8, 1) * wide[2]
    )
    qkv = jnp.concatenate([turned, value[:, 2 * width :]], axis=1).astype(jnp.bfloat16)
    return all_tokens, all_vectors, normed, qkv, weight


def on_device(
    tokens,
    cotangent,
    qkv_weight,
    qkv_bias,
    out_weight,
    gate_up_weight,
    down_weight,
    norm1_gain,
    norm1_shift,
    norm2_gain,
    norm2_shift,
    seq_lengths,
):
    shards = lax.axis_size("shard")
    copies = lax.axis_size("replica")
    here = lax.axis_index("shard")
    row_count = tokens.shape[0]
    group_rows = row_count * shards
    width = D // shards
    f32 = jnp.float32
    low = jnp.bfloat16

    index = jnp.arange(group_rows, dtype=jnp.int32)
    segment, position = group_layout(seq_lengths[0], index)
    seg_rows = jnp.broadcast_to(segment[:, None], (group_rows, 128))
    seg_columns = jnp.broadcast_to(segment[None, :], (8, group_rows))
    cosine, sine_value = rope_tables(position)
    half_rot = ROT_DIM // 2
    rest = HEAD_DIM - ROT_DIM
    none = jnp.zeros((group_rows, half_rot), f32)
    empty = jnp.zeros((group_rows, rest), f32)
    cosine = jnp.tile(jnp.concatenate([cosine, cosine, empty + 1.0], axis=1), (1, 2))
    minus = jnp.tile(jnp.concatenate([-sine_value, none, empty], axis=1), (1, 2))
    plus = jnp.tile(jnp.concatenate([none, sine_value, empty], axis=1), (1, 2))

    vectors = jnp.concatenate(
        [qkv_bias, norm1_gain, norm1_shift, norm2_gain, norm2_shift, jnp.zeros((width,), low)]
    )
    vectors = vectors.astype(f32).reshape(8, width)
    weight_out = gather_rows(out_weight)
    weight_gate_up = spread_rows(gate_up_weight, 2)
    begin = functools.partial(start_call, shards) if copies == 8 else start_plain
    all_tokens, all_vectors, normed_low, qkv, weight_qkv = begin(
        tokens, vectors, qkv_weight, cosine, minus, plus
    )
    gain_one, shift_one, gain_two, shift_two = (
        all_vectors[:, 3 + i].reshape(D) for i in range(4)
    )
    cotangent_later, qkv = lax.optimization_barrier((cotangent, qkv))
    group_cotangent = lax.all_gather(cotangent_later, "shard", axis=0, tiled=True)

    def local(array):
        return lax.dynamic_slice_in_dim(array, here * row_count, row_count, axis=0)

    attended, stats = attend_call(shards, row_count, qkv, seg_rows, seg_columns)
    inputs = all_tokens.reshape(group_rows, D).astype(f32)
    middle = inputs + jnp.dot(attended, weight_out, preferred_element_type=f32)
    unit_two, inverse_two = norm_stats(middle)
    normed_two_low = (unit_two * gain_two + shift_two).astype(low)
    gate_up = jnp.dot(normed_two_low, weight_gate_up, preferred_element_type=f32)
    hidden, swiglu_pull = jax.vjp(swiglu, gate_up)
    hidden_low = hidden.astype(low)
    d_hidden = contract_last(group_cotangent, down_weight)
    d_gate_up_low = swiglu_pull(d_hidden)[0].astype(low)
    d_normed_two_part = contract_last(d_gate_up_low, weight_gate_up).astype(low)
    d_normed_two = scatter_call(shards, d_normed_two_part.reshape(shards, row_count, D), 3)
    unit_two_own = local(unit_two)
    d_middle = cotangent.astype(f32) + norm_back(
        d_normed_two, unit_two_own, local(inverse_two), gain_two
    )
    d_gain_two = jnp.sum(d_normed_two * unit_two_own, axis=0)
    d_shift_two = jnp.sum(d_normed_two, axis=0)
    d_middle_low = d_middle.astype(low)
    d_attended_own = contract_last(d_middle_low, weight_out).astype(low)
    d_attended, d_middle_columns = exchange_call(shards, d_attended_own, d_middle_low)
    d_projected_low, bias_part = attend_back_call(
        row_count, qkv, d_attended.reshape(group_rows, width), stats, seg_rows, seg_columns,
        cosine, minus, plus,
    )
    d_normed_part = contract_last(d_projected_low, weight_qkv).astype(low)
    d_normed = scatter_call(shards, d_normed_part.reshape(shards, row_count, D), 4)
    unit_one, inverse_one = norm_stats(tokens.astype(f32))
    input_grad = d_middle + norm_back(d_normed, unit_one, inverse_one, gain_one)
    d_gain_one = jnp.sum(d_normed * unit_one, axis=0)
    d_shift_one = jnp.sum(d_normed, axis=0)

    down_part = jnp.dot(hidden_low, down_weight, preferred_element_type=f32).astype(low)
    down_own = lax.psum_scatter(down_part, "shard", scatter_dimension=0, tiled=True)
    mixed = (local(middle) + down_own.astype(f32)).astype(low)
    down_grad = lax.psum(
        contract_first(hidden_low, group_cotangent).astype(low), "replica"
    ).astype(f32)
    gate_up_grad = sum_columns(normed_two_low, d_gate_up_low, 2)
    out_grad = sum_columns(attended, d_middle_columns.reshape(group_rows, width), 1)
    qkv_grad = sum_columns(normed_low, d_projected_low, 3)

    bias_part = bias_part[0].reshape(3, 1, width)
    bias_wide = lax.dynamic_update_slice(
        jnp.zeros((3, shards, width), f32), bias_part, (0, here, 0)
    ).reshape(shards, 3 * width)
    small = jnp.concatenate(
        [bias_wide]
        + [v.reshape(shards, width) for v in (d_gain_one, d_shift_one, d_gain_two, d_shift_two)],
        axis=1,
    )
    small = lax.psum(small, ("replica", "shard"))
    small = lax.dynamic_index_in_dim(small, here, axis=0, keepdims=False)
    bias_rows = 3 * width
    return (
        mixed,
        input_grad,
        qkv_grad,
        small[:bias_rows],
        out_grad,
        gate_up_grad,
        down_grad,
    ) + tuple(small[bias_rows + i * width : bias_rows + (i + 1) * width] for i in range(4))


def solution(mesh):
    placed = (
        P(("replica", "shard"), None),
        P(("replica", "shard"), None),
        P("shard", None),
        P("shard"),
        P("shard", None),
        P("shard", None),
        P("shard", None),
        P("shard"),
        P("shard"),
        P("shard"),
        P("shard"),
        P("replica", None),
    )
    return jax.shard_map(
        on_device,
        mesh=mesh,
        in_specs=placed,
        out_specs=(
            P(("replica", "shard"), None),
            P(("replica", "shard"), None),
            P("shard", None),
            P("shard"),
            P("shard", None),
            P("shard", None),
            P("shard", None),
            P("shard"),
            P("shard"),
            P("shard"),
            P("shard"),
        ),
        check_vma=False,
    )
```

time: 1210 us -> 1040 us (0.86)
  Pallas kernels: 0 us -> 392 us
  waiting for transfers between devices: 620 us -> 281 us
  blocking collectives: 221 us -> 72.2 us
  matrix products: 169 us -> 114 us
  other arithmetic: 78 us -> 53.2 us
    pallas_call x0 -> x6, Pallas kernels: none -> 392 us  [the longest x1 123 us: attend_call(): pl.pallas_call(functools.partial(attend_kernel, shards, rows), out_shape=...]
    all_gather x6 -> x2, waiting for transfers between devices: 198 us -> 0.01 us  [the longest x1 0.01 us: spread_rows(): full = lax.all_gather(swap_pieces(piece), 'replica', axis=0, tiled=False)]
    all_to_all x5 -> x0, blocking collectives: 169 us -> none  [the longest x2 101 us: spread_rows(): lax.all_to_all(piece, 'shard', split_axis=0, concat_axis=0, tiled=True)]
    reduce_scatter x2 -> x0, waiting for transfers between devices: 121 us -> none  [the longest x1 61 us: on_device(): lax.psum_scatter(d_normed_two_part, 'shard', scatter_dimension=0, tiled=T...]
    ppermute x0 -> x15, waiting for transfers between devices: none -> 114 us  [swap_pieces(): piece = lax.ppermute(piece, 'shard', [(i, i ^ k) for i in range(shards)])]
    psum x1, waiting for transfers between devices: 61.1 us -> 0.01 us  [on_device(): lax.psum(contract_first(hidden_low, group_cotangent).astype(low), 'replica')]
    reduce_scatter x1, waiting for transfers between devices: 54.3 us -> 0.01 us  [on_device(): lax.psum_scatter(down_part, 'shard', scatter_dimension=0, tiled=True)]
    dot_general x7 -> x1, matrix products: 54.6 us -> 10.6 us  [on_device(): middle = inputs + jnp.dot(attended, weight_out, preferred_element_type=f32)]
  transfers between devices with their start and end apart: 19 -> 26, of which waited for: 15 -> 19; matrix products, arithmetic and copies ran while one was open for 21% -> 17% of each run, Pallas kernels for 0% -> 29%
where the time goes in v2:
time: 1040 us; the launch traced here: 1030 us
  Pallas kernels  392 us (38%)
  waiting for transfers between devices  281 us (27%)
  matrix products  114 us (11%)
  local copies, waits for them, and re-layouts  85.9 us (8%)
  blocking collectives  72.2 us (7%)
  other arithmetic  53.2 us (5%)
  between operations  15 us (1%)
  starting transfers between devices  14 us (1%)
    pallas_call x1, Pallas kernels, attend_call(): pl.pallas_call(functools.partial(attend_kernel, shards, rows), out_shape=...  123 us
    pallas_call x2, Pallas kernels, scatter_call(): pl.pallas_call(functools.partial(scatter_kernel, shards, cuts), out_shape...  116 us
    ppermute x15, waiting for transfers between devices, swap_pieces(): piece = lax.ppermute(piece, 'shard', [(i, i ^ k) for i in range(shards)])  114 us
    all_gather x3, waiting for transfers between devices, sum_columns(): lax.all_gather(moved, 'replica', axis=0, tiled=True).astype(jnp.float32)  94.6 us
    pallas_call x1, Pallas kernels, start_call(): pl.pallas_call(functools.partial(start_kernel, shards), out_shape=[jax.Sh...  93.8 us
    reduce_scatter x3, waiting for transfers between devices, sum_columns(): part = lax.psum_scatter(term, 'replica', scatter_dimension=0, tiled=True)  72.2 us
    psum x1, blocking collectives, on_device(): small = lax.psum(small, ('replica', 'shard'))  72.2 us
    dot_general x4, matrix products, contract_last(): lax.dot_general(left, right, (((1,), (1,)), ((), ())), preferred_element_...  44.3 us
  transfers between devices with their start and end apart: 26, of which 19 were waited for; matrix products, arithmetic and copies ran while one was open for 17% of the time, Pallas kernels for 29%

profile of v2, /device:TPU:9, one launch (start us, length us, event | category | flops | bytes accessed | tf_op | source)
XLA Modules:
  0.0 1027.8 jit_solution(1195020882992918705)
XLA Ops:
  22.7 11.1 %collective-permute-done.2 = bf16[1,64,2048]{2,1,0:T(8,128)(2,1)S(1)} collective-permute-done((bf16[1,64,2048]{2,1,0:T(8,128)(2,1)S(1)}, bf16[1,64,2048]{2,1,0:T(8,128)(2,1)S(1)}, u32[]{:S(2)}, u32[]{:S(2)}) %collective-permute-start.2) | collective-permute-done | bytes 262176 | tf_op jit(solution)/shard_map/ppermute | solution.py:668
  58.8 14.4 %collective-permute-done.5 = bf16[1,64,2816]{2,1,0:T(8,128)(2,1)} collective-permute-done((bf16[1,64,2816]{2,1,0:T(8,128)(2,1)S(1)}, bf16[1,64,2816]{2,1,0:T(8,128)(2,1)}, u32[]{:S(2)}, u32[]{:S(2)}) %collective-permute-start.5) | collective-permute-done | bytes 360480 | tf_op jit(solution)/shard_map/ppermute | solution.py:668
  78.1 93.8 %start.1 = (bf16[4,192,2048]{2,1,0:T(8,128)(2,1)}, f32[4,8,512]{2,1,0:T(8,128)S(1)}, bf16[768,2048]{1,0:T(8,128)(2,1)}, bf16[768,1536]{1,0:T(8,128)(2,1)S(1)}, bf16[2048,1536]{1,0:T(8,128)(2,1)}) custom-call(bf16[192,2048]{1,0:T(8,128)(2,1)S(1)} %copy-done.2, f32[8,512]{1,0:T(8,128)S(1)} %reshape.289.vectors, bf16[512,6144]{1,0:T(8,128)(2,1)} %weight.1, ...), custom_call_target="tpu_custom_call" | custom-call | flops 4831838208 | bytes 150000000 | tf_op jit(solution)/shard_map/start/pallas_call | solution.py:292
  176.0 122.9 %attend.1 = (bf16[768,2048]{1,0:T(8,128)(2,1)}, f32[768,128]{1,0:T(8,128)S(1)}) custom-call(bf16[768,1536]{1,0:T(8,128)(2,1)S(1)} %copy-done.6, s32[768,128]{1,0:T(8,128)S(1)} %broadcast_in_dim.17.seg_rows, s32[8,768]{1,0:T(8,128)S(1)} %broadcast_in_dim.18.seg_columns), custom_call_target="tpu_custom_call" | custom-call | flops 1000000000 | bytes 150000000 | tf_op jit(solution)/shard_map/attend/pallas_call | solution.py:424
  307.6 10.6 %fusion.22 = (f32[768]{0:T(1024)S(1)}, f32[768,2048]{1,0:T(8,128)S(1)}) fusion(bf16[768,2048]{1,0:T(8,128)(2,1)} %get-tuple-element.27, bf16[2048,2048]{1,0:T(8,128)(2,1)} %bitcast.142, bf16[768,2048]{1,0:T(8,128)(2,1)} %bitcast.145), kind=kOutput, calls=%fused_computation.100 | convolution fusion | flops 6447168512 | bytes 20974592 | tf_op jit(solution)/shard_map/dot_general | solution.py:814
  336.1 11.3 %fusion.23 = f32[768,2816]{1,0:T(8,128)} fusion(bf16[768,2048]{1,0:T(8,128)(2,1)S(1)} %copy-done.8, bf16[2048,2816]{1,0:T(8,128)(2,1)S(1)} %bitcast.108), kind=kOutput, calls=%fused_computation.101 | convolution fusion | flops 8858370048 | bytes 23330816 | tf_op jit(solution)/shard_map/dot_general | solution.py:817
  347.4 13.9 %fusion.14 = (f32[768,1408]{1,0:T(8,128)}, f32[768,1408]{1,0:T(8,128)}, bf16[768,1408]{1,0:T(8,128)(2,1)}) fusion(f32[768,2816]{1,0:T(8,128)} %fusion.23, bf16[768,2048]{1,0:T(8,128)(2,1)} %all-gather.11.cloned.1.call-done, bf16[1408,2048]{1,0:T(8,128)(2,1)} %param.18), kind=kOutput, calls=%fused_computation.39 | convolution fusion | flops 4444323840 | bytes 28377088 | tf_op jit(solution)/shard_map/dot_general | solution.py:40
  361.4 15.1 %convolution_convert_fusion.4 = bf16[768,2048]{1,0:T(8,128)(2,1)S(1)} fusion(bf16[2048,2816]{1,0:T(8,128)(2,1)} %bitcast.109, f32[768,1408]{1,0:T(8,128)} %get-tuple-element.52, f32[768,1408]{1,0:T(8,128)} %get-tuple-element.51), kind=kOutput, calls=%fused_computation.15 | convolution fusion | flops 8864268288 | bytes 23330816 | tf_op jit(solution)/shard_map/dot_general | solution.py:40
  376.5 58.0 %scatter.2 = f32[192,2048]{1,0:T(8,128)S(1)} custom-call(bf16[4,192,2048]{2,1,0:T(8,128)(2,1)S(1)} %bitcast.103), custom_call_target="tpu_custom_call" | custom-call | bytes 200000000 | tf_op jit(solution)/shard_map/scatter/pallas_call | solution.py:589
  447.6 35.8 %exchange.1 = (bf16[4,192,512]{2,1,0:T(8,128)(2,1)}, bf16[4,192,512]{2,1,0:T(8,128)(2,1)}) custom-call(bf16[192,2048]{1,0:T(8,128)(2,1)} %convolution_convert_fusion.7.first, bf16[192,2048]{1,0:T(8,128)(2,1)} %copy-done.13), custom_call_target="tpu_custom_call" | custom-call | bytes 100000000 | tf_op jit(solution)/shard_map/exchange/pallas_call | solution.py:649
  496.2 23.1 %attend_back.1 = (bf16[768,1536]{1,0:T(8,128)(2,1)}, f32[8,1536]{1,0:T(8,128)S(1)}) custom-call(bf16[768,1536]{1,0:T(8,128)(2,1)} %copy-done.5, bf16[768,512]{1,0:T(8,128)(2,1)S(1)} %bitcast.104, f32[768,128]{1,0:T(8,128)S(1)} %get-tuple-element.31.stats, s32[768,128]{1,0:T(8,128)S(1)} %broadcast_in_dim.17.seg_rows, ...), custom_call_target="tpu_custom_call" | custom-call | flops 3000000000 | bytes 100000000 | tf_op jit(solution)/shard_map/attend_back/pallas_call | solution.py:513
  534.8 15.1 %convolution_convert_fusion = bf16[2048,2816]{1,0:T(8,128)(2,1)} fusion(bf16[768,2048]{0,1:T(8,128)(2,1)S(1)} %bitcast.117, f32[768,1408]{1,0:T(8,128)} %get-tuple-element.52, f32[768,1408]{1,0:T(8,128)} %get-tuple-element.51), kind=kOutput, calls=%fused_computation | convolution fusion | flops 8868462592 | bytes 23330816 | tf_op jit(solution)/shard_map/dot_general | solution.py:504
  550.2 10.3 %convolution_convert_fusion.2 = bf16[1408,2048]{1,0:T(8,128)(2,1)} fusion(bf16[768,1408]{1,0:T(8,128)(2,1)} %get-tuple-element.53, bf16[768,2048]{1,0:T(8,128)(2,1)} %all-gather.11.cloned.1.call-done), kind=kOutput, calls=%fused_computation.3 | convolution fusion | flops 4432068608 | bytes 11075584 | tf_op jit(solution)/shard_map/dot_general | solution.py:504
  580.7 15.5 %reduce-scatter.7.cloned.1.call-done = bf16[256,1536]{1,0:T(8,128)(2,1)} async-done(((bf16[2048,1536]{1,0:T(8,128)(2,1)}), bf16[256,1536]{1,0:T(8,128)(2,1)}) %reduce-scatter.7.cloned.1.call-update) | async-done | bytes 786448 | tf_op jit(solution)/shard_map/reduce_scatter | solution.py:707
  606.9 13.0 %collective-permute-done.7 = bf16[1,64,1536]{2,1,0:T(8,128)(2,1)S(1)} collective-permute-done((bf16[1,64,1536]{2,1,0:T(8,128)(2,1)S(1)}, bf16[1,64,1536]{2,1,0:T(8,128)(2,1)S(1)}, u32[]{:S(2)}, u32[]{:S(2)}) %collective-permute-start.7) | collective-permute-done | bytes 196640 | tf_op jit(solution)/shard_map/ppermute | solution.py:668
  630.4 56.7 %reduce-scatter.11.cloned.1.call-done = bf16[256,2816]{1,0:T(8,128)(2,1)} async-done(((bf16[2048,2816]{1,0:T(8,128)(2,1)}), bf16[256,2816]{1,0:T(8,128)(2,1)}) %reduce-scatter.11.cloned.1.call-update) | async-done | bytes 1441808 | tf_op jit(solution)/shard_map/reduce_scatter | solution.py:707
  688.3 9.0 collective-permute-done.12
  701.5 23.6 %collective-permute-done.13 = bf16[1,64,2816]{2,1,0:T(8,128)(2,1)S(1)} collective-permute-done((bf16[1,64,2816]{2,1,0:T(8,128)(2,1)S(1)}, bf16[1,64,2816]{2,1,0:T(8,128)(2,1)S(1)}, u32[]{:S(2)}, u32[]{:S(2)}) %collective-permute-start.13) | collective-permute-done | bytes 360480 | tf_op jit(solution)/shard_map/ppermute | solution.py:668
  752.1 58.4 %scatter.3 = f32[192,2048]{1,0:T(8,128)S(1)} custom-call(bf16[4,192,2048]{2,1,0:T(8,128)(2,1)S(1)} %bitcast.102), custom_call_target="tpu_custom_call" | custom-call | bytes 200000000 | tf_op jit(solution)/shard_map/scatter/pallas_call | solution.py:589
  811.6 72.2 %psum.14 = f32[4,3584]{1,0:T(4,128)S(1)} all-reduce(f32[4,3584]{1,0:T(4,128)S(1)} %constant_dynamic-update-slice_fusion), channel_id=1, replica_groups=mesh['replica'=8,'shard'=4] {'replica','shard'}, use_global_device_ids=true, to_apply=%region_17.18 | all-reduce | flops 14336 | bytes 114688 | tf_op jit(solution)/shard_map/psum | solution.py:863
  904.0 34.0 %all-gather.13.cloned.1.call-done = bf16[512,6144]{1,0:T(8,128)(2,1)} async-done(((bf16[64,6144]{1,0:T(8,128)(2,1)}), bf16[512,6144]{1,0:T(8,128)(2,1)}) %all-gather.13.cloned.1.call-update) | async-done | bytes 6291472 | tf_op jit(solution)/shard_map/all_gather | solution.py:711
  938.0 9.2 convert_element_type.102
  947.2 60.6 %all-gather.17.cloned.1.call-done = bf16[512,11264]{1,0:T(8,128)(2,1)} async-done(((bf16[64,11264]{1,0:T(8,128)(2,1)}), bf16[512,11264]{1,0:T(8,128)(2,1)}) %all-gather.17.cloned.1.call-update) | async-done | bytes 11534352 | tf_op jit(solution)/shard_map/all_gather | solution.py:711
  1007.8 13.0 %convert_element_type.106 = f32[512,11264]{1,0:T(8,128)} convert(bf16[512,11264]{1,0:T(8,128)(2,1)} %all-gather.17.cloned.1.call-done) | non-fusion elementwise | flops 5767168 | bytes 34603008 | tf_op jit(solution)/shard_map/convert_element_type | solution.py:711
  (207 shorter events, 212.0 us)
Async XLA Ops:
  7.2 300.4 %all-gather.7.cloned.1.call-start = ((), (), s32[]{:S(2)}) async-start(), calls=%async_computation.4 | async-start | bytes 9437184 | tf_op jit(solution)/shard_map/all_gather | solution.py:691
  8.8 10.1 collective-permute-start
  8.9 13.8 %collective-permute-start.1 = (bf16[1,64,2048]{2,1,0:T(8,128)(2,1)S(1)}, bf16[1,64,2048]{2,1,0:T(8,128)(2,1)S(1)}, u32[]{:S(2)}, u32[]{:S(2)}) collective-permute-start(bf16[1,64,2048]{2,1,0:T(8,128)(2,1)S(1)} %fusion.44), channel_id=1, source_target_pairs={{0,2},{1,3},{2,0},{3,1},{4,6},{5,7},{6,4},{7,5},{8,10},{9,11},{10,... | collective-permute-start | bytes 786440 | tf_op jit(solution)/shard_map/ppermute | solution.py:668
  11.3 22.5 %collective-permute-start.2 = (bf16[1,64,2048]{2,1,0:T(8,128)(2,1)S(1)}, bf16[1,64,2048]{2,1,0:T(8,128)(2,1)S(1)}, u32[]{:S(2)}, u32[]{:S(2)}) collective-permute-start(bf16[1,64,2048]{2,1,0:T(8,128)(2,1)S(1)} %fusion.44), channel_id=1, source_target_pairs={{0,3},{1,2},{2,1},{3,0},{4,7},{5,6},{6,5},{7,4},{8,11},{9,10},{10,... | collective-permute-start | bytes 786440 | tf_op jit(solution)/shard_map/ppermute | solution.py:668
  34.9 290.4 %all-gather.9.cloned.1.call-start = ((), (), s32[]{:S(2)}) async-start(), calls=%async_computation.5 | async-start | bytes 12976128 | tf_op jit(solution)/shard_map/all_gather | solution.py:683
  40.6 12.5 %collective-permute-start.3 = (bf16[1,64,2816]{2,1,0:T(8,128)(2,1)}, bf16[1,64,2816]{2,1,0:T(8,128)(2,1)}, u32[]{:S(2)}, u32[]{:S(2)}) collective-permute-start(bf16[1,64,2816]{2,1,0:T(8,128)(2,1)} %get-tuple-element.59), channel_id=1, source_target_pairs={{0,1},{1,0},{2,3},{3,2},{4,5},{5,4},{6,7},{7,6},{8,9},{9,8},{10,11... | collective-permute-start | bytes 1081352 | tf_op jit(solution)/shard_map/ppermute | solution.py:668
  40.6 17.2 %collective-permute-start.4 = (bf16[1,64,2816]{2,1,0:T(8,128)(2,1)}, bf16[1,64,2816]{2,1,0:T(8,128)(2,1)}, u32[]{:S(2)}, u32[]{:S(2)}) collective-permute-start(bf16[1,64,2816]{2,1,0:T(8,128)(2,1)} %get-tuple-element.58), channel_id=1, source_target_pairs={{0,2},{1,3},{2,0},{3,1},{4,6},{5,7},{6,4},{7,5},{8,10},{9,11},{10,... | collective-permute-start | bytes 1081352 | tf_op jit(solution)/shard_map/ppermute | solution.py:668
  43.1 30.1 %collective-permute-start.5 = (bf16[1,64,2816]{2,1,0:T(8,128)(2,1)S(1)}, bf16[1,64,2816]{2,1,0:T(8,128)(2,1)}, u32[]{:S(2)}, u32[]{:S(2)}) collective-permute-start(bf16[1,64,2816]{2,1,0:T(8,128)(2,1)S(1)} %get-tuple-element.57), channel_id=1, source_target_pairs={{0,3},{1,2},{2,1},{3,0},{4,7},{5,6},{6,5},{7,4},{8,11},{9,10},{10,... | collective-permute-start | bytes 1081352 | tf_op jit(solution)/shard_map/ppermute | solution.py:668
  75.3 272.2 %all-gather.11.cloned.1.call-start = ((), (), s32[]{:S(2)}) async-start(), calls=%async_computation.7 | async-start | bytes 3932160 | tf_op jit(solution)/shard_map/all_gather | solution.py:807
  173.4 396.1 %reduce-scatter.9.cloned.1.call-start = ((), (), s32[]{:S(2)}) async-start(), calls=%async_computation.10 | async-start | bytes 2359296 | tf_op jit(solution)/shard_map/reduce_scatter | solution.py:707
  488.8 107.5 %reduce-scatter.7.cloned.1.call-start = ((), (), s32[]{:S(2)}) async-start(), calls=%async_computation.8 | async-start | bytes 7077888 | tf_op jit(solution)/shard_map/reduce_scatter | solution.py:707
  527.9 159.1 %reduce-scatter.11.cloned.1.call-start = ((), (), s32[]{:S(2)}) async-start(), calls=%async_computation.12 | async-start | bytes 12976128 | tf_op jit(solution)/shard_map/reduce_scatter | solution.py:707
  550.0 338.3 %all-reduce.4.cloned.1.call-start = ((), (), s32[]{:S(2)}) async-start(), calls=%async_computation.14 | async-start | bytes 11534336 | tf_op jit(solution)/shard_map/psum | solution.py:847
  560.6 336.4 %reduce-scatter.5.cloned.1.call-start = ((), (), s32[]{:S(2)}) async-start(), calls=%async_computation.6 | async-start | bytes 3932160 | tf_op jit(solution)/shard_map/reduce_scatter | solution.py:845
  569.5 330.2 %all-gather.15.cloned.1.call-start = ((), (), s32[]{:S(2)}) async-start(), calls=%async_computation.11 | async-start | bytes 2359296 | tf_op jit(solution)/shard_map/all_gather | solution.py:711
  571.6 6.5 collective-permute-start.11
  580.7 357.3 %all-gather.13.cloned.1.call-start = ((), (), s32[]{:S(2)}) async-start(), calls=%async_computation.9 | async-start | bytes 7077888 | tf_op jit(solution)/shard_map/all_gather | solution.py:711
  597.2 5.8 collective-permute-start.6
  604.8 15.1 %collective-permute-start.7 = (bf16[1,64,1536]{2,1,0:T(8,128)(2,1)S(1)}, bf16[1,64,1536]{2,1,0:T(8,128)(2,1)S(1)}, u32[]{:S(2)}, u32[]{:S(2)}) collective-permute-start(bf16[1,64,1536]{2,1,0:T(8,128)(2,1)S(1)} %get-tuple-element.61), channel_id=1, source_target_pairs={{0,2},{1,3},{2,0},{3,1},{4,6},{5,7},{6,4},{7,5},{8,10},{9,11},{10,... | collective-permute-start | bytes 589832 | tf_op jit(solution)/shard_map/ppermute | solution.py:668
  606.9 17.2 %collective-permute-start.8 = (bf16[1,64,1536]{2,1,0:T(8,128)(2,1)S(1)}, bf16[1,64,1536]{2,1,0:T(8,128)(2,1)S(1)}, u32[]{:S(2)}, u32[]{:S(2)}) collective-permute-start(bf16[1,64,1536]{2,1,0:T(8,128)(2,1)S(1)} %get-tuple-element.60), channel_id=1, source_target_pairs={{0,3},{1,2},{2,1},{3,0},{4,7},{5,6},{6,5},{7,4},{8,11},{9,10},{10,... | collective-permute-start | bytes 589832 | tf_op jit(solution)/shard_map/ppermute | solution.py:668
  630.0 377.7 %all-gather.17.cloned.1.call-start = ((), (), s32[]{:S(2)}) async-start(), calls=%async_computation.13 | async-start | bytes 12976128 | tf_op jit(solution)/shard_map/all_gather | solution.py:711
  688.0 9.4 collective-permute-start.12
  699.3 25.7 %collective-permute-start.13 = (bf16[1,64,2816]{2,1,0:T(8,128)(2,1)S(1)}, bf16[1,64,2816]{2,1,0:T(8,128)(2,1)S(1)}, u32[]{:S(2)}, u32[]{:S(2)}) collective-permute-start(bf16[1,64,2816]{2,1,0:T(8,128)(2,1)S(1)} %get-tuple-element.55), channel_id=1, source_target_pairs={{0,2},{1,3},{2,0},{3,1},{4,6},{5,7},{6,4},{7,5},{8,10},{9,11},{10,... | collective-permute-start | bytes 1081352 | tf_op jit(solution)/shard_map/ppermute | solution.py:668
  701.5 31.3 %collective-permute-start.14 = (bf16[1,64,2816]{2,1,0:T(8,128)(2,1)S(1)}, bf16[1,64,2816]{2,1,0:T(8,128)(2,1)S(1)}, u32[]{:S(2)}, u32[]{:S(2)}) collective-permute-start(bf16[1,64,2816]{2,1,0:T(8,128)(2,1)S(1)} %get-tuple-element.54), channel_id=1, source_target_pairs={{0,3},{1,2},{2,1},{3,0},{4,7},{5,6},{6,5},{7,4},{8,11},{9,10},{10,... | collective-permute-start | bytes 1081352 | tf_op jit(solution)/shard_map/ppermute | solution.py:668
  (23 other events, 427.9 us)
Sparse Core Ops, SparseCore 0:
  35.0 59.8 all-gather.6
  97.4 82.8 all-gather.8
  181.9 96.5 all-gather.10
  488.9 41.3 reduce-scatter.8
  534.5 61.7 reduce-scatter.6
  600.2 86.7 reduce-scatter.10
  690.9 98.2 all-reduce.3
  792.2 68.9 reduce-scatter.4
  863.3 26.5 all-gather.14
  892.3 45.6 all-gather.12
  940.1 67.6 all-gather.16

commit v3 on v2

--- a/solution.py
+++ b/solution.py
@@ -441,8 +441,12 @@
     )(qkv, seg_rows, seg_columns)
 
 
-def attend_back_kernel(rows, qkv, d_attended, stats, seg_rows, seg_columns, cosine, minus, plus,
-                       d_qkv, bias_grad, d_keys, d_values):
+def attend_back_kernel(rows, *refs):
+    attend_back_body(rows, *refs, [])
+
+
+def attend_back_body(rows, qkv, d_attended, stats, seg_rows, seg_columns, cosine, minus, plus,
+                     d_qkv, bias_grad, d_keys, d_values, steps):
     width = qkv.shape[1] // 3
     group = qkv.shape[0]
     blocks = group // rows
@@ -494,6 +498,8 @@
             d_qkv[at:count, width + 128 * pair : width + 128 * pair + 128] = k_out
             v_out = d_values[at:count, lanes].astype(jnp.bfloat16)
             d_qkv[at:count, 2 * width + 128 * pair : 2 * width + 128 * pair + 128] = v_out
+            if steps:
+                steps.pop(0)()
     for part in range(3 * pairs):
         lanes = slice(128 * part, 128 * part + 128)
         bias_grad[:, lanes] = jnp.broadcast_to(
@@ -658,6 +664,588 @@
     )(first, second)
 
 
+class Cube:
+    def __init__(self):
+        r = lax.axis_index("replica")
+        self.core, self.x, self.y = r % 2, (r // 2) % 2, r // 4
+        self.place = 2 * self.y + self.x
+        self.to_x = {"replica": r + 2 - 4 * self.x}
+        self.to_y = {"replica": r + 4 - 8 * self.y}
+        self.to_core = {"replica": r + 1 - 2 * self.core}
+
+    def partners(self, shards):
+        z = lax.axis_index("shard")
+        return [((z != o), {"shard": o}) for o in range(shards)] + [
+            (z >= 0, d) for d in (self.to_x, self.to_y, self.to_core)
+        ]
+
+
+def rows_of(ref, start, unit, count):
+    return ref.at[pl.ds(pl.multiple_of(start, unit), count)]
+
+
+def add_rows(target, source, count):
+    step = 16
+
+    @pl.loop(0, count // step)
+    def _(i):
+        block = pl.ds(aligned(i, step), step)
+        target[block, :] = (
+            target[block, :].astype(jnp.float32) + source[block, :].astype(jnp.float32)
+        ).astype(target.dtype)
+
+
+class Reducer:
+    def __init__(self, cube, share, term, core, near, last, send, recv):
+        self.cube, self.share = cube, share
+        self.cut = 16 * ((share // 16 + 1) // 2)
+        self.term, self.core, self.near, self.last = term, core, near, last
+        self.send, self.recv = send, recv
+        self.chunks = term.shape[0]
+
+    def share_rows(self, chunk, place, half):
+        first, count = (0, self.cut) if half == 0 else (self.cut, self.share - self.cut)
+        start = self.cube.core * 4 * self.share + place * self.share + first
+        return rows_of(self.term.at[chunk], start, 16, count)
+
+    def own(self, chunk):
+        start = (self.cube.core * 4 + self.cube.place) * self.share
+        return rows_of(self.term.at[chunk], start, 16, self.share)
+
+    def core_copy(self, chunk):
+        source = rows_of(self.term.at[chunk], (1 - self.cube.core) * 4 * self.share, 16, 4 * self.share)
+        return remote(source, self.core.at[chunk], self.send.at[chunk, 0], self.recv.at[chunk, 0], self.cube.to_core)
+
+    def near_place(self, half, other):
+        c = self.cube
+        if half == 0:
+            return 2 * other + (1 - c.x), 2 * other + c.x
+        return 2 * (1 - c.y) + other, 2 * c.y + other
+
+    def near_slot(self, chunk, half, other):
+        count = self.cut if half == 0 else self.share - self.cut
+        start = other * count + (2 * self.cut if half == 1 else 0)
+        return self.near.at[chunk, pl.ds(start, count)]
+
+    def near_copy(self, chunk, half, other):
+        source = self.share_rows(chunk, self.near_place(half, other)[0], half)
+        slot = 1 + 2 * half + other
+        device = self.cube.to_x if half == 0 else self.cube.to_y
+        return remote(source, self.near_slot(chunk, half, other), self.send.at[chunk, slot], self.recv.at[chunk, slot], device)
+
+    def last_slot(self, chunk, half):
+        first, count = (0, self.cut) if half == 0 else (self.cut, self.share - self.cut)
+        return self.last.at[chunk, pl.ds(first, count)]
+
+    def last_copy(self, chunk, half):
+        c = self.cube
+        place = 2 * (1 - c.y) + c.x if half == 0 else 2 * c.y + (1 - c.x)
+        device = c.to_y if half == 0 else c.to_x
+        source = self.share_rows(chunk, place, half)
+        return remote(source, self.last_slot(chunk, half), self.send.at[chunk, 5 + half], self.recv.at[chunk, 5 + half], device)
+
+    def start(self, chunk):
+        self.core_copy(chunk).start()
+
+    def after_core(self, chunk):
+        self.core_copy(chunk).wait_recv()
+        mine = rows_of(self.term.at[chunk], self.cube.core * 4 * self.share, 16, 4 * self.share)
+        add_rows(mine, self.core.at[chunk], 4 * self.share)
+        for half in (0, 1):
+            for other in (0, 1):
+                self.near_copy(chunk, half, other).start()
+
+    def after_near(self, chunk):
+        for half in (0, 1):
+            count = self.cut if half == 0 else self.share - self.cut
+            for other in (0, 1):
+                self.near_copy(chunk, half, other).wait_recv()
+                stays = self.share_rows(chunk, self.near_place(half, other)[1], half)
+                add_rows(stays, self.near_slot(chunk, half, other), count)
+            self.last_copy(chunk, half).start()
+
+    def after_last(self, chunk):
+        c = self.cube
+        for half in (0, 1):
+            count = self.cut if half == 0 else self.share - self.cut
+            self.last_copy(chunk, half).wait_recv()
+            add_rows(self.share_rows(chunk, c.place, half), self.last_slot(chunk, half), count)
+
+    def finish(self, chunk):
+        self.core_copy(chunk).wait_send()
+        for half in (0, 1):
+            for other in (0, 1):
+                self.near_copy(chunk, half, other).wait_send()
+            self.last_copy(chunk, half).wait_send()
+
+
+class Owners:
+    def __init__(self, cube, shards, share, parts, reducer, out, send, recv, loc):
+        self.cube, self.shards, self.share, self.parts = cube, shards, share, parts
+        self.source, self.out, self.send, self.recv, self.loc = reducer, out, send, recv, loc
+        self.z = lax.axis_index("shard")
+
+    def target(self, shard, part):
+        width = self.out.shape[1] // (self.shards * self.parts)
+        start = (self.cube.core * 4 + self.cube.place) * self.share
+        return self.out.at[
+            pl.ds(pl.multiple_of(start, 16), self.share), pl.ds(aligned(part * self.shards + shard, width), width)
+        ]
+
+    def piece(self, o, part):
+        width = self.out.shape[1] // (self.shards * self.parts)
+        return self.source(o).at[:, pl.ds(part * width, width)]
+
+    def copy(self, o, part):
+        return remote(self.piece(o, part), self.target(self.z, part), self.send.at[o, part], self.recv.at[self.z, part], {"shard": o})
+
+    def arrival(self, o, part):
+        place = self.target(o, part)
+        return remote(place, place, self.send.at[o, part], self.recv.at[o, part], {"shard": o})
+
+    def local(self, o, part):
+        return pltpu.make_async_copy(self.piece(o, part), self.target(o, part), self.loc.at[part])
+
+    def start(self, o):
+        for part in range(self.parts):
+            @pl.when(self.z != o)
+            def _():
+                self.copy(o, part).start()
+
+            @pl.when(self.z == o)
+            def _():
+                self.local(o, part).start()
+
+    def arrive(self):
+        for o in range(self.shards):
+            for part in range(self.parts):
+                @pl.when(self.z != o)
+                def _():
+                    self.arrival(o, part).wait_recv()
+
+                @pl.when(self.z == o)
+                def _():
+                    self.local(o, part).wait()
+
+    def finish(self):
+        for o in range(self.shards):
+            for part in range(self.parts):
+                @pl.when(self.z != o)
+                def _():
+                    self.copy(o, part).wait_send()
+
+
+class Gatherer:
+    def __init__(self, cube, share, out, send, recv):
+        self.cube, self.share, self.out, self.send, self.recv = cube, share, out, send, recv
+        self.cut = 16 * ((share // 16 + 1) // 2)
+
+    def rows(self, place, half=None):
+        first, count = {None: (0, self.share), 0: (0, self.cut), 1: (self.cut, self.share - self.cut)}[half]
+        start = (self.cube.core * 4 + place) * self.share + first
+        return rows_of(self.out, start, 16, count)
+
+    def copy(self, kind):
+        c = self.cube
+        at_x, at_y = 2 * c.y + 1 - c.x, 2 * (1 - c.y) + c.x
+        block, device = (
+            (self.rows(c.place), c.to_x),
+            (self.rows(c.place), c.to_y),
+            (self.rows(at_x, 0), c.to_y),
+            (self.rows(at_y, 1), c.to_x),
+            (self.rows(c.place), c.to_core),
+            (self.rows(at_x), c.to_core),
+            (self.rows(at_y), c.to_core),
+            (self.rows(3 - c.place), c.to_core),
+        )[kind]
+        return remote(block, block, self.send.at[kind], self.recv.at[kind], device)
+
+    def start(self):
+        for kind in (0, 1, 4):
+            self.copy(kind).start()
+
+    def pass_on(self):
+        self.copy(0).wait_recv()
+        self.copy(2).start()
+        self.copy(1).wait_recv()
+        self.copy(3).start()
+        self.copy(5).start()
+        self.copy(6).start()
+
+    def pass_last(self):
+        self.copy(2).wait_recv()
+        self.copy(3).wait_recv()
+        self.copy(7).start()
+
+    def finish(self):
+        for kind in (4, 5, 6, 7):
+            self.copy(kind).wait_recv()
+        for kind in range(8):
+            self.copy(kind).wait_send()
+
+
+class LineSum:
+    def __init__(self, shards, cuts, own, got, send, recv):
+        self.z = lax.axis_index("shard")
+        self.shards, self.cuts, self.own, self.got, self.send, self.recv = shards, cuts, own, got, send, recv
+        self.step = own.shape[1] // cuts
+
+    def piece(self, cut):
+        return pl.ds(cut * self.step, self.step)
+
+    def copy(self, way, block, cut, source=None):
+        target = self.z + 1 if way == 0 else self.z - 1
+        place = self.got.at[way, block, self.piece(cut)]
+        return remote(place if source is None else source, place, self.send.at[way, block, cut], self.recv.at[way, block, cut], {"shard": target})
+
+    def order(self, t):
+        last = self.z // (self.shards - 1)
+        return self.shards - 1 - t + last * (2 * t - self.shards + 1)
+
+    def ready(self, block):
+        for way in (0, 1):
+            @pl.when((self.z == (0 if way == 0 else self.shards - 1)) & (block != self.z))
+            def _():
+                for cut in range(self.cuts):
+                    self.copy(way, block, cut, self.own.at[block, self.piece(cut)]).start()
+
+    def step_on(self, far, cut):
+        for way in (0, 1):
+            block = self.shards - 1 - far if way == 0 else far
+            sends = (self.z < block) & (self.z > 0) if way == 0 else (self.z > block) & (self.z < self.shards - 1)
+
+            @pl.when(sends)
+            def _():
+                self.copy(way, block, cut).wait_recv()
+                place = self.got.at[way, block, self.piece(cut)]
+                add_rows(place, self.own.at[block, self.piece(cut)], self.step)
+                self.copy(way, block, cut).start()
+
+    def result(self, total):
+        rows = self.own.shape[1]
+        for way in (0, 1):
+            @pl.when(self.z >= 1 if way == 0 else self.z + 1 < self.shards)
+            def _():
+                for cut in range(self.cuts):
+                    self.copy(way, self.z, cut).wait_recv()
+
+        @pl.loop(0, rows // 16)
+        def _(i):
+            block = pl.ds(aligned(i, 16), 16)
+            total[block, :] = self.own[self.z, block, :].astype(jnp.float32)
+
+            @pl.when(self.z >= 1)
+            def _():
+                total[block, :] += self.got[0, self.z, block, :].astype(jnp.float32)
+
+            @pl.when(self.z + 1 < self.shards)
+            def _():
+                total[block, :] += self.got[1, self.z, block, :].astype(jnp.float32)
+
+    def finish(self):
+        for far in range(self.shards - 1):
+            for cut in range(self.cuts):
+                for way in (0, 1):
+                    block = self.shards - 1 - far if way == 0 else far
+
+                    @pl.when(self.z < block if way == 0 else self.z > block)
+                    def _():
+                        self.copy(way, block, cut).wait_send()
+
+
+def line_scratch(shards, rows, columns, cuts):
+    dma = pltpu.SemaphoreType.DMA
+    return [
+        pltpu.VMEM((shards, rows, columns), jnp.bfloat16),
+        pltpu.VMEM((2, shards, rows, columns), jnp.bfloat16),
+        dma((2, shards, cuts)), dma((2, shards, cuts)),
+    ]
+
+
+def reducer_scratch(chunks, share, columns):
+    dma = pltpu.SemaphoreType.DMA
+    return [pltpu.VMEM((chunks, n * share, columns), jnp.bfloat16) for n in (8, 4, 2, 1)] + [
+        dma((chunks, 7)), dma((chunks, 7)),
+    ]
+
+
+def block_product(own, block, slopes, weight, tile=256):
+    rows = own.shape[1]
+
+    @pl.loop(0, own.shape[2] // tile)
+    def _(t):
+        columns = pl.ds(aligned(t, tile), tile)
+        value = contract_last(slopes[pl.ds(aligned(block, rows), rows), :], weight[columns, :])
+        own[block, :, columns] = value.astype(own.dtype)
+
+
+def term_product(term, chunk, left, right, tile):
+    columns = right.shape[1]
+
+    @pl.loop(0, columns // tile)
+    def _(t):
+        place = pl.ds(aligned(t, tile), tile)
+        term[chunk, :, place] = contract_first(left[...], right[:, place]).astype(term.dtype)
+
+
+def hidden_back_kernel(shards, slopes, weight, hidden, cotangent, total, down_grad,
+                       own, got, z_send, z_recv, term, core, near, last, r_send, r_recv,
+                       share_send, share_recv, loc):
+    cube = Cube()
+    z = lax.axis_index("shard")
+    greet(cube.partners(shards), shards + 2)
+    line = LineSum(shards, 3, own, got, z_send, z_recv)
+    share = hidden.shape[1] // 8
+    chunks = term.shape[0]
+    columns = term.shape[2]
+    reducer = Reducer(cube, share, term, core, near, last, r_send, r_recv)
+    gatherer = Gatherer(cube, share, down_grad, share_send, share_recv)
+    for k in range(chunks):
+        term[k] = contract_first(hidden[...], cotangent[:, k * columns : (k + 1) * columns]).astype(term.dtype)
+        reducer.start(k)
+    for t in range(shards):
+        block = line.order(t)
+        block_product(own, block, slopes, weight)
+        line.ready(block)
+        if t < chunks:
+            reducer.after_core(t)
+    for t in range(shards, chunks):
+        reducer.after_core(t)
+    steps = [functools.partial(reducer.after_near, k) for k in range(chunks)]
+    steps += [functools.partial(reducer.after_last, k) for k in range(chunks)]
+    moves = [functools.partial(line.step_on, far, cut) for far in range(shards - 1) for cut in range(3)]
+    for i in range(max(len(steps), len(moves))):
+        if i < len(moves):
+            moves[i]()
+        if i < len(steps):
+            steps[i]()
+    keep = []
+    for k in range(chunks):
+        target = down_grad.at[pl.ds(pl.multiple_of((cube.core * 4 + cube.place) * share, 16), share), pl.ds(k * columns, columns)]
+        copy = pltpu.make_async_copy(reducer.own(k), target, loc.at[k])
+        copy.start()
+        keep.append(copy)
+    for copy in keep:
+        copy.wait()
+    gatherer.start()
+    line.result(total)
+    gatherer.pass_on()
+    gatherer.pass_last()
+    line.finish()
+    for k in range(chunks):
+        reducer.finish(k)
+    gatherer.finish()
+
+
+def hidden_back_call(shards, slopes, weight, hidden, cotangent):
+    group, inner = hidden.shape
+    rows = group // shards
+    share = inner // 8
+    chunks = 4
+    vm = pl.BlockSpec(memory_space=pltpu.VMEM)
+    dma = pltpu.SemaphoreType.DMA
+    return pl.pallas_call(
+        functools.partial(hidden_back_kernel, shards),
+        out_shape=[jax.ShapeDtypeStruct((rows, D), jnp.float32), jax.ShapeDtypeStruct((inner, D), jnp.bfloat16)],
+        in_specs=[vm] * 4,
+        out_specs=[vm, pl.BlockSpec(memory_space=pl.ANY)],
+        scratch_shapes=line_scratch(shards, rows, D, 3) + reducer_scratch(chunks, share, D // chunks)
+        + [dma((8,)), dma((8,)), dma((chunks,))],
+        compiler_params=pltpu.CompilerParams(collective_id=6, has_side_effects=True, vmem_limit_bytes=56 * 2**20),
+        name="hidden_back",
+        cost_estimate=pl.CostEstimate(flops=10**10, bytes_accessed=200 * 10**6, transcendentals=0),
+    )(slopes, weight, hidden, cotangent)
+
+
+def heads_back_kernel(shards, rows, d_attended_own, d_middle_own, qkv, stats, seg_rows, seg_columns, cosine, minus, plus,
+                      normed_two, slopes, d_qkv, bias_grad, d_middle_columns, share_out,
+                      d_keys, d_values, d_attended, term, core, near, last, r_send, r_recv, e_send, e_recv, loc):
+    cube = Cube()
+    z = lax.axis_index("shard")
+    greet(cube.partners(shards), shards + 2)
+    width = D // shards
+    arrays = ((d_attended_own, d_attended), (d_middle_own, d_middle_columns))
+
+    def move(k, o):
+        source, target = arrays[k]
+        return remote(source.at[:, pl.ds(o * width, width)], target.at[pl.ds(aligned(z, rows), rows)],
+                      e_send.at[k, o], e_recv.at[k, z], {"shard": o})
+
+    def arrival(k, o):
+        place = arrays[k][1].at[pl.ds(o * rows, rows)]
+        return remote(place, place, e_send.at[k, o], e_recv.at[k, o], {"shard": o})
+
+    def here(k, o):
+        source, target = arrays[k]
+        return pltpu.make_async_copy(source.at[:, pl.ds(o * width, width)], target.at[pl.ds(o * rows, rows)], loc.at[k])
+
+    for k in (0, 1):
+        for o in range(shards):
+            @pl.when(z != o)
+            def _():
+                move(k, o).start()
+
+            @pl.when(z == o)
+            def _():
+                here(k, o).start()
+    share = D // shards // 8
+    reducer = Reducer(cube, share, term, core, near, last, r_send, r_recv)
+    for k in range(shards):
+        term_product(term, k, normed_two.at[:, pl.ds(k * width, width)], slopes, 256)
+        reducer.start(k)
+    for k in (0, 1):
+        for o in range(shards):
+            @pl.when(z != o)
+            def _():
+                arrival(k, o).wait_recv()
+
+            @pl.when(z == o)
+            def _():
+                here(k, o).wait()
+    steps = [functools.partial(reducer.after_core, k) for k in range(shards)]
+    steps += [functools.partial(reducer.after_near, k) for k in range(shards)]
+    steps += [functools.partial(reducer.after_last, k) for k in range(shards)]
+    attend_back_body(rows, qkv, d_attended, stats, seg_rows, seg_columns, cosine, minus, plus,
+                     d_qkv, bias_grad, d_keys, d_values, steps)
+    for step in steps:
+        step()
+    keep = [pltpu.make_async_copy(reducer.own(k), share_out.at[k], loc.at[2 + k]) for k in range(shards)]
+    for copy in keep:
+        copy.start()
+    for k in (0, 1):
+        for o in range(shards):
+            @pl.when(z != o)
+            def _():
+                move(k, o).wait_send()
+    for k in range(shards):
+        reducer.finish(k)
+    for copy in keep:
+        copy.wait()
+
+
+def heads_back_call(shards, rows, d_attended_own, d_middle_own, qkv, stats, seg_rows, seg_columns, cosine, minus, plus, normed_two, slopes):
+    group = qkv.shape[0]
+    width = D // shards
+    share = width // 8
+    columns = slopes.shape[1]
+    vm = pl.BlockSpec(memory_space=pltpu.VMEM)
+    any_ = pl.BlockSpec(memory_space=pl.ANY)
+    dma = pltpu.SemaphoreType.DMA
+    low = jnp.bfloat16
+    return pl.pallas_call(
+        functools.partial(heads_back_kernel, shards, rows),
+        out_shape=[
+            jax.ShapeDtypeStruct((group, 3 * width), low),
+            jax.ShapeDtypeStruct((8, 3 * width), jnp.float32),
+            jax.ShapeDtypeStruct((group, width), low),
+            jax.ShapeDtypeStruct((shards, share, columns), low),
+        ],
+        in_specs=[any_, any_] + [vm] * 9,
+        out_specs=[vm, vm, any_, any_],
+        scratch_shapes=[
+            pltpu.VMEM((group, width), jnp.float32), pltpu.VMEM((group, width), jnp.float32),
+            pltpu.VMEM((group, width), low),
+        ] + reducer_scratch(shards, share, columns) + [dma((2, shards)), dma((2, shards)), dma((2 + shards,))],
+        compiler_params=pltpu.CompilerParams(collective_id=7, has_side_effects=True, vmem_limit_bytes=56 * 2**20),
+        name="heads_back",
+        cost_estimate=pl.CostEstimate(flops=10**10, bytes_accessed=200 * 10**6, transcendentals=0),
+    )(d_attended_own, d_middle_own, qkv, stats, seg_rows, seg_columns, cosine, minus, plus, normed_two, slopes)
+
+
+def input_back_kernel(shards, slopes, weight, normed, attended, d_middle, gate_up_share,
+                      total, qkv_grad, out_grad, gate_up_grad,
+                      own, got, z_send, z_recv,
+                      term, core, near, last, r_send, r_recv,
+                      o_term, o_core, o_near, o_last, o_send, o_recv,
+                      t_send, t_recv, loc, g_send, g_recv):
+    cube = Cube()
+    greet(cube.partners(shards), shards + 2)
+    width = D // shards
+    share = width // 8
+    line = LineSum(shards, 3, own, got, z_send, z_recv)
+    reducer = Reducer(cube, share, term, core, near, last, r_send, r_recv)
+    o_reducer = Reducer(cube, share, o_term, o_core, o_near, o_last, o_send, o_recv)
+    sources = (lambda o: gate_up_share.at[o], o_reducer.own, reducer.own)
+    outs = (gate_up_grad, out_grad, qkv_grad)
+    owners = [Owners(cube, shards, share, p, s, out, t_send.at[i], t_recv.at[i], loc.at[i])
+              for i, (p, s, out) in enumerate(zip((2, 1, 3), sources, outs))]
+    gatherers = [Gatherer(cube, share, out, g_send.at[i], g_recv.at[i]) for i, out in enumerate(outs)]
+    for o in range(shards):
+        owners[0].start(o)
+    for k in range(shards):
+        term_product(term, k, normed.at[:, pl.ds(k * width, width)], slopes, 256)
+        reducer.start(k)
+    for t in range(shards):
+        block = line.order(t)
+        block_product(own, block, slopes, weight)
+        line.ready(block)
+        if t == 0:
+            owners[0].arrive()
+            gatherers[0].start()
+        reducer.after_core(t)
+    for k in range(shards):
+        term_product(o_term, k, attended.at[:, pl.ds(k * width, width)], d_middle, width)
+        o_reducer.start(k)
+    steps = [gatherers[0].pass_on]
+    steps += [functools.partial(reducer.after_near, k) for k in range(shards)]
+    steps += [functools.partial(o_reducer.after_core, k) for k in range(shards)]
+    steps += [gatherers[0].pass_last]
+    for k in range(shards):
+        steps += [functools.partial(reducer.after_last, k), functools.partial(owners[2].start, k)]
+    steps += [functools.partial(o_reducer.after_near, k) for k in range(shards)]
+    for k in range(shards):
+        steps += [functools.partial(o_reducer.after_last, k), functools.partial(owners[1].start, k)]
+    moves = [functools.partial(line.step_on, far, cut) for far in range(shards - 1) for cut in range(3)]
+    for i in range(max(len(steps), len(moves))):
+        if i < len(moves):
+            moves[i]()
+        if i < len(steps):
+            steps[i]()
+    line.result(total)
+    for i in (2, 1):
+        owners[i].arrive()
+        gatherers[i].start()
+    for i in (2, 1):
+        gatherers[i].pass_on()
+    for i in (2, 1):
+        gatherers[i].pass_last()
+    line.finish()
+    for k in range(shards):
+        reducer.finish(k)
+        o_reducer.finish(k)
+    for i in range(3):
+        owners[i].finish()
+        gatherers[i].finish()
+
+
+def input_back_call(shards, slopes, weight, normed, attended, d_middle, gate_up_share):
+    group = slopes.shape[0]
+    rows = group // shards
+    width = D // shards
+    share = width // 8
+    vm = pl.BlockSpec(memory_space=pltpu.VMEM)
+    any_ = pl.BlockSpec(memory_space=pl.ANY)
+    dma = pltpu.SemaphoreType.DMA
+    low = jnp.bfloat16
+    return pl.pallas_call(
+        functools.partial(input_back_kernel, shards),
+        out_shape=[
+            jax.ShapeDtypeStruct((rows, D), jnp.float32),
+            jax.ShapeDtypeStruct((width, 3 * D), low),
+            jax.ShapeDtypeStruct((width, D), low),
+            jax.ShapeDtypeStruct((width, shards * gate_up_share.shape[2]), low),
+        ],
+        in_specs=[vm] * 5 + [any_],
+        out_specs=[vm, any_, any_, any_],
+        scratch_shapes=line_scratch(shards, rows, D, 3)
+        + reducer_scratch(shards, share, 3 * width) + reducer_scratch(shards, share, width)
+        + [dma((3, shards, 3)), dma((3, shards, 3)), dma((3, 3)), dma((3, 8)), dma((3, 8))],
+        compiler_params=pltpu.CompilerParams(collective_id=8, has_side_effects=True, vmem_limit_bytes=60 * 2**20),
+        name="input_back",
+        cost_estimate=pl.CostEstimate(flops=10**10, bytes_accessed=200 * 10**6, transcendentals=0),
+    )(slopes, weight, normed, attended, d_middle, gate_up_share)
+
+
 def swap_pieces(pieces):
     shards = lax.axis_size("shard")
     here = lax.axis_index("shard")
@@ -708,7 +1296,7 @@
     own = part.shape[0] // shards
     moved = swap_pieces(part.reshape(shards, own, -1))
     moved = moved.reshape(shards, own, columns, -1).transpose(1, 2, 0, 3).reshape(own, -1)
-    return lax.all_gather(moved, "replica", axis=0, tiled=True).astype(jnp.float32)
+    return lax.all_gather(moved, "replica", axis=0, tiled=True)
 
 
 def swiglu(gate_up):
@@ -819,37 +1407,54 @@
     hidden_low = hidden.astype(low)
     d_hidden = contract_last(group_cotangent, down_weight)
     d_gate_up_low = swiglu_pull(d_hidden)[0].astype(low)
-    d_normed_two_part = contract_last(d_gate_up_low, weight_gate_up).astype(low)
-    d_normed_two = scatter_call(shards, d_normed_two_part.reshape(shards, row_count, D), 3)
+    down_part = jnp.dot(hidden_low, down_weight, preferred_element_type=f32).astype(low)
     unit_two_own = local(unit_two)
+    inverse_two_own = local(inverse_two)
+    middle_own = local(middle)
+
+    if copies == 8:
+        d_normed_two, down_grad = hidden_back_call(
+            shards, d_gate_up_low, weight_gate_up, hidden_low, group_cotangent
+        )
+    else:
+        d_normed_two_part = contract_last(d_gate_up_low, weight_gate_up).astype(low)
+        d_normed_two = scatter_call(shards, d_normed_two_part.reshape(shards, row_count, D), 3)
+        down_grad = lax.psum(contract_first(hidden_low, group_cotangent).astype(low), "replica")
     d_middle = cotangent.astype(f32) + norm_back(
-        d_normed_two, unit_two_own, local(inverse_two), gain_two
+        d_normed_two, unit_two_own, inverse_two_own, gain_two
     )
     d_gain_two = jnp.sum(d_normed_two * unit_two_own, axis=0)
     d_shift_two = jnp.sum(d_normed_two, axis=0)
     d_middle_low = d_middle.astype(low)
     d_attended_own = contract_last(d_middle_low, weight_out).astype(low)
-    d_attended, d_middle_columns = exchange_call(shards, d_attended_own, d_middle_low)
-    d_projected_low, bias_part = attend_back_call(
-        row_count, qkv, d_attended.reshape(group_rows, width), stats, seg_rows, seg_columns,
-        cosine, minus, plus,
-    )
-    d_normed_part = contract_last(d_projected_low, weight_qkv).astype(low)
-    d_normed = scatter_call(shards, d_normed_part.reshape(shards, row_count, D), 4)
+    if copies == 8:
+        d_projected_low, bias_part, d_middle_columns, gate_up_share = heads_back_call(
+            shards, row_count, d_attended_own, d_middle_low, qkv, stats, seg_rows, seg_columns,
+            cosine, minus, plus, normed_two_low, d_gate_up_low,
+        )
+        down_part, d_projected_low = lax.optimization_barrier((down_part, d_projected_low))
+    else:
+        d_attended, d_middle_columns = exchange_call(shards, d_attended_own, d_middle_low)
+        d_projected_low, bias_part = attend_back_call(
+            row_count, qkv, d_attended.reshape(group_rows, width), stats, seg_rows, seg_columns,
+            cosine, minus, plus,
+        )
+    down_own = lax.psum_scatter(down_part, "shard", scatter_dimension=0, tiled=True)
+    mixed = (middle_own + down_own.astype(f32)).astype(low)
+    if copies == 8:
+        d_normed, qkv_grad, out_grad, gate_up_grad = input_back_call(
+            shards, d_projected_low, weight_qkv, normed_low, attended, d_middle_columns, gate_up_share
+        )
+    else:
+        d_normed_part = contract_last(d_projected_low, weight_qkv).astype(low)
+        d_normed = scatter_call(shards, d_normed_part.reshape(shards, row_count, D), 4)
+        gate_up_grad = sum_columns(normed_two_low, d_gate_up_low, 2)
+        out_grad = sum_columns(attended, d_middle_columns.reshape(group_rows, width), 1)
+        qkv_grad = sum_columns(normed_low, d_projected_low, 3)
     unit_one, inverse_one = norm_stats(tokens.astype(f32))
     input_grad = d_middle + norm_back(d_normed, unit_one, inverse_one, gain_one)
     d_gain_one = jnp.sum(d_normed * unit_one, axis=0)
     d_shift_one = jnp.sum(d_normed, axis=0)
-
-    down_part = jnp.dot(hidden_low, down_weight, preferred_element_type=f32).astype(low)
-    down_own = lax.psum_scatter(down_part, "shard", scatter_dimension=0, tiled=True)
-    mixed = (local(middle) + down_own.astype(f32)).astype(low)
-    down_grad = lax.psum(
-        contract_first(hidden_low, group_cotangent).astype(low), "replica"
-    ).astype(f32)
-    gate_up_grad = sum_columns(normed_two_low, d_gate_up_low, 2)
-    out_grad = sum_columns(attended, d_middle_columns.reshape(group_rows, width), 1)
-    qkv_grad = sum_columns(normed_low, d_projected_low, 3)
 
     bias_part = bias_part[0].reshape(3, 1, width)
     bias_wide = lax.dynamic_update_slice(
@@ -866,11 +1471,11 @@
     return (
         mixed,
         input_grad,
-        qkv_grad,
+        qkv_grad.astype(f32),
         small[:bias_rows],
-        out_grad,
-        gate_up_grad,
-        down_grad,
+        out_grad.astype(f32),
+        gate_up_grad.astype(f32),
+        down_grad.astype(f32),
     ) + tuple(small[bias_rows + i * width : bias_rows + (i + 1) * width] for i in range(4))
 
 

time: 1040 us -> 893 us (0.86)
  Pallas kernels: 392 us -> 628 us
  waiting for transfers between devices: 281 us -> 49.2 us
  matrix products: 114 us -> 52.8 us
  local copies, waits for them, and re-layouts: 85.9 us -> 35.3 us
  blocking collectives: 72.2 us -> 37.6 us
    pallas_call x4 -> x3, Pallas kernels: 175 us -> 411 us  [the longest x1 200 us: input_back_call(): pl.pallas_call(functools.partial(input_back_kernel, shards), out_shape=[j...]
    all_gather x3 -> x0, waiting for transfers between devices: 94.6 us -> none  [sum_columns(): lax.all_gather(moved, 'replica', axis=0, tiled=True).astype(jnp.float32)]
    reduce_scatter x3 -> x0, waiting for transfers between devices: 72.2 us -> none  [sum_columns(): part = lax.psum_scatter(term, 'replica', scatter_dimension=0, tiled=True)]
    ppermute x15 -> x6, waiting for transfers between devices: 114 us -> 49.1 us  [swap_pieces(): piece = lax.ppermute(piece, 'shard', [(i, i ^ k) for i in range(shards)])]
    dot_general x4 -> x0, matrix products: 39.3 us -> none  [contract_first(): lax.dot_general(left, right, (((0,), (0,)), ((), ())), preferred_element_...]
    psum x1, blocking collectives: 72.2 us -> 37.6 us  [on_device(): small = lax.psum(small, ('replica', 'shard'))]
    dot_general x4 -> x2, matrix products: 44.3 us -> 21 us  [contract_last(): lax.dot_general(left, right, (((1,), (1,)), ((), ())), preferred_element_...]
    reshape x5 -> x0, local copies, waits for them, and re-layouts: 14.1 us -> none  [sum_columns(): moved.reshape(shards, own, columns, -1).transpose(1, 2, 0, 3)]
  transfers between devices with their start and end apart: 26 -> 10, of which waited for: 19 -> 6; matrix products, arithmetic and copies ran while one was open for 17% -> 10% of each run, Pallas kernels for 29% -> 47%
where the time goes in v3:
time: 893 us; the launch traced here: 882 us
  Pallas kernels  628 us (70%)
  other arithmetic  58.8 us (7%)
  matrix products  52.8 us (6%)
  waiting for transfers between devices  49.2 us (6%)
  blocking collectives  37.6 us (4%)
  local copies, waits for them, and re-layouts  35.3 us (4%)
  between operations  14.8 us (2%)
    pallas_call x1, Pallas kernels, input_back_call(): pl.pallas_call(functools.partial(input_back_kernel, shards), out_shape=[j...  200 us
    pallas_call x1, Pallas kernels, attend_call(): pl.pallas_call(functools.partial(attend_kernel, shards, rows), out_shape=...  123 us
    pallas_call x1, Pallas kernels, hidden_back_call(): pl.pallas_call(functools.partial(hidden_back_kernel, shards), out_shape=[...  115 us
    pallas_call x1, Pallas kernels, heads_back_call(): pl.pallas_call(functools.partial(heads_back_kernel, shards, rows), out_sh...  96.8 us
    pallas_call x1, Pallas kernels, start_call(): pl.pallas_call(functools.partial(start_kernel, shards), out_shape=[jax.Sh...  93.9 us
    ppermute x6, waiting for transfers between devices, swap_pieces(): piece = lax.ppermute(piece, 'shard', [(i, i ^ k) for i in range(shards)])  49.1 us
    psum x1, blocking collectives, on_device(): small = lax.psum(small, ('replica', 'shard'))  37.6 us
    dot_general x2, matrix products, contract_last(): lax.dot_general(left, right, (((1,), (1,)), ((), ())), preferred_element_...  21 us
  transfers between devices with their start and end apart: 10, of which 6 were waited for; matrix products, arithmetic and copies ran while one was open for 10% of the time, Pallas kernels for 47%

profile of v3, /device:TPU:9, one launch (start us, length us, event | category | flops | bytes accessed | tf_op | source)
XLA Modules:
  0.0 881.9 jit_solution(265986006770254443)
XLA Ops:
  11.5 7.3 collective-permute-done
  22.7 11.1 %collective-permute-done.2 = bf16[1,64,2048]{2,1,0:T(8,128)(2,1)S(1)} collective-permute-done((bf16[1,64,2048]{2,1,0:T(8,128)(2,1)S(1)}, bf16[1,64,2048]{2,1,0:T(8,128)(2,1)S(1)}, u32[]{:S(2)}, u32[]{:S(2)}) %collective-permute-start.2) | collective-permute-done | bytes 262176 | tf_op jit(solution)/shard_map/ppermute | solution.py:1256
  44.2 8.9 %collective-permute-done.3 = bf16[1,64,2816]{2,1,0:T(8,128)(2,1)} collective-permute-done((bf16[1,64,2816]{2,1,0:T(8,128)(2,1)}, bf16[1,64,2816]{2,1,0:T(8,128)(2,1)}, u32[]{:S(2)}, u32[]{:S(2)}) %collective-permute-start.3) | collective-permute-done | bytes 360480 | tf_op jit(solution)/shard_map/ppermute | solution.py:1256
  54.0 3.7 collective-permute-done.4
  58.8 14.4 %collective-permute-done.5 = bf16[1,64,2816]{2,1,0:T(8,128)(2,1)} collective-permute-done((bf16[1,64,2816]{2,1,0:T(8,128)(2,1)S(1)}, bf16[1,64,2816]{2,1,0:T(8,128)(2,1)}, u32[]{:S(2)}, u32[]{:S(2)}) %collective-permute-start.5) | collective-permute-done | bytes 360480 | tf_op jit(solution)/shard_map/ppermute | solution.py:1256
  78.2 93.9 %start.1 = (bf16[4,192,2048]{2,1,0:T(8,128)(2,1)}, f32[4,8,512]{2,1,0:T(8,128)S(1)}, bf16[768,2048]{1,0:T(8,128)(2,1)}, bf16[768,1536]{1,0:T(8,128)(2,1)S(1)}, bf16[2048,1536]{1,0:T(8,128)(2,1)}) custom-call(bf16[192,2048]{1,0:T(8,128)(2,1)S(1)} %copy-done.2, f32[8,512]{1,0:T(8,128)S(1)} %reshape.197.vectors, bf16[512,6144]{1,0:T(8,128)(2,1)} %weight.1, ...), custom_call_target="tpu_custom_call" | custom-call | flops 4831838208 | bytes 150000000 | tf_op jit(solution)/shard_map/start/pallas_call | solution.py:292
  175.6 122.9 %attend.1 = (bf16[768,2048]{1,0:T(8,128)(2,1)}, f32[768,128]{1,0:T(8,128)S(1)}) custom-call(bf16[768,1536]{1,0:T(8,128)(2,1)S(1)} %copy-done.9, s32[768,128]{1,0:T(8,128)S(1)} %broadcast_in_dim.17.seg_rows, s32[8,768]{1,0:T(8,128)S(1)} %broadcast_in_dim.18.seg_columns), custom_call_target="tpu_custom_call" | custom-call | flops 1000000000 | bytes 150000000 | tf_op jit(solution)/shard_map/attend/pallas_call | solution.py:424
  298.5 10.9 %fusion.19 = (f32[768]{0:T(1024)S(1)}, f32[768,2048]{1,0:T(8,128)S(1)}) fusion(bf16[768,2048]{1,0:T(8,128)(2,1)} %get-tuple-element.35.attended, bf16[2048,2048]{1,0:T(8,128)(2,1)} %bitcast.71, bf16[768,2048]{1,0:T(8,128)(2,1)} %bitcast.73), kind=kOutput, calls=%fused_computation.72 | convolution fusion | flops 6447168512 | bytes 20974592 | tf_op jit(solution)/shard_map/dot_general | solution.py:1402
  312.1 4.4 add_convert_fusion.1
  316.5 6.4 copy.67
  322.9 4.4 copy-done.12
  327.3 11.3 %fusion.20 = f32[768,2816]{1,0:T(8,128)} fusion(bf16[768,2048]{1,0:T(8,128)(2,1)S(1)} %copy-done.18, bf16[2048,2816]{1,0:T(8,128)(2,1)S(1)} %bitcast.51), kind=kOutput, calls=%fused_computation.73 | convolution fusion | flops 8858370048 | bytes 23330816 | tf_op jit(solution)/shard_map/dot_general | solution.py:1405
  338.6 13.6 %fusion.14 = (f32[768,1408]{1,0:T(8,128)}, f32[768,1408]{1,0:T(8,128)}, bf16[768,1408]{1,0:T(8,128)(2,1)S(1)}) fusion(f32[768,2816]{1,0:T(8,128)} %fusion.20, bf16[768,2048]{1,0:T(8,128)(2,1)} %all-gather.8.cloned.1.call-done.cotangent, bf16[1408,2048]{1,0:T(8,128)(2,1)} %param.18), kind=kOutput, calls=%fused_computation.32 | convolution fusion | flops 4444323840 | bytes 28377088 | tf_op jit(solution)/shard_map/dot_general | solution.py:40
  353.5 9.6 %convolution_convert_fusion = bf16[768,2048]{1,0:T(8,128)(2,1)} fusion(bf16[768,1408]{1,0:T(8,128)(2,1)S(1)} %get-tuple-element.69.hidden, bf16[1408,2048]{1,0:T(8,128)(2,1)} %param.18), kind=kOutput, calls=%fused_computation.11 | convolution fusion | flops 4430757888 | bytes 11075584 | tf_op jit(solution)/shard_map/dot_general | solution.py:1410
  363.1 6.0 add_convert_fusion.slopes
  369.2 114.9 %hidden_back.1 = (f32[192,2048]{1,0:T(8,128)}, bf16[1408,2048]{1,0:T(8,128)(2,1)}) custom-call(bf16[768,2816]{1,0:T(8,128)(2,1)} %add_convert_fusion.slopes, bf16[2048,2816]{1,0:T(8,128)(2,1)} %bitcast.52, bf16[768,1408]{1,0:T(8,128)(2,1)} %copy-done.27, bf16[768,2048]{1,0:T(8,128)(2,1)} %all-gather.8.cloned.1.call-done.cotangent), custom_call_target="tpu_custom_call" | custom-call | flops 10000000000 | bytes 200000000 | tf_op jit(solution)/shard_map/hidden_back/pallas_call | solution.py:1047
  489.8 7.5 convolution_convert_fusion.1.d_attended_own
  497.3 96.8 %heads_back.1 = (bf16[768,1536]{1,0:T(8,128)(2,1)}, f32[8,1536]{1,0:T(8,128)}, bf16[768,512]{1,0:T(8,128)(2,1)}, bf16[4,64,2816]{2,1,0:T(8,128)(2,1)}) custom-call(bf16[192,2048]{1,0:T(8,128)(2,1)} %convolution_convert_fusion.1.d_attended_own, bf16[192,2048]{1,0:T(8,128)(2,1)} %copy-done.20, bf16[768,1536]{1,0:T(8,128)(2,1)} %copy-done.8, ...), custom_call_target="tpu_custom_call" | custom-call | flops 10000000000 | bytes 200000000 | tf_op jit(solution)/shard_map/heads_back/pallas_call | solution.py:1135
  594.6 199.5 %input_back.1 = (f32[192,2048]{1,0:T(8,128)}, bf16[512,6144]{1,0:T(8,128)(2,1)}, bf16[512,2048]{1,0:T(8,128)(2,1)}, bf16[512,11264]{1,0:T(8,128)(2,1)}) custom-call(bf16[768,1536]{1,0:T(8,128)(2,1)} %get-tuple-element.42.slopes, bf16[2048,1536]{1,0:T(8,128)(2,1)} %get-tuple-element.43.weight, bf16[768,2048]{1,0:T(8,128)(2,1)} %get-tuple-element.44.normed, ...), custom_call_target="tpu_custom_call" | custom-call | flops 10000000000 | bytes 200000000 | tf_op jit(solution)/shard_map/input_back/pallas_call | solution.py:1230
  794.2 13.0 %convert_element_type.83 = f32[512,11264]{1,0:T(8,128)} convert(bf16[512,11264]{1,0:T(8,128)(2,1)} %get-tuple-element.51) | non-fusion elementwise | flops 5767168 | bytes 34603008 | tf_op jit(solution)/shard_map/convert_element_type | solution.py:1477
  808.9 9.4 %convert_element_type.81 = f32[512,6144]{1,0:T(8,128)} convert(bf16[512,6144]{1,0:T(8,128)(2,1)} %get-tuple-element.48) | non-fusion elementwise | flops 3145728 | bytes 18874368 | tf_op jit(solution)/shard_map/convert_element_type | solution.py:1474
  820.8 8.7 convert_element_type.84
  829.5 37.6 %psum.7 = f32[4,3584]{1,0:T(4,128)S(1)} all-reduce(f32[4,3584]{1,0:T(4,128)S(1)} %constant_dynamic-update-slice_fusion), channel_id=1, replica_groups=mesh['replica'=8,'shard'=4] {'replica','shard'}, use_global_device_ids=true, to_apply=%region_16.17 | all-reduce | flops 14336 | bytes 114688 | tf_op jit(solution)/shard_map/psum | solution.py:1468
  868.4 3.8 fusion.11
  (150 shorter events, 47.4 us)
Async XLA Ops:
  7.2 291.3 %all-gather.4.cloned.1.call-start = ((), (), s32[]{:S(2)}) async-start(), calls=%async_computation.1 | async-start | bytes 9437184 | tf_op jit(solution)/shard_map/all_gather | solution.py:1279
  8.8 10.1 %collective-permute-start = (bf16[1,64,2048]{2,1,0:T(8,128)(2,1)S(1)}, bf16[1,64,2048]{2,1,0:T(8,128)(2,1)S(1)}, u32[]{:S(2)}, u32[]{:S(2)}) collective-permute-start(bf16[1,64,2048]{2,1,0:T(8,128)(2,1)S(1)} %fusion.31), channel_id=1, source_target_pairs={{0,1},{1,0},{2,3},{3,2},{4,5},{5,4},{6,7},{7,6},{8,9},{9,8},{10,11... | collective-permute-start | bytes 786440 | tf_op jit(solution)/shard_map/ppermute | solution.py:1256
  8.9 13.8 %collective-permute-start.1 = (bf16[1,64,2048]{2,1,0:T(8,128)(2,1)S(1)}, bf16[1,64,2048]{2,1,0:T(8,128)(2,1)S(1)}, u32[]{:S(2)}, u32[]{:S(2)}) collective-permute-start(bf16[1,64,2048]{2,1,0:T(8,128)(2,1)S(1)} %fusion.31), channel_id=1, source_target_pairs={{0,2},{1,3},{2,0},{3,1},{4,6},{5,7},{6,4},{7,5},{8,10},{9,11},{10,... | collective-permute-start | bytes 786440 | tf_op jit(solution)/shard_map/ppermute | solution.py:1256
  11.3 22.5 %collective-permute-start.2 = (bf16[1,64,2048]{2,1,0:T(8,128)(2,1)S(1)}, bf16[1,64,2048]{2,1,0:T(8,128)(2,1)S(1)}, u32[]{:S(2)}, u32[]{:S(2)}) collective-permute-start(bf16[1,64,2048]{2,1,0:T(8,128)(2,1)S(1)} %fusion.31), channel_id=1, source_target_pairs={{0,3},{1,2},{2,1},{3,0},{4,7},{5,6},{6,5},{7,4},{8,11},{9,10},{10,... | collective-permute-start | bytes 786440 | tf_op jit(solution)/shard_map/ppermute | solution.py:1256
  34.9 281.6 %all-gather.6.cloned.1.call-start = ((), (), s32[]{:S(2)}) async-start(), calls=%async_computation.2 | async-start | bytes 12976128 | tf_op jit(solution)/shard_map/all_gather | solution.py:1271
  40.6 12.5 %collective-permute-start.3 = (bf16[1,64,2816]{2,1,0:T(8,128)(2,1)}, bf16[1,64,2816]{2,1,0:T(8,128)(2,1)}, u32[]{:S(2)}, u32[]{:S(2)}) collective-permute-start(bf16[1,64,2816]{2,1,0:T(8,128)(2,1)} %get-tuple-element.72), channel_id=1, source_target_pairs={{0,1},{1,0},{2,3},{3,2},{4,5},{5,4},{6,7},{7,6},{8,9},{9,8},{10,11... | collective-permute-start | bytes 1081352 | tf_op jit(solution)/shard_map/ppermute | solution.py:1256
  40.6 17.2 %collective-permute-start.4 = (bf16[1,64,2816]{2,1,0:T(8,128)(2,1)}, bf16[1,64,2816]{2,1,0:T(8,128)(2,1)}, u32[]{:S(2)}, u32[]{:S(2)}) collective-permute-start(bf16[1,64,2816]{2,1,0:T(8,128)(2,1)} %get-tuple-element.71), channel_id=1, source_target_pairs={{0,2},{1,3},{2,0},{3,1},{4,6},{5,7},{6,4},{7,5},{8,10},{9,11},{10,... | collective-permute-start | bytes 1081352 | tf_op jit(solution)/shard_map/ppermute | solution.py:1256
  43.0 32.3 %copy-start.26 = (s32[1,3]{1,0:T(1,128)S(1)}, s32[1,3]{1,0:T(1,128)}, u32[]{:S(2)}) copy-start(s32[1,3]{1,0:T(1,128)} %param.23) | copy-start | bytes 40
  43.0 30.1 %collective-permute-start.5 = (bf16[1,64,2816]{2,1,0:T(8,128)(2,1)S(1)}, bf16[1,64,2816]{2,1,0:T(8,128)(2,1)}, u32[]{:S(2)}, u32[]{:S(2)}) collective-permute-start(bf16[1,64,2816]{2,1,0:T(8,128)(2,1)S(1)} %get-tuple-element.70), channel_id=1, source_target_pairs={{0,3},{1,2},{2,1},{3,0},{4,7},{5,6},{6,5},{7,4},{8,11},{9,10},{10,... | collective-permute-start | bytes 1081352 | tf_op jit(solution)/shard_map/ppermute | solution.py:1256
  75.3 2.9 copy-start.2
  75.3 263.3 %all-gather.8.cloned.1.call-start = ((), (), s32[]{:S(2)}) async-start(), calls=%async_computation.3 | async-start | bytes 3932160 | tf_op jit(solution)/shard_map/all_gather | solution.py:1395
  76.3 95.7 %copy-start.3 = (f32[768,128]{1,0:T(8,128)}, f32[768,128]{1,0:T(8,128)S(1)}, u32[]{:S(2)}) copy-start(f32[768,128]{1,0:T(8,128)S(1)} %copy.60.cosine) | copy-start | bytes 1179652
  76.5 95.5 %copy-start.4 = (f32[768,128]{1,0:T(8,128)}, f32[768,128]{1,0:T(8,128)S(1)}, u32[]{:S(2)}) copy-start(f32[768,128]{1,0:T(8,128)S(1)} %copy.61.minus) | copy-start | bytes 1179652
  76.8 95.3 %copy-start.5 = (f32[768,128]{1,0:T(8,128)}, f32[768,128]{1,0:T(8,128)S(1)}, u32[]{:S(2)}) copy-start(f32[768,128]{1,0:T(8,128)S(1)} %copy.62.plus) | copy-start | bytes 1179652
  173.5 698.7 %reduce-scatter.2.cloned.1.call-start = ((), (), s32[]{:S(2)}) async-start(), calls=%async_computation.4 | async-start | bytes 3932160 | tf_op jit(solution)/shard_map/reduce_scatter | solution.py:1442
  173.7 135.7 %copy-start.6 = (s32[768,128]{1,0:T(8,128)}, s32[768,128]{1,0:T(8,128)S(1)}, u32[]{:S(2)}) copy-start(s32[768,128]{1,0:T(8,128)S(1)} %broadcast_in_dim.17.seg_rows) | copy-start | bytes 1179652
  175.6 133.8 %copy-start.7 = (s32[8,768]{1,0:T(8,128)}, s32[8,768]{1,0:T(8,128)S(1)}, u32[]{:S(2)}) copy-start(s32[8,768]{1,0:T(8,128)S(1)} %broadcast_in_dim.18.seg_columns) | copy-start | bytes 73732
  298.5 10.9 %copy-start.10 = (f32[768,128]{1,0:T(8,128)}, f32[768,128]{1,0:T(8,128)S(1)}, u32[]{:S(2)}) copy-start(f32[768,128]{1,0:T(8,128)S(1)} %get-tuple-element.39.stats) | copy-start | bytes 1179652
  316.5 10.8 %copy-start.18 = (bf16[768,2048]{1,0:T(8,128)(2,1)S(1)}, bf16[768,2048]{1,0:T(8,128)(2,1)}, u32[]{:S(2)}) copy-start(bf16[768,2048]{1,0:T(8,128)(2,1)} %get-tuple-element.65.normed_two) | copy-start | bytes 9437188
  322.9 4.4 copy-start.12
  489.8 7.5 copy-start.20
  794.2 13.0 %copy-start.13 = (f32[192,2048]{1,0:T(8,128)S(1)}, f32[192,2048]{1,0:T(8,128)}, u32[]{:S(2)}) copy-start(f32[192,2048]{1,0:T(8,128)} %get-tuple-element.47) | copy-start | bytes 4718596
  808.9 9.4 %copy-start.19 = (bf16[512,2048]{1,0:T(8,128)(2,1)S(1)}, bf16[512,2048]{1,0:T(8,128)(2,1)}, u32[]{:S(2)}) copy-start(bf16[512,2048]{1,0:T(8,128)(2,1)} %get-tuple-element.50) | copy-start | bytes 6291460
  868.4 6.5 copy-start.1
  (14 other events, 26.5 us)
Sparse Core Ops, SparseCore 0:
  35.0 59.8 all-gather.3
  97.4 82.9 all-gather.5
  181.9 96.4 all-gather.7
  594.2 101.7 reduce-scatter.1

commit v4 on v3

--- a/solution.py
+++ b/solution.py
@@ -67,220 +67,328 @@
     )
 
 
-def start_kernel(shards, tokens, vectors, weight, cosine, minus, plus,
-                 all_tokens, all_vectors, normed, qkv, kept_weight,
-                 x_buf, v_buf, w_buf, n_buf, out_buf,
-                 x_send, x_recv, v_send, v_recv, w_send, w_recv, xy_send, xy_recv, c_send, c_recv, loc):
+class Cube:
+    def __init__(self):
+        r = lax.axis_index("replica")
+        self.core, self.x, self.y = r % 2, (r // 2) % 2, r // 4
+        self.place = 2 * self.y + self.x
+        self.to_x = {"replica": r + 2 - 4 * self.x}
+        self.to_y = {"replica": r + 4 - 8 * self.y}
+        self.to_core = {"replica": r + 1 - 2 * self.core}
+
+    def partners(self, shards):
+        z = lax.axis_index("shard")
+        return [((z != o), {"shard": o}) for o in range(shards)] + [
+            (z >= 0, d) for d in (self.to_x, self.to_y, self.to_core)
+        ]
+
+
+def rows_of(ref, start, unit, count):
+    return ref.at[pl.ds(pl.multiple_of(start, unit), count)]
+
+
+class Spreader:
+    def __init__(self, cube, shards, share, parts, source, out, sems):
+        self.cube, self.shards, self.share, self.parts = cube, shards, share, parts
+        self.source, self.out = source, out
+        self.z_send, self.z_recv, self.send, self.recv, self.loc = sems
+        self.cut = 16 * ((share // 16 + 1) // 2)
+        self.z = lax.axis_index("shard")
+        r = lax.axis_index("replica")
+        self.who = (r, r + 2 - 4 * cube.x, r + 4 - 8 * cube.y, 4 * (1 - cube.y) + 2 * (1 - cube.x) + cube.core)
+
+    def rows(self, o, kind, half=None):
+        first, count = {None: (0, self.share), 0: (0, self.cut), 1: (self.cut, self.share - self.cut)}[half]
+        return rows_of(self.out, (o * 8 + self.who[kind]) * self.share + first, 16, count)
+
+    def target(self, o, part):
+        width = self.out.shape[1] // self.parts
+        return self.rows(o, 0).at[:, pl.ds(part * width, width)]
+
+    def z_copy(self, o, part):
+        return remote(self.source(o, part), self.target(self.z, part), self.z_send.at[o, part], self.z_recv.at[self.z, part], {"shard": o})
+
+    def z_arrival(self, o, part):
+        place = self.target(o, part)
+        return remote(place, place, self.z_send.at[o, part], self.z_recv.at[o, part], {"shard": o})
+
+    def local(self, o, part):
+        return pltpu.make_async_copy(self.source(o, part), self.target(o, part), self.loc.at[part])
+
+    def start_own(self):
+        for part in range(self.parts):
+            self.local(self.z, part).start()
+
+    def start(self):
+        for o in range(self.shards):
+            for part in range(self.parts):
+                @pl.when(self.z != o)
+                def _():
+                    self.z_copy(o, part).start()
+
+    def sent(self):
+        for o in range(self.shards):
+            for part in range(self.parts):
+                @pl.when(self.z != o)
+                def _():
+                    self.z_copy(o, part).wait_send()
+
+    def copy(self, kind, o):
+        c = self.cube
+        block, device = (
+            (self.rows(o, 0), c.to_x),
+            (self.rows(o, 0), c.to_y),
+            (self.rows(o, 1, 0), c.to_y),
+            (self.rows(o, 2, 1), c.to_x),
+            (self.rows(o, 0), c.to_core),
+            (self.rows(o, 1), c.to_core),
+            (self.rows(o, 2), c.to_core),
+            (self.rows(o, 3), c.to_core),
+        )[kind]
+        return remote(block, block, self.send.at[kind, o], self.recv.at[kind, o], device)
+
+    def arrive(self, distance):
+        for o in range(self.shards):
+            @pl.when((self.z - o == distance) | (o - self.z == distance))
+            def _():
+                for part in range(self.parts):
+                    if distance == 0:
+                        self.local(o, part).wait()
+                    else:
+                        self.z_arrival(o, part).wait_recv()
+                for kind in (0, 1, 4):
+                    self.copy(kind, o).start()
+
+    def pass_on(self, o):
+        self.copy(0, o).wait_recv()
+        self.copy(2, o).start()
+        self.copy(5, o).start()
+        self.copy(1, o).wait_recv()
+        self.copy(3, o).start()
+        self.copy(6, o).start()
+
+    def pass_last(self, o):
+        self.copy(2, o).wait_recv()
+        self.copy(3, o).wait_recv()
+        self.copy(7, o).start()
+
+    def landed(self):
+        for o in range(self.shards):
+            for kind in (4, 5, 6, 7):
+                self.copy(kind, o).wait_recv()
+
+    def finish(self):
+        for o in range(self.shards):
+            for kind in range(8):
+                self.copy(kind, o).wait_send()
+
+
+def spread_sems(shards, parts):
+    dma = pltpu.SemaphoreType.DMA
+    return [dma((shards, parts)), dma((shards, parts)), dma((8, shards)), dma((8, shards)), dma((parts,))]
+
+
+class Line:
+    def __init__(self, shards, pieces, own, buf, send, recv):
+        self.z = lax.axis_index("shard")
+        self.shards, self.pieces, self.own, self.buf, self.send, self.recv = shards, pieces, own, buf, send, recv
+        self.rows = buf.shape[1] // pieces
+
+    def copy(self, way, step, piece):
+        target = self.z + 1 if way == 0 else self.z - 1
+        owner = self.z - step if way == 0 else self.z + step
+        block = pl.ds(piece * self.rows, self.rows)
+        place = self.buf.at[owner, block]
+        source = self.own.at[block] if step == 0 and self.own is not None else place
+        return remote(source, place, self.send.at[way, step, piece], self.recv.at[way, step, piece], {"shard": target})
+
+    def sends(self, way, step):
+        if way == 0:
+            return (self.z + 1 < self.shards) & (self.z - step >= 0)
+        return (self.z >= 1) & (self.z + step < self.shards)
+
+    def gets(self, way, step):
+        return (self.z - step >= 1) if way == 0 else (self.z + step + 1 < self.shards)
+
+    def start(self, piece):
+        for way in (0, 1):
+            @pl.when(self.sends(way, 0))
+            def _():
+                self.copy(way, 0, piece).start()
+
+    def relay(self, step, piece):
+        for way in (0, 1):
+            @pl.when(self.gets(way, step))
+            def _():
+                self.copy(way, step, piece).wait_recv()
+            if step + 1 < self.shards - 1:
+                @pl.when(self.sends(way, step + 1))
+                def _():
+                    self.copy(way, step + 1, piece).start()
+
+    def finish(self):
+        for step in range(self.shards - 1):
+            for piece in range(self.pieces):
+                for way in (0, 1):
+                    @pl.when(self.sends(way, step))
+                    def _():
+                        self.copy(way, step, piece).wait_send()
+
+
+def line_sems(shards, pieces):
+    dma = pltpu.SemaphoreType.DMA
+    return [dma((2, shards - 1, pieces)), dma((2, shards - 1, pieces))]
+
+
+def layer_norm_rows(values, gain, shift):
+    centered = values - jnp.mean(values, axis=-1, keepdims=True)
+    spread = jnp.mean(centered * centered, axis=-1, keepdims=True)
+    return (centered * lax.rsqrt(spread + norm_eps) * gain + shift).astype(jnp.bfloat16)
+
+
+def bias_piece(v_buf, z, t, tile, shards, per_part):
+    flat = (t // per_part) * shards + z
+    return v_buf[flat // 3, pl.ds(flat % 3, 1), pl.ds(aligned(t % per_part, tile), tile)]
+
+
+def start_kernel(shards, tokens, vectors, weight, out_weight, cosine, minus, plus,
+                 all_tokens, all_vectors, normed, qkv, kept_weight, all_out,
+                 x_buf, v_buf, w_buf, n_buf, q_buf, *sems):
+    cube = Cube()
     z = lax.axis_index("shard")
     r = lax.axis_index("replica")
     rows = tokens.shape[0]
-    depth = weight.shape[0]
-    share = depth // 8
-    half = share // 2
+    share = weight.shape[0] // 8
     width = w_buf.shape[1] // 3
-    core, x, y = r % 2, (r // 2) % 2, r // 4
-    xr, yr, cr = r + 2 - 4 * x, r + 4 - 8 * y, r + 1 - 2 * core
-    dr = 4 * (1 - y) + 2 * (1 - x) + core
-    true = z >= 0
-    greet(
-        [((z != o), {"shard": o}) for o in range(shards)]
-        + [(true, {"replica": d}) for d in (xr, yr, cr)],
-        shards + 2,
-    )
-
-    def w_rows(owner, replica):
-        return pl.ds(aligned(owner * 8 + replica, share), share)
-
-    def vec_copy(o):
+    x_send, x_recv, v_send, v_recv, loc = sems[:5]
+    line = Line(shards, 1, tokens, x_buf, x_send, x_recv)
+    mine = pl.ds(aligned(r, share), share)
+    spread = Spreader(
+        cube, shards, share, 3,
+        lambda o, part: weight.at[mine, pl.ds(aligned(part * shards + o, width), width)], w_buf, sems[5:10],
+    )
+    spread_out = Spreader(cube, shards, share, 1, lambda o, part: out_weight.at[mine], all_out, sems[10:15])
+    greet(cube.partners(shards), shards + 2)
+
+    def v_copy(o):
         return remote(vectors, v_buf.at[z], v_send.at[o], v_recv.at[z], {"shard": o})
-
-    def w_copy(o, part):
-        return remote(
-            weight.at[pl.ds(aligned(r, share), share), pl.ds(aligned(part * shards + o, width), width)],
-            w_buf.at[w_rows(z, r), pl.ds(part * width, width)],
-            w_send.at[o, part], w_recv.at[z, part], {"shard": o},
-        )
-
-    def w_arrival(o, part):
-        block = w_buf.at[w_rows(o, r), pl.ds(part * width, width)]
-        return remote(block, block, w_send.at[o, part], w_recv.at[o, part], {"shard": o})
 
     def v_arrival(o):
         return remote(vectors, v_buf.at[o], v_send.at[o], v_recv.at[o], {"shard": o})
 
-    def x_copy(way, step):
-        target = z + 1 if way == 0 else z - 1
-        chunk = z - step if way == 0 else z + step
-        source = tokens if step == 0 else x_buf.at[chunk]
-        return remote(source, x_buf.at[chunk], x_send.at[way, step], x_recv.at[way, step], {"shard": target})
-
-    def x_sends(way, step):
-        if way == 0:
-            return (z + 1 < shards) & (z - step >= 0)
-        return (z >= 1) & (z + step < shards)
-
-    def x_gets(way, step):
-        return (z - step >= 1) if way == 0 else (z + step + 1 < shards)
-
+    own_x = pltpu.make_async_copy(tokens, x_buf.at[z], loc.at[0, 0])
+    own_v = pltpu.make_async_copy(vectors, v_buf.at[z], loc.at[1, 0])
+    own_x.start()
+    own_v.start()
     for o in range(shards):
         @pl.when(z != o)
         def _():
-            vec_copy(o).start()
-            for part in range(3):
-                w_copy(o, part).start()
-    for way in (0, 1):
-        @pl.when(x_sends(way, 0))
-        def _():
-            x_copy(way, 0).start()
-    own_x = pltpu.make_async_copy(tokens, x_buf.at[z], loc.at[0])
-    own_x.start()
-    own_v = pltpu.make_async_copy(vectors, v_buf.at[z], loc.at[1])
-    own_v.start()
-    own_w = [
-        pltpu.make_async_copy(
-            weight.at[pl.ds(aligned(r, share), share), pl.ds(aligned(part * shards + z, width), width)],
-            w_buf.at[w_rows(z, r), pl.ds(part * width, width)], loc.at[2 + part],
-        )
-        for part in range(3)
-    ]
-    for copy in own_w:
-        copy.start()
-
-    def to_x(o):
-        block = w_buf.at[w_rows(o, r)]
-        return remote(block, block, xy_send.at[0, o], xy_recv.at[0, o], {"replica": xr})
-
-    def to_y(o):
-        block = w_buf.at[w_rows(o, r)]
-        return remote(block, block, xy_send.at[1, o], xy_recv.at[1, o], {"replica": yr})
-
-    def on_to_y(o):
-        block = w_buf.at[pl.ds(aligned((o * 8 + xr) * 2, half), half)]
-        return remote(block, block, xy_send.at[2, o], xy_recv.at[2, o], {"replica": yr})
-
-    def on_to_x(o):
-        block = w_buf.at[pl.ds(aligned((o * 8 + yr) * 2 + 1, half), half)]
-        return remote(block, block, xy_send.at[3, o], xy_recv.at[3, o], {"replica": xr})
-
-    def to_core(o, kind):
-        whose = (r, xr, yr, dr)[kind]
-        block = w_buf.at[w_rows(o, whose)]
-        return remote(block, block, c_send.at[kind, o], c_recv.at[kind, o], {"replica": cr})
-
-    for copy in own_w:
-        copy.wait()
-    for step in range(shards):
-        for o in range(shards):
-            @pl.when((z - o == step) | (o - z == step))
-            def _():
-                if step > 0:
-                    for part in range(3):
-                        w_arrival(o, part).wait_recv()
-                to_x(o).start()
-                to_y(o).start()
-                to_core(o, 0).start()
-        if step + 1 < shards:
-            for way in (0, 1):
-                @pl.when(x_gets(way, step))
-                def _():
-                    x_copy(way, step).wait_recv()
-                @pl.when(x_sends(way, step + 1))
-                def _():
-                    x_copy(way, step + 1).start()
-    for o in range(shards):
-        to_x(o).wait_recv()
-        on_to_y(o).start()
-        to_core(o, 1).start()
-        to_y(o).wait_recv()
-        on_to_x(o).start()
-        to_core(o, 2).start()
+            v_copy(o).start()
+    spread.start_own()
+    spread_out.start_own()
+    spread.start()
+    spread.arrive(0)
+    spread_out.arrive(0)
+    line.start(0)
+    spread_out.start()
+    for distance in range(1, shards):
+        spread.arrive(distance)
     own_x.wait()
     own_v.wait()
     for o in range(shards):
         @pl.when(z != o)
         def _():
             v_arrival(o).wait_recv()
-
-    keep_x = pltpu.make_async_copy(x_buf, all_tokens, loc.at[5])
-    keep_x.start()
-    keep_v = pltpu.make_async_copy(v_buf, all_vectors, loc.at[6])
+    keep_v = pltpu.make_async_copy(v_buf, all_vectors, loc.at[2, 0])
     keep_v.start()
     gain = jnp.concatenate([v_buf[o, 3:4, :] for o in range(shards)], axis=1)
     shift = jnp.concatenate([v_buf[o, 4:5, :] for o in range(shards)], axis=1)
-    for o in range(shards):
-        @pl.loop(0, rows, step=32)
-        def _(at):
-            block = pl.ds(pl.multiple_of(at, 32), 32)
-            values = x_buf[o, block, :].astype(jnp.float32)
-            centered = values - jnp.mean(values, axis=-1, keepdims=True)
-            spread = jnp.mean(centered * centered, axis=-1, keepdims=True)
-            out = centered * lax.rsqrt(spread + norm_eps) * gain + shift
-            n_buf[pl.ds(pl.multiple_of(o * rows + at, 32), 32), :] = out.astype(jnp.bfloat16)
-    keep_n = pltpu.make_async_copy(n_buf, normed, loc.at[7])
-    keep_n.start()
-
-    for o in range(shards):
-        on_to_y(o).wait_recv()
-        on_to_x(o).wait_recv()
-        to_core(o, 3).start()
-    for o in range(shards):
-        for kind in range(4):
-            to_core(o, kind).wait_recv()
-    keep_w = pltpu.make_async_copy(w_buf, kept_weight, loc.at[8])
-    keep_w.start()
+
+    def put(source, target, o, i):
+        block = pl.ds(aligned(o, rows), rows)
+        copy = pltpu.make_async_copy(source.at[block], target.at[block], loc.at[4 + i, o])
+        copy.start()
+
+    def normalize(o):
+        @pl.loop(0, rows // 32)
+        def _(i):
+            values = x_buf[o, pl.ds(aligned(i, 32), 32), :].astype(jnp.float32)
+            n_buf[pl.ds(pl.multiple_of(o * rows + i * 32, 32), 32), :] = layer_norm_rows(values, gain, shift)
+        put(n_buf, normed, o, 0)
+        pltpu.make_async_copy(x_buf.at[o], all_tokens.at[o], loc.at[6, o]).start()
 
     tile = 256
     per_part = width // tile
 
-    @pl.loop(0, 3 * per_part)
-    def _(t):
-        columns = pl.ds(aligned(t, tile), tile)
-        bias_row = bias_piece(v_buf, z, t, tile, shards, per_part)
-        value = jnp.dot(n_buf[...], w_buf[:, columns], preferred_element_type=jnp.float32) + bias_row
-
-        @pl.when(t < 2 * per_part)
-        def _():
-            wide = jnp.concatenate([cosine[...]] * (tile // 128), axis=1)
-            wide_minus = jnp.concatenate([minus[...]] * (tile // 128), axis=1)
-            wide_plus = jnp.concatenate([plus[...]] * (tile // 128), axis=1)
-            turned = value * wide + pltpu.roll(value, tile - 8, 1) * wide_minus + pltpu.roll(value, 8, 1) * wide_plus
-            out_buf[:, columns] = turned.astype(jnp.bfloat16)
-
-        @pl.when(t >= 2 * per_part)
-        def _():
-            out_buf[:, columns] = value.astype(jnp.bfloat16)
-    keep_q = pltpu.make_async_copy(out_buf, qkv, loc.at[9])
-    keep_q.start()
-
+    def project(o):
+        block = pl.ds(aligned(o, rows), rows)
+
+        @pl.loop(0, 3 * per_part)
+        def _(t):
+            columns = pl.ds(aligned(t, tile), tile)
+            value = jnp.dot(n_buf[block, :], w_buf[:, columns], preferred_element_type=jnp.float32)
+            value = value + bias_piece(v_buf, z, t, tile, shards, per_part)
+
+            @pl.when(t < 2 * per_part)
+            def _():
+                wide, wide_minus, wide_plus = (
+                    jnp.concatenate([table[block, :]] * (tile // 128), axis=1) for table in (cosine, minus, plus)
+                )
+                turned = value * wide + pltpu.roll(value, tile - 8, 1) * wide_minus + pltpu.roll(value, 8, 1) * wide_plus
+                q_buf[block, columns] = turned.astype(jnp.bfloat16)
+
+            @pl.when(t >= 2 * per_part)
+            def _():
+                q_buf[block, columns] = value.astype(jnp.bfloat16)
+        put(q_buf, qkv, o, 1)
+
+    normalize(z)
+    line.relay(0, 0)
     for o in range(shards):
+        spread.pass_on(o)
+    for o in range(shards):
+        spread.pass_last(o)
+    spread.landed()
+    keep_w = pltpu.make_async_copy(w_buf, kept_weight, loc.at[3, 0])
+    keep_w.start()
+    project(z)
+    for distance in range(1, shards):
+        spread_out.arrive(distance)
+    for step in range(shards - 1):
+        if step > 0:
+            line.relay(step, 0)
+        for way in (0, 1):
+            owner = z - step - 1 if way == 0 else z + step + 1
+
+            @pl.when(line.gets(way, step))
+            def _():
+                normalize(owner)
+                project(owner)
+        if step == min(1, shards - 2):
+            for o in range(shards):
+                spread_out.pass_on(o)
+    for o in range(shards):
+        spread_out.pass_last(o)
+    spread_out.landed()
+    line.finish()
+    spread.sent()
+    spread.finish()
+    spread_out.sent()
+    spread_out.finish()
+    for o in range(shards):
+        block = pl.ds(o * rows, rows)
+
         @pl.when(z != o)
         def _():
-            vec_copy(o).wait_send()
-            for part in range(3):
-                w_copy(o, part).wait_send()
-        to_x(o).wait_send()
-        to_y(o).wait_send()
-        on_to_y(o).wait_send()
-        on_to_x(o).wait_send()
-        for kind in range(4):
-            to_core(o, kind).wait_send()
-    for step in range(shards - 1):
-        for way in (0, 1):
-            @pl.when(x_sends(way, step))
-            def _():
-                x_copy(way, step).wait_send()
-    for copy in (keep_x, keep_v, keep_n, keep_w, keep_q):
-        copy.wait()
-
-
-def bias_piece(v_buf, z, t, tile, shards, per_part):
-    part = t // per_part
-    at = t % per_part
-    flat = part * shards + z
-    return v_buf[flat // 3, pl.ds(flat % 3, 1), pl.ds(aligned(at, tile), tile)]
-
-
-def start_call(shards, tokens, vectors, weight, cosine, minus, plus):
+            v_copy(o).wait_send()
+        pltpu.make_async_copy(n_buf.at[block], normed.at[block], loc.at[4, o]).wait()
+        pltpu.make_async_copy(q_buf.at[block], qkv.at[block], loc.at[5, o]).wait()
+        pltpu.make_async_copy(x_buf.at[o], all_tokens.at[o], loc.at[6, o]).wait()
+    keep_v.wait()
+    keep_w.wait()
+
+
+def start_call(shards, tokens, vectors, weight, out_weight, cosine, minus, plus):
     rows = tokens.shape[0]
     group = rows * shards
     depth = weight.shape[0]
@@ -297,28 +405,236 @@
             jax.ShapeDtypeStruct((group, D), low),
             jax.ShapeDtypeStruct((group, width), low),
             jax.ShapeDtypeStruct((depth * shards, width), low),
+            jax.ShapeDtypeStruct((depth * shards, D), low),
         ],
-        in_specs=[any_, any_, any_, vm, vm, vm],
-        out_specs=[any_] * 5,
+        in_specs=[any_] * 4 + [vm] * 3,
+        out_specs=[any_] * 6,
         scratch_shapes=[
             pltpu.VMEM((shards, rows, D), low),
             pltpu.VMEM((shards,) + vectors.shape, vectors.dtype),
             pltpu.VMEM((depth * shards, width), low),
             pltpu.VMEM((group, D), low),
             pltpu.VMEM((group, width), low),
-            dma((2, shards)), dma((2, shards)),
-            dma((shards,)), dma((shards,)),
-            dma((shards, 3)), dma((shards, 3)),
-            dma((4, shards)), dma((4, shards)),
-            dma((4, shards)), dma((4, shards)),
-            dma((10,)),
-        ],
+        ] + line_sems(shards, 1) + [dma((shards,)), dma((shards,)), dma((7, shards))]
+        + spread_sems(shards, 3) + spread_sems(shards, 1),
         compiler_params=pltpu.CompilerParams(
             collective_id=1, has_side_effects=True, vmem_limit_bytes=48 * 2**20
         ),
         name="start",
         cost_estimate=pl.CostEstimate(flops=2 * group * D * width, bytes_accessed=150 * 10**6, transcendentals=0),
-    )(tokens, vectors, weight, cosine, minus, plus)
+    )(tokens, vectors, weight, out_weight, cosine, minus, plus)
+
+
+def attend_spread_kernel(shards, rows, qkv, seg_rows, seg_columns, gate_up, attended, stats, all_gate_up, a_buf, *sems):
+    cube = Cube()
+    z = lax.axis_index("shard")
+    r = lax.axis_index("replica")
+    width = qkv.shape[1] // 3
+    blocks = qkv.shape[0] // rows
+    share = gate_up.shape[0] // 8
+    half = all_gate_up.shape[1] // 2
+    mine = pl.ds(aligned(r, share), share)
+    spread = Spreader(
+        cube, shards, share, 2,
+        lambda o, part: gate_up.at[mine, pl.ds(aligned((part * shards + o) * (half // 128), 128), half)], all_gate_up, sems[3:8],
+    )
+    line = Line(shards, blocks, None, a_buf, sems[0], sems[1])
+    loc = sems[2]
+    greet(cube.partners(shards), shards + 2)
+    spread.start_own()
+    spread.start()
+    spread.arrive(0)
+
+    def done(block):
+        line.start(block)
+        if 0 < block < shards:
+            spread.arrive(block)
+
+    attend_body(rows, qkv, seg_rows, seg_columns, a_buf, stats, done)
+    moves = [functools.partial(line.relay, step, block) for step in range(shards - 1) for block in range(blocks)]
+    steps = [functools.partial(spread.pass_on, o) for o in range(shards)]
+    steps += [functools.partial(spread.pass_last, o) for o in range(shards)]
+    for i in range(max(len(moves), len(steps))):
+        if i < len(moves):
+            moves[i]()
+        if i < len(steps):
+            steps[i]()
+    keep = [pltpu.make_async_copy(a_buf.at[o], attended.at[:, pl.ds(o * width, width)], loc.at[o]) for o in range(shards)]
+    for copy in keep:
+        copy.start()
+    spread.landed()
+    line.finish()
+    spread.sent()
+    spread.finish()
+    for copy in keep:
+        copy.wait()
+
+
+def attend_spread_call(shards, rows, qkv, seg_rows, seg_columns, gate_up):
+    group = qkv.shape[0]
+    width = qkv.shape[1] // 3
+    blocks = group // rows
+    vm = pl.BlockSpec(memory_space=pltpu.VMEM)
+    any_ = pl.BlockSpec(memory_space=pl.ANY)
+    dma = pltpu.SemaphoreType.DMA
+    low = jnp.bfloat16
+    return pl.pallas_call(
+        functools.partial(attend_spread_kernel, shards, rows),
+        out_shape=[
+            jax.ShapeDtypeStruct((group, shards * width), low),
+            jax.ShapeDtypeStruct((group, 128), jnp.float32),
+            jax.ShapeDtypeStruct((gate_up.shape[0] * shards, gate_up.shape[1] // shards), low),
+        ],
+        in_specs=[vm, vm, vm, any_],
+        out_specs=[any_, vm, any_],
+        scratch_shapes=[pltpu.VMEM((shards, group, width), low)] + line_sems(shards, blocks) + [dma((shards,))]
+        + spread_sems(shards, 2),
+        compiler_params=pltpu.CompilerParams(
+            collective_id=2, has_side_effects=True, vmem_limit_bytes=48 * 2**20
+        ),
+        name="attend_spread",
+        cost_estimate=pl.CostEstimate(flops=10**9, bytes_accessed=150 * 10**6, transcendentals=0),
+    )(qkv, seg_rows, seg_columns, gate_up)
+
+
+def hidden_kernel(shards, attended, tokens, out_weight, gate_up_weight, down_weight, cotangent, gain, shift,
+                  middle_own, normed_two, hidden, slopes, all_cotangent, down_part,
+                  a_buf, x_buf, o_buf, g_buf, d_buf, c_buf, mid, n_buf, gu, h_buf, s_buf, c_send, c_recv, loc):
+    z = lax.axis_index("shard")
+    greet_line(z, shards)
+    rows = cotangent.shape[0]
+    group = rows * shards
+    inner = h_buf.shape[1]
+    line = Line(shards, 1, cotangent, c_buf, c_send, c_recv)
+    line.start(0)
+    load = [pltpu.make_async_copy(source, target, loc.at[i]) for i, (source, target) in enumerate((
+        (attended, a_buf), (out_weight, o_buf), (tokens, x_buf), (gate_up_weight, g_buf), (down_weight, d_buf),
+        (cotangent, c_buf.at[z])))]
+    for copy in load:
+        copy.start()
+    for copy in load[:3]:
+        copy.wait()
+    tile = 256
+    span = 2 * rows
+    for part in range(group // span):
+        at = part * span
+
+        @pl.loop(0, D // tile)
+        def _(t):
+            columns = pl.ds(aligned(t, tile), tile)
+            value = jnp.dot(a_buf[at : at + span, :], o_buf[:, columns], preferred_element_type=jnp.float32)
+            for k in range(2):
+                mid[k * rows : (k + 1) * rows, columns] = (
+                    value[k * rows : (k + 1) * rows] + x_buf[2 * part + k, :, columns].astype(jnp.float32)
+                )
+
+        @pl.loop(0, span // 32)
+        def _(i):
+            block = pl.ds(aligned(i, 32), 32)
+            n_buf[pl.ds(pl.multiple_of(at + i * 32, 32), 32), :] = layer_norm_rows(mid[block, :], gain[...], shift[...])
+        for k in range(2):
+            @pl.when(z == 2 * part + k)
+            def _():
+                middle_own[...] = mid[k * rows : (k + 1) * rows, :]
+    keep_n = pltpu.make_async_copy(n_buf, normed_two, loc.at[6])
+    keep_n.start()
+    line.relay(0, 0)
+    load[3].wait()
+
+    @pl.loop(0, 2 * inner // tile)
+    def _(t):
+        columns = pl.ds(aligned(t, tile), tile)
+        gu[:, columns] = jnp.dot(n_buf[...], g_buf[:, columns], preferred_element_type=jnp.float32)
+
+    @pl.loop(0, group // 32)
+    def _(i):
+        block = pl.ds(aligned(i, 32), 32)
+        gate = gu[block, :inner]
+        h_buf[block, :] = (gate / (1.0 + jnp.exp(-gate)) * gu[block, inner:]).astype(jnp.bfloat16)
+    keep_h = pltpu.make_async_copy(h_buf, hidden, loc.at[7])
+    keep_h.start()
+    if shards > 2:
+        line.relay(1, 0)
+    load[4].wait()
+
+    @pl.loop(0, D // tile)
+    def _(t):
+        columns = pl.ds(aligned(t, tile), tile)
+        a_buf[:, columns] = jnp.dot(h_buf[...], d_buf[:, columns], preferred_element_type=jnp.float32).astype(jnp.bfloat16)
+    keep_p = pltpu.make_async_copy(a_buf, down_part, loc.at[8])
+    keep_p.start()
+    load[5].wait()
+
+    def back(o):
+        mid[:rows, :inner] = contract_last(c_buf[o], d_buf[...])
+
+        @pl.loop(0, rows // 32)
+        def _(i):
+            value = mid[pl.ds(aligned(i, 32), 32), :inner]
+            place = pl.ds(pl.multiple_of(o * rows + i * 32, 32), 32)
+            gate = gu[place, :inner]
+            up = gu[place, inner:]
+            sigmoid = 1.0 / (1.0 + jnp.exp(-gate))
+            s_buf[place, :inner] = (value * up * (sigmoid * (1.0 + gate * (1.0 - sigmoid)))).astype(jnp.bfloat16)
+            s_buf[place, inner:] = (value * (gate * sigmoid)).astype(jnp.bfloat16)
+
+    back(z)
+    for step in range(shards - 1):
+        if step >= 2:
+            line.relay(step, 0)
+        for way in (0, 1):
+            owner = z - step - 1 if way == 0 else z + step + 1
+
+            @pl.when(line.gets(way, step))
+            def _():
+                back(owner)
+    keep = [pltpu.make_async_copy(c_buf, all_cotangent, loc.at[9]), pltpu.make_async_copy(s_buf, slopes, loc.at[10])]
+    for copy in keep:
+        copy.start()
+    line.finish()
+    for copy in keep + [keep_n, keep_h, keep_p]:
+        copy.wait()
+
+
+def hidden_call(shards, attended, tokens, out_weight, gate_up_weight, down_weight, cotangent, gain, shift):
+    rows = cotangent.shape[0]
+    group = rows * shards
+    inner = down_weight.shape[0]
+    low = jnp.bfloat16
+    f32 = jnp.float32
+    vm = pl.BlockSpec(memory_space=pltpu.VMEM)
+    any_ = pl.BlockSpec(memory_space=pl.ANY)
+    return pl.pallas_call(
+        functools.partial(hidden_kernel, shards),
+        out_shape=[
+            jax.ShapeDtypeStruct((rows, D), f32),
+            jax.ShapeDtypeStruct((group, D), low),
+            jax.ShapeDtypeStruct((group, inner), low),
+            jax.ShapeDtypeStruct((group, 2 * inner), low),
+            jax.ShapeDtypeStruct((shards, rows, D), low),
+            jax.ShapeDtypeStruct((group, D), low),
+        ],
+        in_specs=[any_] * 6 + [vm, vm],
+        out_specs=[vm] + [any_] * 5,
+        scratch_shapes=[
+            pltpu.VMEM((group, D), low),
+            pltpu.VMEM((shards, rows, D), low),
+            pltpu.VMEM(out_weight.shape, low),
+            pltpu.VMEM(gate_up_weight.shape, low),
+            pltpu.VMEM(down_weight.shape, low),
+            pltpu.VMEM((shards, rows, D), low),
+            pltpu.VMEM((2 * rows, D), f32),
+            pltpu.VMEM((group, D), low),
+            pltpu.VMEM((group, 2 * inner), f32),
+            pltpu.VMEM((group, inner), low),
+            pltpu.VMEM((group, 2 * inner), low),
+        ] + line_sems(shards, 1) + [pltpu.SemaphoreType.DMA((11,))],
+        compiler_params=pltpu.CompilerParams(
+            collective_id=9, has_side_effects=True, vmem_limit_bytes=63 * 2**20
+        ),
+        name="hidden",
+        cost_estimate=pl.CostEstimate(flops=24 * 10**9, bytes_accessed=150 * 10**6, transcendentals=0),
+    )(attended, tokens, out_weight, gate_up_weight, down_weight, cotangent, gain, shift)
 
 
 def head_mask(even, rows):
@@ -337,33 +653,12 @@
     return (column <= row) & (seg_rows[at : at + rows, :1] == seg_columns[:1, :count])
 
 
-def line_sends(z, shards, way, step):
-    if way == 0:
-        return (z + 1 < shards) & (z - step >= 0)
-    return (z >= 1) & (z + step < shards)
-
-
-def line_gets(z, shards, way, step):
-    return (z - step >= 1) if way == 0 else (z + step + 1 < shards)
-
-
-def attend_kernel(shards, rows, qkv, seg_rows, seg_columns, attended, stats,
-                  a_buf, a_send, a_recv, loc):
+def attend_body(rows, qkv, seg_rows, seg_columns, a_buf, stats, done):
     z = lax.axis_index("shard")
     width = qkv.shape[1] // 3
-    group = qkv.shape[0]
     pairs = width // 128
-    greet_line(z, shards)
-
-    def a_copy(way, step, block):
-        target = z + 1 if way == 0 else z - 1
-        owner = z - step if way == 0 else z + step
-        piece = a_buf.at[owner, pl.ds(block * rows, rows)]
-        return remote(piece, piece, a_send.at[way, step, block], a_recv.at[way, step, block], {"shard": target})
-
     scale = HEAD_DIM ** (-0.5)
-    blocks = group // rows
-    for block in range(blocks):
+    for block in range(qkv.shape[0] // rows):
         at = block * rows
         count = at + rows
         seen = block_visible(at, rows, seg_rows, seg_columns)
@@ -387,30 +682,24 @@
                 stats[at:count, 64 + head : 65 + head] = 1.0 / total
             merged = jnp.where(head_mask(True, rows), results[0], results[1])
             a_buf[z, at:count, lanes] = merged.astype(jnp.bfloat16)
-        for way in (0, 1):
-            @pl.when(line_sends(z, shards, way, 0))
-            def _():
-                a_copy(way, 0, block).start()
+        done(block)
+
+
+def attend_kernel(shards, rows, qkv, seg_rows, seg_columns, attended, stats, a_buf, a_send, a_recv, loc):
+    z = lax.axis_index("shard")
+    width = qkv.shape[1] // 3
+    blocks = qkv.shape[0] // rows
+    greet_line(z, shards)
+    line = Line(shards, blocks, None, a_buf, a_send, a_recv)
+    attend_body(rows, qkv, seg_rows, seg_columns, a_buf, stats, line.start)
     for step in range(shards - 1):
         for block in range(blocks):
-            for way in (0, 1):
-                @pl.when(line_gets(z, shards, way, step))
-                def _():
-                    a_copy(way, step, block).wait_recv()
-                if step + 1 < shards - 1:
-                    @pl.when(line_sends(z, shards, way, step + 1))
-                    def _():
-                        a_copy(way, step + 1, block).start()
-    keep_a = [pltpu.make_async_copy(a_buf.at[o], attended.at[:, pl.ds(o * width, width)], loc.at[o]) for o in range(shards)]
-    for copy in keep_a:
+            line.relay(step, block)
+    keep = [pltpu.make_async_copy(a_buf.at[o], attended.at[:, pl.ds(o * width, width)], loc.at[o]) for o in range(shards)]
+    for copy in keep:
         copy.start()
-    for step in range(shards - 1):
-        for block in range(blocks):
-            for way in (0, 1):
-                @pl.when(line_sends(z, shards, way, step))
-                def _():
-                    a_copy(way, step, block).wait_send()
-    for copy in keep_a:
+    line.finish()
+    for copy in keep:
         copy.wait()
 
 
@@ -664,26 +953,6 @@
     )(first, second)
 
 
-class Cube:
-    def __init__(self):
-        r = lax.axis_index("replica")
-        self.core, self.x, self.y = r % 2, (r // 2) % 2, r // 4
-        self.place = 2 * self.y + self.x
-        self.to_x = {"replica": r + 2 - 4 * self.x}
-        self.to_y = {"replica": r + 4 - 8 * self.y}
-        self.to_core = {"replica": r + 1 - 2 * self.core}
-
-    def partners(self, shards):
-        z = lax.axis_index("shard")
-        return [((z != o), {"shard": o}) for o in range(shards)] + [
-            (z >= 0, d) for d in (self.to_x, self.to_y, self.to_core)
-        ]
-
-
-def rows_of(ref, start, unit, count):
-    return ref.at[pl.ds(pl.multiple_of(start, unit), count)]
-
-
 def add_rows(target, source, count):
     step = 16
 
@@ -780,21 +1049,17 @@
 
 
 class Owners:
-    def __init__(self, cube, shards, share, parts, reducer, out, send, recv, loc):
-        self.cube, self.shards, self.share, self.parts = cube, shards, share, parts
-        self.source, self.out, self.send, self.recv, self.loc = reducer, out, send, recv, loc
+    def __init__(self, shards, parts, source, out, send, recv, loc):
+        self.shards, self.parts, self.source, self.out = shards, parts, source, out
+        self.send, self.recv, self.loc = send, recv, loc
         self.z = lax.axis_index("shard")
+        self.width = out.shape[1] // (shards * parts)
 
     def target(self, shard, part):
-        width = self.out.shape[1] // (self.shards * self.parts)
-        start = (self.cube.core * 4 + self.cube.place) * self.share
-        return self.out.at[
-            pl.ds(pl.multiple_of(start, 16), self.share), pl.ds(aligned(part * self.shards + shard, width), width)
-        ]
+        return self.out.at[:, pl.ds(aligned((part * self.shards + shard) * (self.width // 128), 128), self.width)]
 
     def piece(self, o, part):
-        width = self.out.shape[1] // (self.shards * self.parts)
-        return self.source(o).at[:, pl.ds(part * width, width)]
+        return self.source(o).at[:, pl.ds(part * self.width, self.width)]
 
     def copy(self, o, part):
         return remote(self.piece(o, part), self.target(self.z, part), self.send.at[o, part], self.recv.at[self.z, part], {"shard": o})
@@ -835,15 +1100,21 @@
                     self.copy(o, part).wait_send()
 
 
+def owner_sems(shards, parts):
+    dma = pltpu.SemaphoreType.DMA
+    return [dma((shards, parts)), dma((shards, parts)), dma((parts,))]
+
+
 class Gatherer:
-    def __init__(self, cube, share, out, send, recv):
-        self.cube, self.share, self.out, self.send, self.recv = cube, share, out, send, recv
-        self.cut = 16 * ((share // 16 + 1) // 2)
+    def __init__(self, cube, share, out, sems):
+        self.cube, self.share, self.out = cube, share, out
+        self.send, self.recv, self.loc = sems
+        self.count = share.shape[0]
+        self.cut = 16 * ((self.count // 16 + 1) // 2)
 
     def rows(self, place, half=None):
-        first, count = {None: (0, self.share), 0: (0, self.cut), 1: (self.cut, self.share - self.cut)}[half]
-        start = (self.cube.core * 4 + place) * self.share + first
-        return rows_of(self.out, start, 16, count)
+        first, count = {None: (0, self.count), 0: (0, self.cut), 1: (self.cut, self.count - self.cut)}[half]
+        return rows_of(self.out, (self.cube.core * 4 + place) * self.count + first, 16, count)
 
     def copy(self, kind):
         c = self.cube
@@ -858,18 +1129,23 @@
             (self.rows(at_y), c.to_core),
             (self.rows(3 - c.place), c.to_core),
         )[kind]
-        return remote(block, block, self.send.at[kind], self.recv.at[kind], device)
+        source = self.share if kind in (0, 1, 4) else block
+        return remote(source, block, self.send.at[kind], self.recv.at[kind], device)
+
+    def local(self):
+        return pltpu.make_async_copy(self.share, self.rows(self.cube.place), self.loc.at[0])
 
     def start(self):
         for kind in (0, 1, 4):
             self.copy(kind).start()
+        self.local().start()
 
     def pass_on(self):
         self.copy(0).wait_recv()
         self.copy(2).start()
+        self.copy(5).start()
         self.copy(1).wait_recv()
         self.copy(3).start()
-        self.copy(5).start()
         self.copy(6).start()
 
     def pass_last(self):
@@ -882,6 +1158,12 @@
             self.copy(kind).wait_recv()
         for kind in range(8):
             self.copy(kind).wait_send()
+        self.local().wait()
+
+
+def gatherer_sems():
+    dma = pltpu.SemaphoreType.DMA
+    return [dma((8,)), dma((8,)), dma((1,))]
 
 
 class LineSum:
@@ -898,16 +1180,20 @@
         place = self.got.at[way, block, self.piece(cut)]
         return remote(place if source is None else source, place, self.send.at[way, block, cut], self.recv.at[way, block, cut], {"shard": target})
 
-    def order(self, t):
-        last = self.z // (self.shards - 1)
-        return self.shards - 1 - t + last * (2 * t - self.shards + 1)
-
-    def ready(self, block):
+    def pair(self, t):
+        half = self.shards // 2
+        upper = self.z // half
+        return half - 1 - t + upper * (2 * t - half + 1)
+
+    def ready(self, pair):
         for way in (0, 1):
-            @pl.when((self.z == (0 if way == 0 else self.shards - 1)) & (block != self.z))
-            def _():
-                for cut in range(self.cuts):
-                    self.copy(way, block, cut, self.own.at[block, self.piece(cut)]).start()
+            for i in (0, 1):
+                block = 2 * pair + (1 - i if way == 0 else i)
+
+                @pl.when((self.z == (0 if way == 0 else self.shards - 1)) & (block != self.z))
+                def _():
+                    for cut in range(self.cuts):
+                        self.copy(way, block, cut, self.own.at[block, self.piece(cut)]).start()
 
     def step_on(self, far, cut):
         for way in (0, 1):
@@ -969,102 +1255,160 @@
     ]
 
 
-def block_product(own, block, slopes, weight, tile=256):
+def pair_product(own, pair, slopes, weight, tile=512):
     rows = own.shape[1]
 
     @pl.loop(0, own.shape[2] // tile)
     def _(t):
         columns = pl.ds(aligned(t, tile), tile)
-        value = contract_last(slopes[pl.ds(aligned(block, rows), rows), :], weight[columns, :])
-        own[block, :, columns] = value.astype(own.dtype)
-
-
-def term_product(term, chunk, left, right, tile):
-    columns = right.shape[1]
-
-    @pl.loop(0, columns // tile)
-    def _(t):
-        place = pl.ds(aligned(t, tile), tile)
-        term[chunk, :, place] = contract_first(left[...], right[:, place]).astype(term.dtype)
-
-
-def hidden_back_kernel(shards, slopes, weight, hidden, cotangent, total, down_grad,
-                       own, got, z_send, z_recv, term, core, near, last, r_send, r_recv,
-                       share_send, share_recv, loc):
-    cube = Cube()
-    z = lax.axis_index("shard")
-    greet(cube.partners(shards), shards + 2)
-    line = LineSum(shards, 3, own, got, z_send, z_recv)
-    share = hidden.shape[1] // 8
-    chunks = term.shape[0]
-    columns = term.shape[2]
-    reducer = Reducer(cube, share, term, core, near, last, r_send, r_recv)
-    gatherer = Gatherer(cube, share, down_grad, share_send, share_recv)
-    for k in range(chunks):
-        term[k] = contract_first(hidden[...], cotangent[:, k * columns : (k + 1) * columns]).astype(term.dtype)
-        reducer.start(k)
-    for t in range(shards):
-        block = line.order(t)
-        block_product(own, block, slopes, weight)
-        line.ready(block)
-        if t < chunks:
-            reducer.after_core(t)
-    for t in range(shards, chunks):
-        reducer.after_core(t)
-    steps = [functools.partial(reducer.after_near, k) for k in range(chunks)]
-    steps += [functools.partial(reducer.after_last, k) for k in range(chunks)]
-    moves = [functools.partial(line.step_on, far, cut) for far in range(shards - 1) for cut in range(3)]
-    for i in range(max(len(steps), len(moves))):
+        value = contract_last(slopes[pl.ds(aligned(pair, 2 * rows), 2 * rows), :], weight[columns, :])
+        own[2 * pair, :, columns] = value[:rows].astype(own.dtype)
+        own[2 * pair + 1, :, columns] = value[rows:].astype(own.dtype)
+
+
+def term_product(term, chunk, left, right):
+    term[chunk] = contract_first(left[...], right[...]).astype(term.dtype)
+
+
+def interleave(moves, steps):
+    for i in range(max(len(moves), len(steps))):
         if i < len(moves):
             moves[i]()
         if i < len(steps):
             steps[i]()
+
+
+def load_all(pairs, loc):
+    copies = [pltpu.make_async_copy(source, target, loc.at[i]) for i, (source, target) in enumerate(pairs)]
+    for copy in copies:
+        copy.start()
+    return copies
+
+
+def hidden_back_kernel(shards, slopes, weight, hidden, cotangent, normed_two, total, down_share, gate_up_share,
+                       s_buf, w_buf, h_buf, c_buf, n_buf, own, got, z_send, z_recv,
+                       term, core, near, last, r_send, r_recv,
+                       g_term, g_core, g_near, g_last, g_send, g_recv, loc):
+    cube = Cube()
+    loads = load_all(((slopes, s_buf), (weight, w_buf), (hidden, h_buf), (cotangent, c_buf), (normed_two, n_buf)), loc)
+    greet(cube.partners(shards), shards + 2)
+    line = LineSum(shards, 3, own, got, z_send, z_recv)
+    share = hidden.shape[1] // 8
+    width = D // shards
+    chunks, _, columns = term.shape
+    early = g_term.shape[0]
+    reducer = Reducer(cube, share, term, core, near, last, r_send, r_recv)
+    g_reducer = Reducer(cube, width // 8, g_term, g_core, g_near, g_last, g_send, g_recv)
+    for copy in loads[:2]:
+        copy.wait()
+    for t in range(shards // 2):
+        pair = line.pair(t)
+        pair_product(own, pair, s_buf, w_buf)
+        line.ready(pair)
+        if t == 0:
+            for copy in loads[2:]:
+                copy.wait()
+            for k in range(chunks):
+                term_product(term, k, h_buf, c_buf.at[:, pl.ds(k * columns, columns)])
+                reducer.start(k)
+    for k in range(chunks):
+        reducer.after_core(k)
+    for k in range(early):
+        term_product(g_term, k, n_buf.at[:, pl.ds(k * width, width)], s_buf)
+        g_reducer.start(k)
     keep = []
-    for k in range(chunks):
-        target = down_grad.at[pl.ds(pl.multiple_of((cube.core * 4 + cube.place) * share, 16), share), pl.ds(k * columns, columns)]
-        copy = pltpu.make_async_copy(reducer.own(k), target, loc.at[k])
+
+    def keep_down(k):
+        copy = pltpu.make_async_copy(reducer.own(k), down_share.at[:, pl.ds(k * columns, columns)], loc.at[5 + k])
         copy.start()
         keep.append(copy)
-    for copy in keep:
-        copy.wait()
-    gatherer.start()
+
+    def keep_gate_up(k):
+        copy = pltpu.make_async_copy(g_reducer.own(k), gate_up_share.at[k], loc.at[5 + chunks + k])
+        copy.start()
+        keep.append(copy)
+
+    steps = [functools.partial(reducer.after_near, k) for k in range(chunks)]
+    steps += [functools.partial(g_reducer.after_core, k) for k in range(early)]
+    for k in range(chunks):
+        steps += [functools.partial(reducer.after_last, k), functools.partial(keep_down, k)]
+    steps += [functools.partial(g_reducer.after_near, k) for k in range(early)]
+    for k in range(early):
+        steps += [functools.partial(g_reducer.after_last, k), functools.partial(keep_gate_up, k)]
+    moves = [functools.partial(line.step_on, far, cut) for far in range(shards - 1) for cut in range(3)]
+    interleave(moves, steps)
     line.result(total)
-    gatherer.pass_on()
-    gatherer.pass_last()
     line.finish()
     for k in range(chunks):
         reducer.finish(k)
-    gatherer.finish()
-
-
-def hidden_back_call(shards, slopes, weight, hidden, cotangent):
+    for k in range(early):
+        g_reducer.finish(k)
+    for copy in keep:
+        copy.wait()
+
+
+def hidden_back_call(shards, slopes, weight, hidden, cotangent, normed_two):
     group, inner = hidden.shape
     rows = group // shards
     share = inner // 8
     chunks = 4
-    vm = pl.BlockSpec(memory_space=pltpu.VMEM)
+    early = shards // 2
+    width = D // shards
+    low = jnp.bfloat16
+    any_ = pl.BlockSpec(memory_space=pl.ANY)
     dma = pltpu.SemaphoreType.DMA
     return pl.pallas_call(
         functools.partial(hidden_back_kernel, shards),
-        out_shape=[jax.ShapeDtypeStruct((rows, D), jnp.float32), jax.ShapeDtypeStruct((inner, D), jnp.bfloat16)],
-        in_specs=[vm] * 4,
-        out_specs=[vm, pl.BlockSpec(memory_space=pl.ANY)],
-        scratch_shapes=line_scratch(shards, rows, D, 3) + reducer_scratch(chunks, share, D // chunks)
-        + [dma((8,)), dma((8,)), dma((chunks,))],
-        compiler_params=pltpu.CompilerParams(collective_id=6, has_side_effects=True, vmem_limit_bytes=56 * 2**20),
+        out_shape=[
+            jax.ShapeDtypeStruct((rows, D), jnp.float32),
+            jax.ShapeDtypeStruct((share, D), low),
+            jax.ShapeDtypeStruct((early, width // 8, 2 * inner), low),
+        ],
+        in_specs=[any_] * 5,
+        out_specs=[pl.BlockSpec(memory_space=pltpu.VMEM), any_, any_],
+        scratch_shapes=[pltpu.VMEM(a.shape, low) for a in (slopes, weight, hidden, cotangent, normed_two)]
+        + line_scratch(shards, rows, D, 3) + reducer_scratch(chunks, share, D // chunks)
+        + reducer_scratch(early, width // 8, 2 * inner) + [dma((5 + chunks + early,))],
+        compiler_params=pltpu.CompilerParams(collective_id=6, has_side_effects=True, vmem_limit_bytes=63 * 2**20),
         name="hidden_back",
         cost_estimate=pl.CostEstimate(flops=10**10, bytes_accessed=200 * 10**6, transcendentals=0),
-    )(slopes, weight, hidden, cotangent)
-
-
-def heads_back_kernel(shards, rows, d_attended_own, d_middle_own, qkv, stats, seg_rows, seg_columns, cosine, minus, plus,
-                      normed_two, slopes, d_qkv, bias_grad, d_middle_columns, share_out,
-                      d_keys, d_values, d_attended, term, core, near, last, r_send, r_recv, e_send, e_recv, loc):
+    )(slopes, weight, hidden, cotangent, normed_two)
+
+
+def norm_back_rows(slope, values, gain):
+    centered = values - jnp.mean(values, axis=-1, keepdims=True)
+    inverse = lax.rsqrt(jnp.mean(centered * centered, axis=-1, keepdims=True) + norm_eps)
+    unit = centered * inverse
+    scaled = slope * gain
+    back = inverse * (
+        scaled
+        - jnp.mean(scaled, axis=-1, keepdims=True)
+        - unit * jnp.mean(scaled * unit, axis=-1, keepdims=True)
+    )
+    return back, unit
+
+
+def heads_back_kernel(shards, rows, d_normed_two, middle, cotangent, gain, out_weight, qkv, stats, seg_rows, seg_columns,
+                      cosine, minus, plus, normed_two, slopes, attended, down_share, gate_up_first,
+                      d_middle, norm_grads, d_qkv, bias_grad, gate_up_rows, out_rows, down_grad,
+                      o_buf, n_buf, s_buf, a_buf, m_low, da_own, d_attended, m_columns, d_keys, d_values,
+                      g_term, g_core, g_near, g_last, g_send, g_recv,
+                      o_term, o_core, o_near, o_last, o_send, o_recv,
+                      e_send, e_recv, loc, *sems):
     cube = Cube()
     z = lax.axis_index("shard")
+    loads = load_all(((out_weight, o_buf), (normed_two, n_buf), (slopes, s_buf), (attended, a_buf)), loc)
     greet(cube.partners(shards), shards + 2)
     width = D // shards
-    arrays = ((d_attended_own, d_attended), (d_middle_own, d_middle_columns))
+    share = width // 8
+    first = gate_up_first.shape[0]
+    gatherer = Gatherer(cube, down_share, down_grad, sems[0:3])
+    g_reducer = Reducer(cube, share, g_term, g_core, g_near, g_last, g_send, g_recv)
+    o_reducer = Reducer(cube, share, o_term, o_core, o_near, o_last, o_send, o_recv)
+    owners = Owners(shards, 2, lambda o: gate_up_first.at[o] if o < first else g_reducer.own(o - first), gate_up_rows, *sems[3:6])
+    o_owners = Owners(shards, 1, o_reducer.own, out_rows, *sems[6:9])
+    gatherer.start()
+    arrays = ((da_own, d_attended), (m_low, m_columns))
 
     def move(k, o):
         source, target = arrays[k]
@@ -1077,148 +1421,240 @@
 
     def here(k, o):
         source, target = arrays[k]
-        return pltpu.make_async_copy(source.at[:, pl.ds(o * width, width)], target.at[pl.ds(o * rows, rows)], loc.at[k])
-
-    for k in (0, 1):
+        return pltpu.make_async_copy(source.at[:, pl.ds(o * width, width)], target.at[pl.ds(o * rows, rows)], loc.at[4 + k])
+
+    def begin(k, o):
+        @pl.when(z != o)
+        def _():
+            move(k, o).start()
+
+        @pl.when(z == o)
+        def _():
+            here(k, o).start()
+
+    def arrive(k):
         for o in range(shards):
             @pl.when(z != o)
             def _():
-                move(k, o).start()
+                arrival(k, o).wait_recv()
 
             @pl.when(z == o)
             def _():
-                here(k, o).start()
-    share = D // shards // 8
-    reducer = Reducer(cube, share, term, core, near, last, r_send, r_recv)
+                here(k, o).wait()
+
+    norm_grads[...] = jnp.zeros_like(norm_grads)
+
+    @pl.loop(0, rows // 16)
+    def _(i):
+        block = pl.ds(aligned(i, 16), 16)
+        slope = d_normed_two[block, :]
+        back, unit = norm_back_rows(slope, middle[block, :], gain[...])
+        value = cotangent[block, :].astype(jnp.float32) + back
+        d_middle[block, :] = value
+        m_low[block, :] = value.astype(jnp.bfloat16)
+        norm_grads[0:8, :] += (slope * unit).reshape(2, 8, D).sum(axis=0)
+        norm_grads[8:16, :] += slope.reshape(2, 8, D).sum(axis=0)
+
+    loads[0].wait()
+    for o in range(shards):
+        da_own[:, o * width : (o + 1) * width] = contract_last(
+            m_low[...], o_buf[o * width : (o + 1) * width, :]).astype(jnp.bfloat16)
+        begin(0, o)
+    for o in range(shards):
+        begin(1, o)
+    loads[1].wait()
+    loads[2].wait()
+    gatherer.pass_on()
+    for k in range(shards - first):
+        at = (first + k) * width
+        term_product(g_term, k, n_buf.at[:, pl.ds(at, width)], s_buf)
+        g_reducer.start(k)
+    gatherer.pass_last()
+    for k in range(shards - first):
+        g_reducer.after_core(k)
+    arrive(0)
+    for o in range(first):
+        owners.start(o)
+    steps = []
+
+    def out_term(k):
+        if k == 0:
+            loads[3].wait()
+            arrive(1)
+        term_product(o_term, k, a_buf.at[:, pl.ds(k * width, width)], m_columns)
+        o_reducer.start(k)
+
+    for k in range(shards - first):
+        steps.append(functools.partial(g_reducer.after_near, k))
     for k in range(shards):
-        term_product(term, k, normed_two.at[:, pl.ds(k * width, width)], slopes, 256)
-        reducer.start(k)
-    for k in (0, 1):
-        for o in range(shards):
-            @pl.when(z != o)
-            def _():
-                arrival(k, o).wait_recv()
-
-            @pl.when(z == o)
-            def _():
-                here(k, o).wait()
-    steps = [functools.partial(reducer.after_core, k) for k in range(shards)]
-    steps += [functools.partial(reducer.after_near, k) for k in range(shards)]
-    steps += [functools.partial(reducer.after_last, k) for k in range(shards)]
+        steps.append(functools.partial(out_term, k))
+    for k in range(shards):
+        steps.append(functools.partial(o_reducer.after_core, k))
+    for k in range(shards - first):
+        steps += [functools.partial(g_reducer.after_last, k), functools.partial(owners.start, first + k)]
+    for k in range(shards):
+        steps.append(functools.partial(o_reducer.after_near, k))
+    for k in range(shards):
+        steps += [functools.partial(o_reducer.after_last, k), functools.partial(o_owners.start, k)]
     attend_back_body(rows, qkv, d_attended, stats, seg_rows, seg_columns, cosine, minus, plus,
                      d_qkv, bias_grad, d_keys, d_values, steps)
     for step in steps:
         step()
-    keep = [pltpu.make_async_copy(reducer.own(k), share_out.at[k], loc.at[2 + k]) for k in range(shards)]
-    for copy in keep:
-        copy.start()
+    owners.arrive()
+    o_owners.arrive()
     for k in (0, 1):
         for o in range(shards):
             @pl.when(z != o)
             def _():
                 move(k, o).wait_send()
+    for k in range(shards - first):
+        g_reducer.finish(k)
     for k in range(shards):
-        reducer.finish(k)
-    for copy in keep:
-        copy.wait()
-
-
-def heads_back_call(shards, rows, d_attended_own, d_middle_own, qkv, stats, seg_rows, seg_columns, cosine, minus, plus, normed_two, slopes):
+        o_reducer.finish(k)
+    owners.finish()
+    o_owners.finish()
+    gatherer.finish()
+
+
+def heads_back_call(shards, rows, d_normed_two, middle, cotangent, gain, out_weight, qkv, stats, seg_rows, seg_columns,
+                    cosine, minus, plus, normed_two, slopes, attended, down_share, gate_up_first):
     group = qkv.shape[0]
     width = D // shards
     share = width // 8
     columns = slopes.shape[1]
+    late = shards - gate_up_first.shape[0]
     vm = pl.BlockSpec(memory_space=pltpu.VMEM)
     any_ = pl.BlockSpec(memory_space=pl.ANY)
     dma = pltpu.SemaphoreType.DMA
     low = jnp.bfloat16
+    f32 = jnp.float32
     return pl.pallas_call(
         functools.partial(heads_back_kernel, shards, rows),
         out_shape=[
+            jax.ShapeDtypeStruct((rows, D), f32),
+            jax.ShapeDtypeStruct((16, D), f32),
             jax.ShapeDtypeStruct((group, 3 * width), low),
-            jax.ShapeDtypeStruct((8, 3 * width), jnp.float32),
-            jax.ShapeDtypeStruct((group, width), low),
-            jax.ShapeDtypeStruct((shards, share, columns), low),
+            jax.ShapeDtypeStruct((8, 3 * width), f32),
+            jax.ShapeDtypeStruct((share, shards * columns), low),
+            jax.ShapeDtypeStruct((share, D), low),
+            jax.ShapeDtypeStruct((8 * down_share.shape[0], D), low),
         ],
-        in_specs=[any_, any_] + [vm] * 9,
-        out_specs=[vm, vm, any_, any_],
+        in_specs=[vm] * 4 + [any_] + [vm] * 7 + [any_] * 5,
+        out_specs=[vm, vm, vm, vm, any_, any_, any_],
         scratch_shapes=[
-            pltpu.VMEM((group, width), jnp.float32), pltpu.VMEM((group, width), jnp.float32),
-            pltpu.VMEM((group, width), low),
-        ] + reducer_scratch(shards, share, columns) + [dma((2, shards)), dma((2, shards)), dma((2 + shards,))],
-        compiler_params=pltpu.CompilerParams(collective_id=7, has_side_effects=True, vmem_limit_bytes=56 * 2**20),
+            pltpu.VMEM(out_weight.shape, low), pltpu.VMEM(normed_two.shape, low), pltpu.VMEM(slopes.shape, low),
+            pltpu.VMEM(attended.shape, low),
+            pltpu.VMEM((rows, D), low), pltpu.VMEM((rows, D), low),
+            pltpu.VMEM((group, width), low), pltpu.VMEM((group, width), low),
+            pltpu.VMEM((group, width), f32), pltpu.VMEM((group, width), f32),
+        ] + reducer_scratch(late, share, columns) + reducer_scratch(shards, share, width)
+        + [dma((2, shards)), dma((2, shards)), dma((6,))] + gatherer_sems() + owner_sems(shards, 2) + owner_sems(shards, 1),
+        compiler_params=pltpu.CompilerParams(collective_id=7, has_side_effects=True, vmem_limit_bytes=63 * 2**20),
         name="heads_back",
         cost_estimate=pl.CostEstimate(flops=10**10, bytes_accessed=200 * 10**6, transcendentals=0),
-    )(d_attended_own, d_middle_own, qkv, stats, seg_rows, seg_columns, cosine, minus, plus, normed_two, slopes)
-
-
-def input_back_kernel(shards, slopes, weight, normed, attended, d_middle, gate_up_share,
-                      total, qkv_grad, out_grad, gate_up_grad,
-                      own, got, z_send, z_recv,
-                      term, core, near, last, r_send, r_recv,
-                      o_term, o_core, o_near, o_last, o_send, o_recv,
-                      t_send, t_recv, loc, g_send, g_recv):
+    )(d_normed_two, middle, cotangent, gain, out_weight, qkv, stats, seg_rows, seg_columns, cosine, minus, plus,
+      normed_two, slopes, attended, down_share, gate_up_first)
+
+
+def input_back_kernel(shards, slopes, weight, normed, tokens, gain, d_middle, bias_grad, norm_grads, gate_up_rows, out_rows,
+                      input_grad, small, qkv_grad, out_grad, gate_up_grad,
+                      w_buf, n_buf, total, part, part_in, own, got, z_send, z_recv,
+                      term, core, near, last, r_send, r_recv, qkv_rows, s_send, s_recv, loc, *sems):
     cube = Cube()
+    z = lax.axis_index("shard")
+    loads = load_all(((weight, w_buf), (normed, n_buf)), loc)
     greet(cube.partners(shards), shards + 2)
+    rows = tokens.shape[0]
     width = D // shards
     share = width // 8
     line = LineSum(shards, 3, own, got, z_send, z_recv)
     reducer = Reducer(cube, share, term, core, near, last, r_send, r_recv)
-    o_reducer = Reducer(cube, share, o_term, o_core, o_near, o_last, o_send, o_recv)
-    sources = (lambda o: gate_up_share.at[o], o_reducer.own, reducer.own)
-    outs = (gate_up_grad, out_grad, qkv_grad)
-    owners = [Owners(cube, shards, share, p, s, out, t_send.at[i], t_recv.at[i], loc.at[i])
-              for i, (p, s, out) in enumerate(zip((2, 1, 3), sources, outs))]
-    gatherers = [Gatherer(cube, share, out, g_send.at[i], g_recv.at[i]) for i, out in enumerate(outs)]
+    owners = Owners(shards, 3, reducer.own, qkv_rows, *sems[0:3])
+    g_gatherer = Gatherer(cube, gate_up_rows, gate_up_grad, sems[3:6])
+    o_gatherer = Gatherer(cube, out_rows, out_grad, sems[6:9])
+    gatherer = Gatherer(cube, qkv_rows, qkv_grad, sems[9:12])
+    loads[0].wait()
+    for t in range(shards // 2):
+        pair = line.pair(t)
+        pair_product(own, pair, slopes, w_buf)
+        line.ready(pair)
+        if t == 0:
+            loads[1].wait()
+            for k in range(shards):
+                term_product(term, k, n_buf.at[:, pl.ds(k * width, width)], slopes)
+                reducer.start(k)
+    steps = [functools.partial(reducer.after_core, k) for k in range(shards)]
+    steps += [g_gatherer.start, o_gatherer.start]
+    steps += [functools.partial(reducer.after_near, k) for k in range(shards)]
+    for k in range(shards):
+        steps += [functools.partial(reducer.after_last, k), functools.partial(owners.start, k)]
+    steps += [o_gatherer.pass_on, g_gatherer.pass_on]
+    moves = [functools.partial(line.step_on, far, cut) for far in range(shards - 1) for cut in range(3)]
+    interleave(moves, steps)
+    line.result(total)
+    owners.arrive()
+    gatherer.start()
+
+    part[...] = jnp.zeros_like(part)
+
+    @pl.loop(0, rows // 16)
+    def _(i):
+        block = pl.ds(aligned(i, 16), 16)
+        slope = total[block, :]
+        back, unit = norm_back_rows(slope, tokens[block, :].astype(jnp.float32), gain[...])
+        input_grad[block, :] = d_middle[block, :] + back
+        ones = (slope * unit).reshape(2, 8, D).sum(axis=0).sum(axis=0, keepdims=True)
+        twos = slope.reshape(2, 8, D).sum(axis=0).sum(axis=0, keepdims=True)
+        for o in range(shards):
+            part[o, 3:4, :] += ones[:, o * width : (o + 1) * width]
+            part[o, 4:5, :] += twos[:, o * width : (o + 1) * width]
     for o in range(shards):
-        owners[0].start(o)
-    for k in range(shards):
-        term_product(term, k, normed.at[:, pl.ds(k * width, width)], slopes, 256)
-        reducer.start(k)
-    for t in range(shards):
-        block = line.order(t)
-        block_product(own, block, slopes, weight)
-        line.ready(block)
-        if t == 0:
-            owners[0].arrive()
-            gatherers[0].start()
-        reducer.after_core(t)
-    for k in range(shards):
-        term_product(o_term, k, attended.at[:, pl.ds(k * width, width)], d_middle, width)
-        o_reducer.start(k)
-    steps = [gatherers[0].pass_on]
-    steps += [functools.partial(reducer.after_near, k) for k in range(shards)]
-    steps += [functools.partial(o_reducer.after_core, k) for k in range(shards)]
-    steps += [gatherers[0].pass_last]
-    for k in range(shards):
-        steps += [functools.partial(reducer.after_last, k), functools.partial(owners[2].start, k)]
-    steps += [functools.partial(o_reducer.after_near, k) for k in range(shards)]
-    for k in range(shards):
-        steps += [functools.partial(o_reducer.after_last, k), functools.partial(owners[1].start, k)]
-    moves = [functools.partial(line.step_on, far, cut) for far in range(shards - 1) for cut in range(3)]
-    for i in range(max(len(steps), len(moves))):
-        if i < len(moves):
-            moves[i]()
-        if i < len(steps):
-            steps[i]()
-    line.result(total)
-    for i in (2, 1):
-        owners[i].arrive()
-        gatherers[i].start()
-    for i in (2, 1):
-        gatherers[i].pass_on()
-    for i in (2, 1):
-        gatherers[i].pass_last()
+        for k in range(2):
+            part[o, 5 + k : 6 + k, :] = jnp.sum(
+                norm_grads[8 * k : 8 * k + 8, o * width : (o + 1) * width], axis=0, keepdims=True)
+    for k in range(3):
+        flat = k * shards + z
+        part[flat // 3, pl.ds(flat % 3, 1), :] = bias_grad[0:1, k * width : (k + 1) * width]
+
+    def small_copy(o):
+        return remote(part.at[o], part_in.at[z], s_send.at[o], s_recv.at[z], {"shard": o})
+
+    def small_arrival(o):
+        return remote(part.at[o], part_in.at[o], s_send.at[o], s_recv.at[o], {"shard": o})
+
+    for o in range(shards):
+        @pl.when(z != o)
+        def _():
+            small_copy(o).start()
+    small[...] = part[z]
+    for o in range(shards):
+        @pl.when(z != o)
+        def _():
+            small_arrival(o).wait_recv()
+            small[...] += part_in[o]
+    sums = [remote(small, part_in.at[shards + i], s_send.at[shards + i], s_recv.at[shards + i], device)
+            for i, device in enumerate((cube.to_core, cube.to_x, cube.to_y))]
+    for i, copy in enumerate(sums):
+        copy.start()
+        copy.wait()
+        small[...] += part_in[shards + i]
+    g_gatherer.pass_last()
+    o_gatherer.pass_last()
+    gatherer.pass_on()
+    gatherer.pass_last()
+    for o in range(shards):
+        @pl.when(z != o)
+        def _():
+            small_copy(o).wait_send()
     line.finish()
     for k in range(shards):
         reducer.finish(k)
-        o_reducer.finish(k)
-    for i in range(3):
-        owners[i].finish()
-        gatherers[i].finish()
-
-
-def input_back_call(shards, slopes, weight, normed, attended, d_middle, gate_up_share):
+    owners.finish()
+    for g in (g_gatherer, o_gatherer, gatherer):
+        g.finish()
+
+
+def input_back_call(shards, slopes, weight, normed, tokens, gain, d_middle, bias_grad, norm_grads, gate_up_rows, out_rows):
     group = slopes.shape[0]
     rows = group // shards
     width = D // shards
@@ -1227,23 +1663,28 @@
     any_ = pl.BlockSpec(memory_space=pl.ANY)
     dma = pltpu.SemaphoreType.DMA
     low = jnp.bfloat16
+    f32 = jnp.float32
     return pl.pallas_call(
         functools.partial(input_back_kernel, shards),
         out_shape=[
-            jax.ShapeDtypeStruct((rows, D), jnp.float32),
+            jax.ShapeDtypeStruct((rows, D), f32),
+            jax.ShapeDtypeStruct((8, width), f32),
             jax.ShapeDtypeStruct((width, 3 * D), low),
             jax.ShapeDtypeStruct((width, D), low),
-            jax.ShapeDtypeStruct((width, shards * gate_up_share.shape[2]), low),
+            jax.ShapeDtypeStruct((width, gate_up_rows.shape[1]), low),
         ],
-        in_specs=[vm] * 5 + [any_],
-        out_specs=[vm, any_, any_, any_],
-        scratch_shapes=line_scratch(shards, rows, D, 3)
-        + reducer_scratch(shards, share, 3 * width) + reducer_scratch(shards, share, width)
-        + [dma((3, shards, 3)), dma((3, shards, 3)), dma((3, 3)), dma((3, 8)), dma((3, 8))],
+        in_specs=[vm, any_, any_, vm, vm, vm, vm, vm, any_, any_],
+        out_specs=[vm, vm, any_, any_, any_],
+        scratch_shapes=[
+            pltpu.VMEM(weight.shape, low), pltpu.VMEM(normed.shape, low), pltpu.VMEM((rows, D), f32),
+            pltpu.VMEM((shards, 8, width), f32), pltpu.VMEM((shards + 3, 8, width), f32),
+        ] + line_scratch(shards, rows, D, 3) + reducer_scratch(shards, share, 3 * width)
+        + [pltpu.VMEM((share, 3 * D), low), dma((shards + 3,)), dma((shards + 3,)), dma((2,))]
+        + owner_sems(shards, 3) + gatherer_sems() * 3,
         compiler_params=pltpu.CompilerParams(collective_id=8, has_side_effects=True, vmem_limit_bytes=60 * 2**20),
         name="input_back",
         cost_estimate=pl.CostEstimate(flops=10**10, bytes_accessed=200 * 10**6, transcendentals=0),
-    )(slopes, weight, normed, attended, d_middle, gate_up_share)
+    )(slopes, weight, normed, tokens, gain, d_middle, bias_grad, norm_grads, gate_up_rows, out_rows)
 
 
 def swap_pieces(pieces):
@@ -1342,6 +1783,119 @@
     return all_tokens, all_vectors, normed, qkv, weight
 
 
+def layer_kernels(shards, tokens, cotangent, weights, vectors, tables):
+    qkv_weight, out_weight, gate_up_weight, down_weight = weights
+    seg_rows, seg_columns, cosine, minus, plus = tables
+    rows = tokens.shape[0]
+    f32 = jnp.float32
+    low = jnp.bfloat16
+    all_tokens, all_vectors, normed, qkv, weight_qkv, weight_out = start_call(
+        shards, tokens, vectors, qkv_weight, out_weight, cosine, minus, plus
+    )
+    gain_one, shift_one, gain_two, shift_two = (
+        all_vectors[:, 3 + i].reshape(1, D) for i in range(4)
+    )
+    attended, stats, weight_gate_up = attend_spread_call(
+        shards, rows, qkv, seg_rows, seg_columns, gate_up_weight
+    )
+    middle, normed_two, hidden, slopes, group_cotangent, down_part = hidden_call(
+        shards, attended, all_tokens, weight_out, weight_gate_up, down_weight, cotangent, gain_two, shift_two
+    )
+    down_own = lax.psum_scatter(down_part, "shard", scatter_dimension=0, tiled=True)
+    d_normed_two, down_share, gate_up_first = hidden_back_call(
+        shards, slopes, weight_gate_up, hidden, group_cotangent.reshape(shards * rows, D), normed_two
+    )
+    d_middle, norm_grads, d_qkv, bias_grad, gate_up_rows, out_rows, down_grad = heads_back_call(
+        shards, rows, d_normed_two, middle, cotangent, gain_two, weight_out, qkv, stats, seg_rows, seg_columns,
+        cosine, minus, plus, normed_two, slopes, attended, down_share, gate_up_first,
+    )
+    input_grad, small, qkv_grad, out_grad, gate_up_grad = input_back_call(
+        shards, d_qkv, weight_qkv, normed, tokens, gain_one, d_middle, bias_grad, norm_grads, gate_up_rows, out_rows
+    )
+    mixed = (middle + down_own.astype(f32)).astype(low)
+    return mixed, input_grad, small, (qkv_grad, out_grad, gate_up_grad, down_grad)
+
+
+def layer_plain(shards, tokens, cotangent, weights, vectors, tables):
+    qkv_weight, out_weight, gate_up_weight, down_weight = weights
+    seg_rows, seg_columns, cosine, minus, plus = tables
+    here = lax.axis_index("shard")
+    row_count = tokens.shape[0]
+    group_rows = row_count * shards
+    width = D // shards
+    f32 = jnp.float32
+    low = jnp.bfloat16
+    weight_out = gather_rows(out_weight)
+    weight_gate_up = spread_rows(gate_up_weight, 2)
+    all_tokens, all_vectors, normed_low, qkv, weight_qkv = start_plain(
+        tokens, vectors, qkv_weight, cosine, minus, plus
+    )
+    gain_one, shift_one, gain_two, shift_two = (
+        all_vectors[:, 3 + i].reshape(D) for i in range(4)
+    )
+    cotangent_later, qkv = lax.optimization_barrier((cotangent, qkv))
+    group_cotangent = lax.all_gather(cotangent_later, "shard", axis=0, tiled=True)
+
+    def local(array):
+        return lax.dynamic_slice_in_dim(array, here * row_count, row_count, axis=0)
+
+    attended, stats = attend_call(shards, row_count, qkv, seg_rows, seg_columns)
+    inputs = all_tokens.reshape(group_rows, D).astype(f32)
+    middle = inputs + jnp.dot(attended, weight_out, preferred_element_type=f32)
+    unit_two, inverse_two = norm_stats(middle)
+    normed_two_low = (unit_two * gain_two + shift_two).astype(low)
+    gate_up = jnp.dot(normed_two_low, weight_gate_up, preferred_element_type=f32)
+    hidden, swiglu_pull = jax.vjp(swiglu, gate_up)
+    hidden_low = hidden.astype(low)
+    d_hidden = contract_last(group_cotangent, down_weight)
+    d_gate_up_low = swiglu_pull(d_hidden)[0].astype(low)
+    down_part = jnp.dot(hidden_low, down_weight, preferred_element_type=f32).astype(low)
+    unit_two_own = local(unit_two)
+    inverse_two_own = local(inverse_two)
+    middle_own = local(middle)
+
+    d_normed_two_part = contract_last(d_gate_up_low, weight_gate_up).astype(low)
+    d_normed_two = scatter_call(shards, d_normed_two_part.reshape(shards, row_count, D), 3)
+    down_grad = lax.psum(contract_first(hidden_low, group_cotangent).astype(low), "replica")
+    d_middle = cotangent.astype(f32) + norm_back(
+        d_normed_two, unit_two_own, inverse_two_own, gain_two
+    )
+    d_gain_two = jnp.sum(d_normed_two * unit_two_own, axis=0)
+    d_shift_two = jnp.sum(d_normed_two, axis=0)
+    d_middle_low = d_middle.astype(low)
+    d_attended_own = contract_last(d_middle_low, weight_out).astype(low)
+    d_attended, d_middle_columns = exchange_call(shards, d_attended_own, d_middle_low)
+    d_projected_low, bias_part = attend_back_call(
+        row_count, qkv, d_attended.reshape(group_rows, width), stats, seg_rows, seg_columns,
+        cosine, minus, plus,
+    )
+    down_own = lax.psum_scatter(down_part, "shard", scatter_dimension=0, tiled=True)
+    mixed = (middle_own + down_own.astype(f32)).astype(low)
+    d_normed_part = contract_last(d_projected_low, weight_qkv).astype(low)
+    d_normed = scatter_call(shards, d_normed_part.reshape(shards, row_count, D), 4)
+    gate_up_grad = sum_columns(normed_two_low, d_gate_up_low, 2)
+    out_grad = sum_columns(attended, d_middle_columns.reshape(group_rows, width), 1)
+    qkv_grad = sum_columns(normed_low, d_projected_low, 3)
+    unit_one, inverse_one = norm_stats(tokens.astype(f32))
+    input_grad = d_middle + norm_back(d_normed, unit_one, inverse_one, gain_one)
+    d_gain_one = jnp.sum(d_normed * unit_one, axis=0)
+    d_shift_one = jnp.sum(d_normed, axis=0)
+
+    bias_part = bias_part[0].reshape(3, 1, width)
+    bias_wide = lax.dynamic_update_slice(
+        jnp.zeros((3, shards, width), f32), bias_part, (0, here, 0)
+    ).reshape(shards, 3 * width)
+    small = jnp.concatenate(
+        [bias_wide]
+        + [v.reshape(shards, width) for v in (d_gain_one, d_shift_one, d_gain_two, d_shift_two)],
+        axis=1,
+    )
+    small = jnp.pad(small, ((0, 0), (0, width)))
+    small = lax.psum(small, ("replica", "shard"))
+    small = lax.dynamic_index_in_dim(small, here, axis=0, keepdims=False)
+    return mixed, input_grad, small, (qkv_grad, out_grad, gate_up_grad, down_grad)
+
+
 def on_device(
     tokens,
     cotangent,
@@ -1358,7 +1912,6 @@
 ):
     shards = lax.axis_size("shard")
     copies = lax.axis_size("replica")
-    here = lax.axis_index("shard")
     row_count = tokens.shape[0]
     group_rows = row_count * shards
     width = D // shards
@@ -1382,100 +1935,24 @@
         [qkv_bias, norm1_gain, norm1_shift, norm2_gain, norm2_shift, jnp.zeros((width,), low)]
     )
     vectors = vectors.astype(f32).reshape(8, width)
-    weight_out = gather_rows(out_weight)
-    weight_gate_up = spread_rows(gate_up_weight, 2)
-    begin = functools.partial(start_call, shards) if copies == 8 else start_plain
-    all_tokens, all_vectors, normed_low, qkv, weight_qkv = begin(
-        tokens, vectors, qkv_weight, cosine, minus, plus
-    )
-    gain_one, shift_one, gain_two, shift_two = (
-        all_vectors[:, 3 + i].reshape(D) for i in range(4)
-    )
-    cotangent_later, qkv = lax.optimization_barrier((cotangent, qkv))
-    group_cotangent = lax.all_gather(cotangent_later, "shard", axis=0, tiled=True)
-
-    def local(array):
-        return lax.dynamic_slice_in_dim(array, here * row_count, row_count, axis=0)
-
-    attended, stats = attend_call(shards, row_count, qkv, seg_rows, seg_columns)
-    inputs = all_tokens.reshape(group_rows, D).astype(f32)
-    middle = inputs + jnp.dot(attended, weight_out, preferred_element_type=f32)
-    unit_two, inverse_two = norm_stats(middle)
-    normed_two_low = (unit_two * gain_two + shift_two).astype(low)
-    gate_up = jnp.dot(normed_two_low, weight_gate_up, preferred_element_type=f32)
-    hidden, swiglu_pull = jax.vjp(swiglu, gate_up)
-    hidden_low = hidden.astype(low)
-    d_hidden = contract_last(group_cotangent, down_weight)
-    d_gate_up_low = swiglu_pull(d_hidden)[0].astype(low)
-    down_part = jnp.dot(hidden_low, down_weight, preferred_element_type=f32).astype(low)
-    unit_two_own = local(unit_two)
-    inverse_two_own = local(inverse_two)
-    middle_own = local(middle)
-
+    weights = (qkv_weight, out_weight, gate_up_weight, down_weight)
+    tables = (seg_rows, seg_columns, cosine, minus, plus)
     if copies == 8:
-        d_normed_two, down_grad = hidden_back_call(
-            shards, d_gate_up_low, weight_gate_up, hidden_low, group_cotangent
-        )
+        outputs = layer_kernels(shards, tokens, cotangent, weights, vectors, tables)
     else:
-        d_normed_two_part = contract_last(d_gate_up_low, weight_gate_up).astype(low)
-        d_normed_two = scatter_call(shards, d_normed_two_part.reshape(shards, row_count, D), 3)
-        down_grad = lax.psum(contract_first(hidden_low, group_cotangent).astype(low), "replica")
-    d_middle = cotangent.astype(f32) + norm_back(
-        d_normed_two, unit_two_own, inverse_two_own, gain_two
-    )
-    d_gain_two = jnp.sum(d_normed_two * unit_two_own, axis=0)
-    d_shift_two = jnp.sum(d_normed_two, axis=0)
-    d_middle_low = d_middle.astype(low)
-    d_attended_own = contract_last(d_middle_low, weight_out).astype(low)
-    if copies == 8:
-        d_projected_low, bias_part, d_middle_columns, gate_up_share = heads_back_call(
-            shards, row_count, d_attended_own, d_middle_low, qkv, stats, seg_rows, seg_columns,
-            cosine, minus, plus, normed_two_low, d_gate_up_low,
-        )
-        down_part, d_projected_low = lax.optimization_barrier((down_part, d_projected_low))
-    else:
-        d_attended, d_middle_columns = exchange_call(shards, d_attended_own, d_middle_low)
-        d_projected_low, bias_part = attend_back_call(
-            row_count, qkv, d_attended.reshape(group_rows, width), stats, seg_rows, seg_columns,
-            cosine, minus, plus,
-        )
-    down_own = lax.psum_scatter(down_part, "shard", scatter_dimension=0, tiled=True)
-    mixed = (middle_own + down_own.astype(f32)).astype(low)
-    if copies == 8:
-        d_normed, qkv_grad, out_grad, gate_up_grad = input_back_call(
-            shards, d_projected_low, weight_qkv, normed_low, attended, d_middle_columns, gate_up_share
-        )
-    else:
-        d_normed_part = contract_last(d_projected_low, weight_qkv).astype(low)
-        d_normed = scatter_call(shards, d_normed_part.reshape(shards, row_count, D), 4)
-        gate_up_grad = sum_columns(normed_two_low, d_gate_up_low, 2)
-        out_grad = sum_columns(attended, d_middle_columns.reshape(group_rows, width), 1)
-        qkv_grad = sum_columns(normed_low, d_projected_low, 3)
-    unit_one, inverse_one = norm_stats(tokens.astype(f32))
-    input_grad = d_middle + norm_back(d_normed, unit_one, inverse_one, gain_one)
-    d_gain_one = jnp.sum(d_normed * unit_one, axis=0)
-    d_shift_one = jnp.sum(d_normed, axis=0)
-
-    bias_part = bias_part[0].reshape(3, 1, width)
-    bias_wide = lax.dynamic_update_slice(
-        jnp.zeros((3, shards, width), f32), bias_part, (0, here, 0)
-    ).reshape(shards, 3 * width)
-    small = jnp.concatenate(
-        [bias_wide]
-        + [v.reshape(shards, width) for v in (d_gain_one, d_shift_one, d_gain_two, d_shift_two)],
-        axis=1,
-    )
-    small = lax.psum(small, ("replica", "shard"))
-    small = lax.dynamic_index_in_dim(small, here, axis=0, keepdims=False)
+        outputs = layer_plain(shards, tokens, cotangent, weights, vectors, tables)
+    mixed, input_grad, small, grads = outputs
     bias_rows = 3 * width
+    small = small.reshape(8 * width)
+    out_dtype = tuple(grad.astype(f32) for grad in grads)
     return (
         mixed,
         input_grad,
-        qkv_grad.astype(f32),
+        out_dtype[0],
         small[:bias_rows],
-        out_grad.astype(f32),
-        gate_up_grad.astype(f32),
-        down_grad.astype(f32),
+        out_dtype[1],
+        out_dtype[2],
+        out_dtype[3],
     ) + tuple(small[bias_rows + i * width : bias_rows + (i + 1) * width] for i in range(4))
 
 

time: 893 us -> 707 us (0.79)
  matrix products: 52.8 us -> 0 us
  waiting for transfers between devices: 49.2 us -> 0.02 us
  blocking collectives: 37.6 us -> 0 us
  other arithmetic: 58.8 us -> 35.7 us
  local copies, waits for them, and re-layouts: 35.3 us -> 15.1 us
    dot_general x5 -> x0, matrix products: 52.8 us -> none  [the longest x2 21 us: contract_last(): lax.dot_general(left, right, (((1,), (1,)), ((), ())), preferred_element_...]
    ppermute x6 -> x0, waiting for transfers between devices: 49.1 us -> none  [swap_pieces(): piece = lax.ppermute(piece, 'shard', [(i, i ^ k) for i in range(shards)])]
    pallas_call x1, Pallas kernels: 200 us -> 162 us  [input_back_call(): pl.pallas_call(functools.partial(input_back_kernel, shards), out_shape=[j...]
    psum x1 -> x0, blocking collectives: 37.6 us -> none  [on_device(): small = lax.psum(small, ('replica', 'shard'))]
    pallas_call x1 -> x2, Pallas kernels: 123 us -> 151 us  [the longest x1 86.2 us: attend_spread_call(): pl.pallas_call(functools.partial(attend_spread_kernel, shards, rows), out...]
    convert_element_type x8 -> x5, other arithmetic: 49.7 us -> 33.2 us  [the longest x4 31 us: on_device(): out_dtype = tuple((grad.astype(f32) for grad in grads))]
    pallas_call x1, Pallas kernels: 96.8 us -> 108 us  [heads_back_call(): pl.pallas_call(functools.partial(heads_back_kernel, shards, rows), out_sh...]
  transfers between devices with their start and end apart: 10 -> 1, of which waited for: 6 -> 0; matrix products, arithmetic and copies ran while one was open for 10% -> 5% of each run, Pallas kernels for 47% -> 55%
where the time goes in v4:
time: 707 us; the launch traced here: 701 us
  Pallas kernels  635 us (90%)
  other arithmetic  35.7 us (5%)
  local copies, waits for them, and re-layouts  15.1 us (2%)
  between operations  14.8 us (2%)
    pallas_call x1, Pallas kernels, input_back_call(): pl.pallas_call(functools.partial(input_back_kernel, shards), out_shape=[j...  162 us
    pallas_call x1, Pallas kernels, hidden_back_call(): pl.pallas_call(functools.partial(hidden_back_kernel, shards), out_shape=[...  115 us
    pallas_call x1, Pallas kernels, heads_back_call(): pl.pallas_call(functools.partial(heads_back_kernel, shards, rows), out_sh...  108 us
    pallas_call x1, Pallas kernels, start_call(): pl.pallas_call(functools.partial(start_kernel, shards), out_shape=[jax.Sh...  99.9 us
    pallas_call x1, Pallas kernels, attend_spread_call(): pl.pallas_call(functools.partial(attend_spread_kernel, shards, rows), out...  86.2 us
    pallas_call x1, Pallas kernels, hidden_call(): pl.pallas_call(functools.partial(hidden_kernel, shards), out_shape=[jax.S...  64.6 us
    convert_element_type x4, other arithmetic, on_device(): out_dtype = tuple((grad.astype(f32) for grad in grads))  31 us
  transfers between devices with their start and end apart: 1, of which 0 were waited for; matrix products, arithmetic and copies ran while one was open for 5% of the time, Pallas kernels for 55%

profile of v4, /device:TPU:9, one launch (start us, length us, event | category | flops | bytes accessed | tf_op | source)
XLA Modules:
  0.0 700.9 jit_solution(2075239175486702859)
XLA Ops:
  7.3 1.0 dynamic-update-slice
  8.3 0.9 dynamic-update-slice.1
  9.1 0.9 dynamic-update-slice.2
  10.0 0.9 dynamic-update-slice.3
  10.9 0.9 dynamic-update-slice.4
  11.9 0.8 reduce-window.8
  13.9 0.8 maximum_maximum_fusion.2
  14.9 1.1 tile.14
  16.1 0.8 tile.31
  17.0 1.1 copy.31.plus
  18.1 1.1 copy-done.7
  19.3 99.9 %start.1 = (bf16[4,192,2048]{2,1,0:T(8,128)(2,1)}, f32[4,8,512]{2,1,0:T(8,128)S(1)}, bf16[768,2048]{1,0:T(8,128)(2,1)}, bf16[768,1536]{1,0:T(8,128)(2,1)}, bf16[...) custom-call(bf16[192,2048]{1,0:T(8,128)(2,1)S(1)} %copy-done.7, f32[8,512]{1,0:T(8,128)S(1)} %reshape.88.vectors, ...), custom_call_target="tpu_custom_call" | custom-call | flops 4831838208 | bytes 150000000 | tf_op jit(solution)/shard_map/start/pallas_call | solution.py:400
  120.0 1.8 copy-done
  121.8 86.2 %attend_spread.1 = (bf16[768,2048]{1,0:T(8,128)(2,1)}, f32[768,128]{1,0:T(8,128)S(1)}, bf16[2048,2816]{1,0:T(8,128)(2,1)}) custom-call(bf16[768,1536]{1,0:T(8,128)(2,1)S(1)} %copy-done, s32[768,128]{1,0:T(8,128)S(1)} %broadcast_in_dim.13.seg_rows, s32[8,768]{1,0:T(8,128)S(1)} %broadcast_in_dim.14.seg_columns, bf16[512,11264]{1,0:T(8,128)(2,1)} %gate_up.1), custom_call_target="tpu_custom_call" | custom-call | flops 1000000000 | bytes 150000000 | tf_op jit(solution)/shard_map/attend_spread/pallas_call | solution.py:481
  208.8 64.6 %hidden.1 = (f32[192,2048]{1,0:T(8,128)}, bf16[768,2048]{1,0:T(8,128)(2,1)}, bf16[768,1408]{1,0:T(8,128)(2,1)}, bf16[768,2816]{1,0:T(8,128)(2,1)}, bf16[4,192,20...) custom-call(bf16[768,2048]{1,0:T(8,128)(2,1)} %get-tuple-element.42.attended, ...), custom_call_target="tpu_custom_call" | custom-call | flops 24000000000 | bytes 150000000 | tf_op jit(solution)/shard_map/hidden/pallas_call | solution.py:607
  273.4 114.8 %hidden_back.1 = (f32[192,2048]{1,0:T(8,128)}, bf16[176,2048]{1,0:T(8,128)(2,1)}, bf16[2,64,2816]{2,1,0:T(8,128)(2,1)}) custom-call(bf16[768,2816]{1,0:T(8,128)(2,1)} %get-tuple-element.49.slopes, bf16[2048,2816]{1,0:T(8,128)(2,1)} %get-tuple-element.45.gate_up_weight.weight, bf16[768,1408]{1,0:T(8,128)(2,1)} %get-tuple-element.50.hidden, ...), custom_call_target="tpu_custom_call" | custom-call | flops 10000000000 | bytes 200000000 | tf_op jit(solution)/shard_map/hidden_back/pallas_call | solution.py:1360
  388.2 108.0 %heads_back.1 = (f32[192,2048]{1,0:T(8,128)}, f32[16,2048]{1,0:T(8,128)}, bf16[768,1536]{1,0:T(8,128)(2,1)}, f32[8,1536]{1,0:T(8,128)}, bf16[64,11264]{1,0:T(8,1...) custom-call(f32[192,2048]{1,0:T(8,128)} %get-tuple-element.53.d_normed_two, ...), custom_call_target="tpu_custom_call" | custom-call | flops 10000000000 | bytes 200000000 | tf_op jit(solution)/shard_map/heads_back/pallas_call | solution.py:1531
  496.3 161.8 %input_back.1 = (f32[192,2048]{1,0:T(8,128)}, f32[8,512]{1,0:T(8,128)}, bf16[512,6144]{1,0:T(8,128)(2,1)}, bf16[512,2048]{1,0:T(8,128)(2,1)}, bf16[512,11264]{1,0:T(8,128)(2,1)}) custom-call(bf16[768,1536]{1,0:T(8,128)(2,1)} %get-tuple-element.57.slopes, bf16[2048,1536]{1,0:T(8,128)(2,1)} %get-tuple-element.58.weight, ...), custom_call_target="tpu_custom_call" | custom-call | flops 10000000000 | bytes 200000000 | tf_op jit(solution)/shard_map/input_back/pallas_call | solution.py:1667
  658.1 9.4 %convert_element_type.41 = f32[512,6144]{1,0:T(8,128)} convert(bf16[512,6144]{1,0:T(8,128)(2,1)} %get-tuple-element.66) | non-fusion elementwise | flops 3145728 | bytes 18874368 | tf_op jit(solution)/shard_map/convert_element_type | solution.py:1947
  668.0 2.7 convert_element_type.42
  670.7 13.0 %convert_element_type.43 = f32[512,11264]{1,0:T(8,128)} convert(bf16[512,11264]{1,0:T(8,128)(2,1)} %get-tuple-element.69) | non-fusion elementwise | flops 5767168 | bytes 34603008 | tf_op jit(solution)/shard_map/convert_element_type | solution.py:1947
  683.7 6.0 convert_element_type.44
  690.3 2.2 add_convert_fusion
  692.5 1.1 copy.42
  (54 shorter events, 4.5 us)
Async XLA Ops:
  7.2 10.9 %copy-start.6 = (bf16[512,2048]{1,0:T(8,128)(2,1)S(1)}, bf16[512,2048]{1,0:T(8,128)(2,1)}, u32[]{:S(2)}) copy-start(bf16[512,2048]{1,0:T(8,128)(2,1)} %out_weight.1) | copy-start | bytes 6291460
  7.2 683.1 %reduce-scatter.2.cloned.1.call-start = ((), (), s32[]{:S(2)}) async-start(), calls=%async_computation.1 | async-start | bytes 3932160 | tf_op jit(solution)/shard_map/reduce_scatter | solution.py:1804
  14.9 104.3 %copy-start.2 = (f32[768,128]{1,0:T(8,128)}, f32[768,128]{1,0:T(8,128)S(1)}, u32[]{:S(2)}) copy-start(f32[768,128]{1,0:T(8,128)S(1)} %copy.29.cosine) | copy-start | bytes 1179652
  16.1 103.0 %copy-start.3 = (f32[768,128]{1,0:T(8,128)}, f32[768,128]{1,0:T(8,128)S(1)}, u32[]{:S(2)}) copy-start(f32[768,128]{1,0:T(8,128)S(1)} %copy.30.minus) | copy-start | bytes 1179652
  18.1 1.1 copy-start.7
  19.3 99.9 %copy-start.4 = (f32[768,128]{1,0:T(8,128)}, f32[768,128]{1,0:T(8,128)S(1)}, u32[]{:S(2)}) copy-start(f32[768,128]{1,0:T(8,128)S(1)} %copy.31.plus) | copy-start | bytes 1179652
  120.0 88.1 %copy-start.1 = (s32[768,128]{1,0:T(8,128)}, s32[768,128]{1,0:T(8,128)S(1)}, u32[]{:S(2)}) copy-start(s32[768,128]{1,0:T(8,128)S(1)} %broadcast_in_dim.13.seg_rows) | copy-start | bytes 1179652
  120.0 1.8 copy-start
  121.8 86.2 %copy-start.5 = (s32[8,768]{1,0:T(8,128)}, s32[8,768]{1,0:T(8,128)S(1)}, u32[]{:S(2)}) copy-start(s32[8,768]{1,0:T(8,128)S(1)} %broadcast_in_dim.14.seg_columns) | copy-start | bytes 73732
  208.0 0.7 copy-start.8
  658.0 9.4 %copy-start.12 = (f32[8,512]{1,0:T(8,128)S(1)}, f32[8,512]{1,0:T(8,128)}, u32[]{:S(2)}) copy-start(f32[8,512]{1,0:T(8,128)} %get-tuple-element.67) | copy-start | bytes 49156
  658.0 10.0 %copy-start.9 = (bf16[512,2048]{1,0:T(8,128)(2,1)S(1)}, bf16[512,2048]{1,0:T(8,128)(2,1)}, u32[]{:S(2)}) copy-start(bf16[512,2048]{1,0:T(8,128)(2,1)} %get-tuple-element.68) | copy-start | bytes 6291460
  668.0 15.6 %slice-start = ((s8[5767168]{0:T(1024)(128)(4,1)}), s8[4194304]{0:T(1024)(128)(4,1)S(1)}, s32[]{:S(2)}) async-start(s8[5767168]{0:T(1024)(128)(4,1)} %bitcast.14), calls=%async_computation.2 | async-start | bytes 8388608
  670.7 13.0 %slice-start.1 = ((s8[5767168]{0:T(1024)(128)(4,1)}), s8[1572864]{0:T(1024)(128)(4,1)S(1)}, s32[]{:S(2)}) async-start(s8[5767168]{0:T(1024)(128)(4,1)} %bitcast.14), calls=%async_computation.3 | async-start | bytes 3145728
  683.7 6.6 copy-start.10
  689.7 2.8 copy-start.11
Sparse Core Ops, SparseCore 0:
  273.5 104.4 reduce-scatter.1

commit v5 on v4

--- a/solution.py
+++ b/solution.py
@@ -20,19 +20,20 @@
 
 
 def group_layout(lengths, token_index):
-    seq_ends = jnp.cumsum(lengths)
-    passed = (token_index[:, None] >= seq_ends[None, :]).astype(jnp.int32)
-    segment = jnp.sum(passed, axis=1)
-    position = token_index - jnp.sum(passed * lengths[None, :], axis=1)
+    segment = jnp.zeros_like(token_index)
+    position = token_index
+    end = jnp.int32(0)
+    for i in range(lengths.shape[0]):
+        end = end + lengths[i]
+        passed = (token_index >= end).astype(jnp.int32)
+        segment = segment + passed
+        position = position - passed * lengths[i]
     return (segment, position)
 
 
-def rope_tables(position):
-    half_rot = ROT_DIM // 2
-    frequency = jnp.exp(
-        -jnp.log(10000.0) * (2.0 * jnp.arange(half_rot, dtype=jnp.float32) / ROT_DIM)
-    )
-    angles = position.astype(jnp.float32)[:, None] * frequency[None, :]
+def rope_tables(position, index):
+    frequency = jnp.exp(-jnp.log(10000.0) * (2.0 * index.astype(jnp.float32) / ROT_DIM))
+    angles = position.astype(jnp.float32)[:, None] * frequency
     return (jnp.cos(angles), jnp.sin(angles))
 
 
@@ -1071,33 +1072,28 @@
     def local(self, o, part):
         return pltpu.make_async_copy(self.piece(o, part), self.target(o, part), self.loc.at[part])
 
-    def start(self, o):
+    def start(self, k):
+        o = lax.rem(self.z + k, self.shards)
         for part in range(self.parts):
-            @pl.when(self.z != o)
-            def _():
+            if k == 0:
+                self.local(o, part).start()
+            else:
                 self.copy(o, part).start()
 
-            @pl.when(self.z == o)
-            def _():
-                self.local(o, part).start()
-
     def arrive(self):
-        for o in range(self.shards):
+        for k in range(self.shards):
+            o = lax.rem(self.z + k, self.shards)
             for part in range(self.parts):
-                @pl.when(self.z != o)
-                def _():
+                if k == 0:
+                    self.local(o, part).wait()
+                else:
                     self.arrival(o, part).wait_recv()
 
-                @pl.when(self.z == o)
-                def _():
-                    self.local(o, part).wait()
-
     def finish(self):
-        for o in range(self.shards):
+        for k in range(1, self.shards):
+            o = lax.rem(self.z + k, self.shards)
             for part in range(self.parts):
-                @pl.when(self.z != o)
-                def _():
-                    self.copy(o, part).wait_send()
+                self.copy(o, part).wait_send()
 
 
 def owner_sems(shards, parts):
@@ -1195,17 +1191,33 @@
                     for cut in range(self.cuts):
                         self.copy(way, block, cut, self.own.at[block, self.piece(cut)]).start()
 
-    def step_on(self, far, cut):
+    def nearest(self):
+        for way in (0, 1):
+            block = 1 if way == 0 else self.shards - 2
+
+            @pl.when(self.z == (0 if way == 0 else self.shards - 1))
+            def _():
+                for cut in range(self.cuts):
+                    self.copy(way, block, cut, self.own.at[block, self.piece(cut)]).start()
+
+    def step_on(self, hop, far, cut):
         for way in (0, 1):
             block = self.shards - 1 - far if way == 0 else far
-            sends = (self.z < block) & (self.z > 0) if way == 0 else (self.z > block) & (self.z < self.shards - 1)
-
-            @pl.when(sends)
+
+            @pl.when(self.z == (hop if way == 0 else self.shards - 1 - hop))
             def _():
                 self.copy(way, block, cut).wait_recv()
                 place = self.got.at[way, block, self.piece(cut)]
                 add_rows(place, self.own.at[block, self.piece(cut)], self.step)
                 self.copy(way, block, cut).start()
+
+    def steps(self):
+        return [
+            functools.partial(self.step_on, hop, far, cut)
+            for far in range(self.shards - 2)
+            for hop in range(1, self.shards - 1 - far)
+            for cut in range(self.cuts)
+        ]
 
     def result(self, total):
         rows = self.own.shape[1]
@@ -1267,7 +1279,17 @@
 
 
 def term_product(term, chunk, left, right):
-    term[chunk] = contract_first(left[...], right[...]).astype(term.dtype)
+    term.at[chunk][...] = contract_first(left[...], right[...]).astype(jnp.bfloat16)
+
+
+def spaced(moves, steps, every):
+    moves = list(moves)
+    for i, step in enumerate(steps):
+        step()
+        if i % every == every - 1 and moves:
+            moves.pop(0)()
+    for move in moves:
+        move()
 
 
 def interleave(moves, steps):
@@ -1285,10 +1307,26 @@
     return copies
 
 
-def hidden_back_kernel(shards, slopes, weight, hidden, cotangent, normed_two, total, down_share, gate_up_share,
+def further(shards):
+    z = lax.axis_index("shard")
+    return [(k, lax.rem(z + k, shards)) for k in (*range(1, shards), 0)]
+
+
+class Chunks:
+    def __init__(self, ref, chunks):
+        self.ref, self.shape = ref, (chunks, ref.shape[0] // chunks, ref.shape[1])
+
+    @property
+    def at(self):
+        return self
+
+    def __getitem__(self, chunk):
+        return self.ref.at[pl.ds(aligned(chunk, self.shape[1]), self.shape[1])]
+
+
+def hidden_back_kernel(shards, slopes, weight, hidden, cotangent, normed_two, total, down_share, gate_up_rows,
                        s_buf, w_buf, h_buf, c_buf, n_buf, own, got, z_send, z_recv,
-                       term, core, near, last, r_send, r_recv,
-                       g_term, g_core, g_near, g_last, g_send, g_recv, loc):
+                       term, core, near, last, r_send, r_recv, g_core, g_near, g_last, g_send, g_recv, loc, *sems):
     cube = Cube()
     loads = load_all(((slopes, s_buf), (weight, w_buf), (hidden, h_buf), (cotangent, c_buf), (normed_two, n_buf)), loc)
     greet(cube.partners(shards), shards + 2)
@@ -1296,26 +1334,27 @@
     share = hidden.shape[1] // 8
     width = D // shards
     chunks, _, columns = term.shape
-    early = g_term.shape[0]
+    g_term = Chunks(w_buf, shards)
     reducer = Reducer(cube, share, term, core, near, last, r_send, r_recv)
     g_reducer = Reducer(cube, width // 8, g_term, g_core, g_near, g_last, g_send, g_recv)
+    owners = Owners(shards, 2, g_reducer.own, gate_up_rows, *sems)
     for copy in loads[:2]:
         copy.wait()
     for t in range(shards // 2):
         pair = line.pair(t)
         pair_product(own, pair, s_buf, w_buf)
         line.ready(pair)
-        if t == 0:
-            for copy in loads[2:]:
-                copy.wait()
-            for k in range(chunks):
-                term_product(term, k, h_buf, c_buf.at[:, pl.ds(k * columns, columns)])
-                reducer.start(k)
-    for k in range(chunks):
-        reducer.after_core(k)
-    for k in range(early):
-        term_product(g_term, k, n_buf.at[:, pl.ds(k * width, width)], s_buf)
+    for copy in loads[2:]:
+        copy.wait()
+
+    def down_term(k):
+        term_product(term, k, h_buf, c_buf.at[:, pl.ds(k * columns, columns)])
+        reducer.start(k)
+
+    def gate_up_term(k):
+        term_product(g_term, k, n_buf.at[:, pl.ds(aligned(k, width), width)], s_buf)
         g_reducer.start(k)
+
     keep = []
 
     def keep_down(k):
@@ -1323,26 +1362,43 @@
         copy.start()
         keep.append(copy)
 
-    def keep_gate_up(k):
-        copy = pltpu.make_async_copy(g_reducer.own(k), gate_up_share.at[k], loc.at[5 + chunks + k])
-        copy.start()
-        keep.append(copy)
-
-    steps = [functools.partial(reducer.after_near, k) for k in range(chunks)]
-    steps += [functools.partial(g_reducer.after_core, k) for k in range(early)]
-    for k in range(chunks):
-        steps += [functools.partial(reducer.after_last, k), functools.partial(keep_down, k)]
-    steps += [functools.partial(g_reducer.after_near, k) for k in range(early)]
-    for k in range(early):
-        steps += [functools.partial(g_reducer.after_last, k), functools.partial(keep_gate_up, k)]
-    moves = [functools.partial(line.step_on, far, cut) for far in range(shards - 1) for cut in range(3)]
-    interleave(moves, steps)
+    def of(call, count):
+        return [functools.partial(call, k) for k in range(count)]
+
+    turn = further(shards)
+
+    def each(call):
+        return [functools.partial(call, o) for _, o in turn]
+
+    moves = line.steps()
+
+    def down_ending(k):
+        reducer.after_last(k)
+        keep_down(k)
+
+    def g_ending(k, o):
+        g_reducer.after_last(o)
+        owners.start(k)
+
+    cores = of(reducer.after_core, chunks) + each(g_reducer.after_core)
+    nears = of(reducer.after_near, chunks) + each(g_reducer.after_near)
+    lasts = of(down_ending, chunks) + [functools.partial(g_ending, k, o) for k, o in turn]
+    g_terms = each(gate_up_term)
+    sequence = of(down_term, chunks) + cores[:2] + g_terms[:2] + nears[:1] + cores[2:3] + g_terms[2:] + nears[1:2] + lasts[:1]
+    sequence += cores[3:4] + moves[:5]
+    for i in range(2, chunks + shards):
+        sequence += nears[i : i + 1] + lasts[i - 1 : i] + cores[i + 2 : i + 3] + moves[i + 3 : i + 4]
+    sequence += lasts[-1:] + moves[chunks + shards + 3 :]
+    for step in sequence:
+        step()
     line.result(total)
     line.finish()
+    owners.arrive()
     for k in range(chunks):
         reducer.finish(k)
-    for k in range(early):
+    for k in range(shards):
         g_reducer.finish(k)
+    owners.finish()
     for copy in keep:
         copy.wait()
 
@@ -1352,7 +1408,6 @@
     rows = group // shards
     share = inner // 8
     chunks = 4
-    early = shards // 2
     width = D // shards
     low = jnp.bfloat16
     any_ = pl.BlockSpec(memory_space=pl.ANY)
@@ -1362,13 +1417,13 @@
         out_shape=[
             jax.ShapeDtypeStruct((rows, D), jnp.float32),
             jax.ShapeDtypeStruct((share, D), low),
-            jax.ShapeDtypeStruct((early, width // 8, 2 * inner), low),
+            jax.ShapeDtypeStruct((width // 8, shards * 2 * inner), low),
         ],
         in_specs=[any_] * 5,
         out_specs=[pl.BlockSpec(memory_space=pltpu.VMEM), any_, any_],
         scratch_shapes=[pltpu.VMEM(a.shape, low) for a in (slopes, weight, hidden, cotangent, normed_two)]
         + line_scratch(shards, rows, D, 3) + reducer_scratch(chunks, share, D // chunks)
-        + reducer_scratch(early, width // 8, 2 * inner) + [dma((5 + chunks + early,))],
+        + reducer_scratch(shards, width // 8, 2 * inner)[1:] + [dma((5 + chunks,))] + owner_sems(shards, 2),
         compiler_params=pltpu.CompilerParams(collective_id=6, has_side_effects=True, vmem_limit_bytes=63 * 2**20),
         name="hidden_back",
         cost_estimate=pl.CostEstimate(flops=10**10, bytes_accessed=200 * 10**6, transcendentals=0),
@@ -1389,25 +1444,21 @@
 
 
 def heads_back_kernel(shards, rows, d_normed_two, middle, cotangent, gain, out_weight, qkv, stats, seg_rows, seg_columns,
-                      cosine, minus, plus, normed_two, slopes, attended, down_share, gate_up_first,
-                      d_middle, norm_grads, d_qkv, bias_grad, gate_up_rows, out_rows, down_grad,
-                      o_buf, n_buf, s_buf, a_buf, m_low, da_own, d_attended, m_columns, d_keys, d_values,
-                      g_term, g_core, g_near, g_last, g_send, g_recv,
-                      o_term, o_core, o_near, o_last, o_send, o_recv,
-                      e_send, e_recv, loc, *sems):
+                      cosine, minus, plus, down_share, gate_up_rows,
+                      d_middle, norm_grads, d_qkv, bias_grad, m_columns, down_grad, gate_up_grad,
+                      o_buf, m_low, da_own, d_attended, d_keys, d_values, e_send, e_recv, loc, *sems):
     cube = Cube()
     z = lax.axis_index("shard")
-    loads = load_all(((out_weight, o_buf), (normed_two, n_buf), (slopes, s_buf), (attended, a_buf)), loc)
+    loads = load_all(((out_weight, o_buf),), loc)
     greet(cube.partners(shards), shards + 2)
     width = D // shards
-    share = width // 8
-    first = gate_up_first.shape[0]
-    gatherer = Gatherer(cube, down_share, down_grad, sems[0:3])
-    g_reducer = Reducer(cube, share, g_term, g_core, g_near, g_last, g_send, g_recv)
-    o_reducer = Reducer(cube, share, o_term, o_core, o_near, o_last, o_send, o_recv)
-    owners = Owners(shards, 2, lambda o: gate_up_first.at[o] if o < first else g_reducer.own(o - first), gate_up_rows, *sems[3:6])
-    o_owners = Owners(shards, 1, o_reducer.own, out_rows, *sems[6:9])
-    gatherer.start()
+    half = gate_up_rows.shape[1] // 2
+    gatherers = [Gatherer(cube, down_share, down_grad, sems[0:3])] + [
+        Gatherer(cube, gate_up_rows.at[:, pl.ds(i * half, half)], gate_up_grad.at[:, pl.ds(i * half, half)], sems[3 * i + 3 : 3 * i + 6])
+        for i in (0, 1)
+    ]
+    gatherers[0].start()
+    gatherers[1].start()
     arrays = ((da_own, d_attended), (m_low, m_columns))
 
     def move(k, o):
@@ -1421,7 +1472,7 @@
 
     def here(k, o):
         source, target = arrays[k]
-        return pltpu.make_async_copy(source.at[:, pl.ds(o * width, width)], target.at[pl.ds(o * rows, rows)], loc.at[4 + k])
+        return pltpu.make_async_copy(source.at[:, pl.ds(o * width, width)], target.at[pl.ds(o * rows, rows)], loc.at[1 + k])
 
     def begin(k, o):
         @pl.when(z != o)
@@ -1462,67 +1513,34 @@
         begin(0, o)
     for o in range(shards):
         begin(1, o)
-    loads[1].wait()
-    loads[2].wait()
-    gatherer.pass_on()
-    for k in range(shards - first):
-        at = (first + k) * width
-        term_product(g_term, k, n_buf.at[:, pl.ds(at, width)], s_buf)
-        g_reducer.start(k)
-    gatherer.pass_last()
-    for k in range(shards - first):
-        g_reducer.after_core(k)
     arrive(0)
-    for o in range(first):
-        owners.start(o)
-    steps = []
-
-    def out_term(k):
-        if k == 0:
-            loads[3].wait()
-            arrive(1)
-        term_product(o_term, k, a_buf.at[:, pl.ds(k * width, width)], m_columns)
-        o_reducer.start(k)
-
-    for k in range(shards - first):
-        steps.append(functools.partial(g_reducer.after_near, k))
-    for k in range(shards):
-        steps.append(functools.partial(out_term, k))
-    for k in range(shards):
-        steps.append(functools.partial(o_reducer.after_core, k))
-    for k in range(shards - first):
-        steps += [functools.partial(g_reducer.after_last, k), functools.partial(owners.start, first + k)]
-    for k in range(shards):
-        steps.append(functools.partial(o_reducer.after_near, k))
-    for k in range(shards):
-        steps += [functools.partial(o_reducer.after_last, k), functools.partial(o_owners.start, k)]
+    gatherers[0].pass_on()
+
+    def nothing():
+        pass
+
+    steps = [nothing, gatherers[1].pass_on, gatherers[2].start] + [nothing] * 4 + [gatherers[0].pass_last] + [nothing] * 3
+    steps += [gatherers[1].pass_last]
     attend_back_body(rows, qkv, d_attended, stats, seg_rows, seg_columns, cosine, minus, plus,
                      d_qkv, bias_grad, d_keys, d_values, steps)
     for step in steps:
         step()
-    owners.arrive()
-    o_owners.arrive()
+    gatherers[2].pass_on()
+    arrive(1)
+    gatherers[2].pass_last()
     for k in (0, 1):
         for o in range(shards):
             @pl.when(z != o)
             def _():
                 move(k, o).wait_send()
-    for k in range(shards - first):
-        g_reducer.finish(k)
-    for k in range(shards):
-        o_reducer.finish(k)
-    owners.finish()
-    o_owners.finish()
-    gatherer.finish()
+    for gatherer in gatherers:
+        gatherer.finish()
 
 
 def heads_back_call(shards, rows, d_normed_two, middle, cotangent, gain, out_weight, qkv, stats, seg_rows, seg_columns,
-                    cosine, minus, plus, normed_two, slopes, attended, down_share, gate_up_first):
+                    cosine, minus, plus, down_share, gate_up_rows):
     group = qkv.shape[0]
     width = D // shards
-    share = width // 8
-    columns = slopes.shape[1]
-    late = shards - gate_up_first.shape[0]
     vm = pl.BlockSpec(memory_space=pltpu.VMEM)
     any_ = pl.BlockSpec(memory_space=pl.ANY)
     dma = pltpu.SemaphoreType.DMA
@@ -1535,62 +1553,87 @@
             jax.ShapeDtypeStruct((16, D), f32),
             jax.ShapeDtypeStruct((group, 3 * width), low),
             jax.ShapeDtypeStruct((8, 3 * width), f32),
-            jax.ShapeDtypeStruct((share, shards * columns), low),
-            jax.ShapeDtypeStruct((share, D), low),
+            jax.ShapeDtypeStruct((group, width), low),
             jax.ShapeDtypeStruct((8 * down_share.shape[0], D), low),
+            jax.ShapeDtypeStruct((8 * gate_up_rows.shape[0], gate_up_rows.shape[1]), low),
         ],
-        in_specs=[vm] * 4 + [any_] + [vm] * 7 + [any_] * 5,
+        in_specs=[vm] * 4 + [any_] + [vm] * 7 + [any_] * 2,
         out_specs=[vm, vm, vm, vm, any_, any_, any_],
         scratch_shapes=[
-            pltpu.VMEM(out_weight.shape, low), pltpu.VMEM(normed_two.shape, low), pltpu.VMEM(slopes.shape, low),
-            pltpu.VMEM(attended.shape, low),
-            pltpu.VMEM((rows, D), low), pltpu.VMEM((rows, D), low),
-            pltpu.VMEM((group, width), low), pltpu.VMEM((group, width), low),
+            pltpu.VMEM(out_weight.shape, low), pltpu.VMEM((rows, D), low), pltpu.VMEM((rows, D), low),
+            pltpu.VMEM((group, width), low),
             pltpu.VMEM((group, width), f32), pltpu.VMEM((group, width), f32),
-        ] + reducer_scratch(late, share, columns) + reducer_scratch(shards, share, width)
-        + [dma((2, shards)), dma((2, shards)), dma((6,))] + gatherer_sems() + owner_sems(shards, 2) + owner_sems(shards, 1),
-        compiler_params=pltpu.CompilerParams(collective_id=7, has_side_effects=True, vmem_limit_bytes=63 * 2**20),
+        ] + [dma((2, shards)), dma((2, shards)), dma((3,))] + gatherer_sems() * 3,
+        compiler_params=pltpu.CompilerParams(collective_id=7, has_side_effects=True, vmem_limit_bytes=56 * 2**20),
         name="heads_back",
         cost_estimate=pl.CostEstimate(flops=10**10, bytes_accessed=200 * 10**6, transcendentals=0),
     )(d_normed_two, middle, cotangent, gain, out_weight, qkv, stats, seg_rows, seg_columns, cosine, minus, plus,
-      normed_two, slopes, attended, down_share, gate_up_first)
-
-
-def input_back_kernel(shards, slopes, weight, normed, tokens, gain, d_middle, bias_grad, norm_grads, gate_up_rows, out_rows,
-                      input_grad, small, qkv_grad, out_grad, gate_up_grad,
-                      w_buf, n_buf, total, part, part_in, own, got, z_send, z_recv,
-                      term, core, near, last, r_send, r_recv, qkv_rows, s_send, s_recv, loc, *sems):
+      down_share, gate_up_rows)
+
+
+def input_back_kernel(shards, slopes, weight, normed, attended, d_middle_columns, tokens, gain, d_middle, bias_grad, norm_grads,
+                      input_grad, small, qkv_grad, out_grad,
+                      w_buf, n_buf, a_buf, m_buf, total, part, part_in, own, got, z_send, z_recv,
+                      term, core, near, last, r_send, r_recv, o_term, o_core, o_near, o_last, o_send, o_recv,
+                      qkv_rows, out_rows, s_send, s_recv, loc, *sems):
     cube = Cube()
     z = lax.axis_index("shard")
-    loads = load_all(((weight, w_buf), (normed, n_buf)), loc)
+    loads = load_all(((attended, a_buf), (d_middle_columns, m_buf), (weight, w_buf), (normed, n_buf)), loc)
     greet(cube.partners(shards), shards + 2)
     rows = tokens.shape[0]
     width = D // shards
     share = width // 8
     line = LineSum(shards, 3, own, got, z_send, z_recv)
     reducer = Reducer(cube, share, term, core, near, last, r_send, r_recv)
+    o_reducer = Reducer(cube, share, o_term, o_core, o_near, o_last, o_send, o_recv)
     owners = Owners(shards, 3, reducer.own, qkv_rows, *sems[0:3])
-    g_gatherer = Gatherer(cube, gate_up_rows, gate_up_grad, sems[3:6])
-    o_gatherer = Gatherer(cube, out_rows, out_grad, sems[6:9])
-    gatherer = Gatherer(cube, qkv_rows, qkv_grad, sems[9:12])
-    loads[0].wait()
-    for t in range(shards // 2):
+    o_owners = Owners(shards, 1, o_reducer.own, out_rows, *sems[3:6])
+    gatherer = Gatherer(cube, qkv_rows, qkv_grad, sems[6:9])
+    o_gatherer = Gatherer(cube, out_rows, out_grad, sems[9:12])
+
+    def qkv_term(o):
+        term_product(term, o, n_buf.at[:, pl.ds(aligned(o, width), width)], slopes)
+        reducer.start(o)
+
+    def out_term(o):
+        term_product(o_term, o, a_buf.at[:, pl.ds(aligned(o, width), width)], m_buf)
+        o_reducer.start(o)
+
+    def product(t):
         pair = line.pair(t)
         pair_product(own, pair, slopes, w_buf)
-        line.ready(pair)
-        if t == 0:
-            loads[1].wait()
-            for k in range(shards):
-                term_product(term, k, n_buf.at[:, pl.ds(k * width, width)], slopes)
-                reducer.start(k)
-    steps = [functools.partial(reducer.after_core, k) for k in range(shards)]
-    steps += [g_gatherer.start, o_gatherer.start]
-    steps += [functools.partial(reducer.after_near, k) for k in range(shards)]
-    for k in range(shards):
-        steps += [functools.partial(reducer.after_last, k), functools.partial(owners.start, k)]
-    steps += [o_gatherer.pass_on, g_gatherer.pass_on]
-    moves = [functools.partial(line.step_on, far, cut) for far in range(shards - 1) for cut in range(3)]
-    interleave(moves, steps)
+        if t + 1 < shards // 2:
+            line.ready(pair)
+
+    turn = further(shards)
+
+    def each(call):
+        return [functools.partial(call, o) for _, o in turn]
+
+    def ending(red, own_, k, o):
+        red.after_last(o)
+        own_.start(k)
+
+    loads[0].wait()
+    loads[1].wait()
+    for _, o in turn:
+        out_term(o)
+    loads[2].wait()
+    moves = line.steps()
+    cores, nears = each(reducer.after_core), each(reducer.after_near)
+    lasts = [functools.partial(ending, reducer, owners, k, o) for k, o in turn]
+    terms = each(qkv_term)
+    sequence = [functools.partial(product, 0)] + each(o_reducer.after_core)
+    sequence += [functools.partial(product, t) for t in range(1, shards // 2)] + [loads[3].wait] + each(o_reducer.after_near)
+    sequence += terms[:2] + cores[:1] + terms[2:3] + cores[1:2] + terms[3:]
+    sequence += [functools.partial(ending, o_reducer, o_owners, k, o) for k, o in turn]
+    sequence += moves[:2] + nears[:1] + cores[2:3] + moves[2:4] + nears[1:2] + lasts[:1] + cores[3:] + moves[4:6]
+    for i in range(2, shards):
+        sequence += nears[i : i + 1] + lasts[i - 1 : i] + moves[i + 4 : i + 5]
+    sequence += lasts[-1:] + [line.nearest] + moves[shards + 4 :]
+    sequence += [o_owners.arrive, o_gatherer.start]
+    for step in sequence:
+        step()
     line.result(total)
     owners.arrive()
     gatherer.start()
@@ -1638,9 +1681,9 @@
         copy.start()
         copy.wait()
         small[...] += part_in[shards + i]
-    g_gatherer.pass_last()
+    o_gatherer.pass_on()
+    gatherer.pass_on()
     o_gatherer.pass_last()
-    gatherer.pass_on()
     gatherer.pass_last()
     for o in range(shards):
         @pl.when(z != o)
@@ -1649,12 +1692,14 @@
     line.finish()
     for k in range(shards):
         reducer.finish(k)
+        o_reducer.finish(k)
     owners.finish()
-    for g in (g_gatherer, o_gatherer, gatherer):
-        g.finish()
-
-
-def input_back_call(shards, slopes, weight, normed, tokens, gain, d_middle, bias_grad, norm_grads, gate_up_rows, out_rows):
+    o_owners.finish()
+    gatherer.finish()
+    o_gatherer.finish()
+
+
+def input_back_call(shards, slopes, weight, normed, attended, d_middle_columns, tokens, gain, d_middle, bias_grad, norm_grads):
     group = slopes.shape[0]
     rows = group // shards
     width = D // shards
@@ -1671,20 +1716,20 @@
             jax.ShapeDtypeStruct((8, width), f32),
             jax.ShapeDtypeStruct((width, 3 * D), low),
             jax.ShapeDtypeStruct((width, D), low),
-            jax.ShapeDtypeStruct((width, gate_up_rows.shape[1]), low),
         ],
-        in_specs=[vm, any_, any_, vm, vm, vm, vm, vm, any_, any_],
-        out_specs=[vm, vm, any_, any_, any_],
+        in_specs=[vm] + [any_] * 4 + [vm] * 5,
+        out_specs=[vm, vm, any_, any_],
         scratch_shapes=[
-            pltpu.VMEM(weight.shape, low), pltpu.VMEM(normed.shape, low), pltpu.VMEM((rows, D), f32),
+            pltpu.VMEM(weight.shape, low), pltpu.VMEM(normed.shape, low), pltpu.VMEM(attended.shape, low),
+            pltpu.VMEM(d_middle_columns.shape, low), pltpu.VMEM((rows, D), f32),
             pltpu.VMEM((shards, 8, width), f32), pltpu.VMEM((shards + 3, 8, width), f32),
-        ] + line_scratch(shards, rows, D, 3) + reducer_scratch(shards, share, 3 * width)
-        + [pltpu.VMEM((share, 3 * D), low), dma((shards + 3,)), dma((shards + 3,)), dma((2,))]
-        + owner_sems(shards, 3) + gatherer_sems() * 3,
+        ] + line_scratch(shards, rows, D, 3) + reducer_scratch(shards, share, 3 * width) + reducer_scratch(shards, share, width)
+        + [pltpu.VMEM((share, 3 * D), low), pltpu.VMEM((share, D), low), dma((shards + 3,)), dma((shards + 3,)), dma((4,))]
+        + owner_sems(shards, 3) + owner_sems(shards, 1) + gatherer_sems() * 2,
         compiler_params=pltpu.CompilerParams(collective_id=8, has_side_effects=True, vmem_limit_bytes=60 * 2**20),
         name="input_back",
         cost_estimate=pl.CostEstimate(flops=10**10, bytes_accessed=200 * 10**6, transcendentals=0),
-    )(slopes, weight, normed, tokens, gain, d_middle, bias_grad, norm_grads, gate_up_rows, out_rows)
+    )(slopes, weight, normed, attended, d_middle_columns, tokens, gain, d_middle, bias_grad, norm_grads)
 
 
 def swap_pieces(pieces):
@@ -1801,16 +1846,17 @@
     middle, normed_two, hidden, slopes, group_cotangent, down_part = hidden_call(
         shards, attended, all_tokens, weight_out, weight_gate_up, down_weight, cotangent, gain_two, shift_two
     )
+    d_normed_two, down_share, gate_up_rows = hidden_back_call(
+        shards, slopes, weight_gate_up, hidden, group_cotangent.reshape(shards * rows, D), normed_two
+    )
+    down_part, d_normed_two = lax.optimization_barrier((down_part, d_normed_two))
     down_own = lax.psum_scatter(down_part, "shard", scatter_dimension=0, tiled=True)
-    d_normed_two, down_share, gate_up_first = hidden_back_call(
-        shards, slopes, weight_gate_up, hidden, group_cotangent.reshape(shards * rows, D), normed_two
-    )
-    d_middle, norm_grads, d_qkv, bias_grad, gate_up_rows, out_rows, down_grad = heads_back_call(
+    d_middle, norm_grads, d_qkv, bias_grad, d_middle_columns, down_grad, gate_up_grad = heads_back_call(
         shards, rows, d_normed_two, middle, cotangent, gain_two, weight_out, qkv, stats, seg_rows, seg_columns,
-        cosine, minus, plus, normed_two, slopes, attended, down_share, gate_up_first,
-    )
-    input_grad, small, qkv_grad, out_grad, gate_up_grad = input_back_call(
-        shards, d_qkv, weight_qkv, normed, tokens, gain_one, d_middle, bias_grad, norm_grads, gate_up_rows, out_rows
+        cosine, minus, plus, down_share, gate_up_rows,
+    )
+    input_grad, small, qkv_grad, out_grad = input_back_call(
+        shards, d_qkv, weight_qkv, normed, attended, d_middle_columns, tokens, gain_one, d_middle, bias_grad, norm_grads
     )
     mixed = (middle + down_own.astype(f32)).astype(low)
     return mixed, input_grad, small, (qkv_grad, out_grad, gate_up_grad, down_grad)
@@ -1918,23 +1964,22 @@
     f32 = jnp.float32
     low = jnp.bfloat16
 
-    index = jnp.arange(group_rows, dtype=jnp.int32)
-    segment, position = group_layout(seq_lengths[0], index)
+    segment, position = group_layout(seq_lengths[0], jnp.arange(group_rows, dtype=jnp.int32))
     seg_rows = jnp.broadcast_to(segment[:, None], (group_rows, 128))
     seg_columns = jnp.broadcast_to(segment[None, :], (8, group_rows))
-    cosine, sine_value = rope_tables(position)
-    half_rot = ROT_DIM // 2
-    rest = HEAD_DIM - ROT_DIM
-    none = jnp.zeros((group_rows, half_rot), f32)
-    empty = jnp.zeros((group_rows, rest), f32)
-    cosine = jnp.tile(jnp.concatenate([cosine, cosine, empty + 1.0], axis=1), (1, 2))
-    minus = jnp.tile(jnp.concatenate([-sine_value, none, empty], axis=1), (1, 2))
-    plus = jnp.tile(jnp.concatenate([none, sine_value, empty], axis=1), (1, 2))
-
-    vectors = jnp.concatenate(
-        [qkv_bias, norm1_gain, norm1_shift, norm2_gain, norm2_shift, jnp.zeros((width,), low)]
-    )
-    vectors = vectors.astype(f32).reshape(8, width)
+    lane = jnp.arange(128, dtype=jnp.int32)[None, :] % HEAD_DIM
+    cosine, sine_value = rope_tables(position, lane % (ROT_DIM // 2))
+    cosine = jnp.where(lane < ROT_DIM, cosine, 1.0)
+    minus = jnp.where(lane < ROT_DIM // 2, -sine_value, 0.0)
+    plus = jnp.where((lane >= ROT_DIM // 2) & (lane < ROT_DIM), sine_value, 0.0)
+
+    def rows_at(vector, first):
+        block = vector.astype(f32).reshape(-1, width)
+        return jnp.pad(block, ((first, 8 - first - block.shape[0]), (0, 0)))
+
+    vectors = rows_at(qkv_bias, 0)
+    for i, vector in enumerate((norm1_gain, norm1_shift, norm2_gain, norm2_shift)):
+        vectors = vectors + rows_at(vector, 3 + i)
     weights = (qkv_weight, out_weight, gate_up_weight, down_weight)
     tables = (seg_rows, seg_columns, cosine, minus, plus)
     if copies == 8:

time: 707 us -> 663 us (0.938)
  Pallas kernels: 635 us -> 590 us
    pallas_call x1, Pallas kernels: 162 us -> 125 us  [input_back_call(): pl.pallas_call(functools.partial(input_back_kernel, shards), out_shape=[j...]
  transfers between devices with their start and end apart: 1 -> 1, of which waited for: 0 -> 0; matrix products, arithmetic and copies ran while one was open for 5% -> 5% of each run, Pallas kernels for 55% -> 35%
where the time goes in v5:
time: 663 us; the launch traced here: 657 us
  Pallas kernels  590 us (89%)
  other arithmetic  36.7 us (6%)
  between operations  16.4 us (2%)
  local copies, waits for them, and re-layouts  13.6 us (2%)
    pallas_call x1, Pallas kernels, input_back_call(): pl.pallas_call(functools.partial(input_back_kernel, shards), out_shape=[j...  125 us
    pallas_call x1, Pallas kernels, hidden_back_call(): pl.pallas_call(functools.partial(hidden_back_kernel, shards), out_shape=[...  109 us
    pallas_call x1, Pallas kernels, heads_back_call(): pl.pallas_call(functools.partial(heads_back_kernel, shards, rows), out_sh...  105 us
    pallas_call x1, Pallas kernels, start_call(): pl.pallas_call(functools.partial(start_kernel, shards), out_shape=[jax.Sh...  99.9 us
    pallas_call x1, Pallas kernels, attend_spread_call(): pl.pallas_call(functools.partial(attend_spread_kernel, shards, rows), out...  86.2 us
    pallas_call x1, Pallas kernels, hidden_call(): pl.pallas_call(functools.partial(hidden_kernel, shards), out_shape=[jax.S...  64.7 us
    convert_element_type x4, other arithmetic, on_device(): out_dtype = tuple((grad.astype(f32) for grad in grads))  31 us
  transfers between devices with their start and end apart: 1, of which 0 were waited for; matrix products, arithmetic and copies ran while one was open for 5% of the time, Pallas kernels for 35%

profile of v5, /device:TPU:9, one launch (start us, length us, event | category | flops | bytes accessed | tf_op | source)
XLA Modules:
  0.0 657.0 jit_solution(15861995952761931758)
XLA Ops:
  7.3 0.7 reshape.147
  7.9 0.7 reshape.146
  8.6 0.7 reshape.145
  9.3 0.7 reshape.144
  10.0 0.7 reshape.143
  10.7 1.4 fusion.10
  14.0 1.9 convert_add_fusion.1
  16.0 1.5 fusion
  17.5 2.0 copy-done.6
  19.5 1.1 copy-done.7
  20.6 99.9 %start.1 = (bf16[4,192,2048]{2,1,0:T(8,128)(2,1)}, f32[4,8,512]{2,1,0:T(8,128)S(1)}, bf16[768,2048]{1,0:T(8,128)(2,1)}, bf16[768,1536]{1,0:T(8,128)(2,1)}, bf16[...) custom-call(bf16[192,2048]{1,0:T(8,128)(2,1)S(1)} %copy-done.7, f32[8,512]{1,0:T(8,128)S(1)} %convert_add_fusion.vectors, ...), custom_call_target="tpu_custom_call" | custom-call | flops 4831838208 | bytes 150000000 | tf_op jit(solution)/shard_map/start/pallas_call | solution.py:401
  121.4 1.8 copy-done
  123.2 86.2 %attend_spread.1 = (bf16[768,2048]{1,0:T(8,128)(2,1)}, f32[768,128]{1,0:T(8,128)S(1)}, bf16[2048,2816]{1,0:T(8,128)(2,1)}) custom-call(bf16[768,1536]{1,0:T(8,128)(2,1)S(1)} %copy-done, s32[768,128]{1,0:T(8,128)S(1)} %broadcast_in_dim.45.seg_rows, s32[8,768]{1,0:T(8,128)S(1)} %broadcast_in_dim.46.seg_columns, bf16[512,11264]{1,0:T(8,128)(2,1)} %gate_up.1), custom_call_target="tpu_custom_call" | custom-call | flops 1000000000 | bytes 150000000 | tf_op jit(solution)/shard_map/attend_spread/pallas_call | solution.py:482
  209.4 0.7 copy-done.8
  210.2 64.7 %hidden.1 = (f32[192,2048]{1,0:T(8,128)}, bf16[768,2048]{1,0:T(8,128)(2,1)}, bf16[768,1408]{1,0:T(8,128)(2,1)}, bf16[768,2816]{1,0:T(8,128)(2,1)}, bf16[4,192,20...) custom-call(bf16[768,2048]{1,0:T(8,128)(2,1)} %get-tuple-element.43.attended, ...), custom_call_target="tpu_custom_call" | custom-call | flops 24000000000 | bytes 150000000 | tf_op jit(solution)/shard_map/hidden/pallas_call | solution.py:608
  274.9 109.2 %hidden_back.1 = (f32[192,2048]{1,0:T(8,128)}, bf16[176,2048]{1,0:T(8,128)(2,1)}, bf16[64,11264]{1,0:T(8,128)(2,1)}) custom-call(bf16[768,2816]{1,0:T(8,128)(2,1)} %get-tuple-element.50.slopes, bf16[2048,2816]{1,0:T(8,128)(2,1)} %get-tuple-element.46.gate_up_weight.weight, bf16[768,1408]{1,0:T(8,128)(2,1)} %get-tuple-element.51.hidden, ...), custom_call_target="tpu_custom_call" | custom-call | flops 10000000000 | bytes 200000000 | tf_op jit(solution)/shard_map/hidden_back/pallas_call | solution.py:1415
  384.2 105.2 %heads_back.1 = (f32[192,2048]{1,0:T(8,128)}, f32[16,2048]{1,0:T(8,128)}, bf16[768,1536]{1,0:T(8,128)(2,1)}, f32[8,1536]{1,0:T(8,128)}, bf16[768,512]{1,0:T(8,12...) custom-call(f32[192,2048]{1,0:T(8,128)} %get-tuple-element.56.d_normed_two, ...), custom_call_target="tpu_custom_call" | custom-call | flops 10000000000 | bytes 200000000 | tf_op jit(solution)/shard_map/heads_back/pallas_call | solution.py:1549
  489.3 125.0 %input_back.1 = (f32[192,2048]{1,0:T(8,128)}, f32[8,512]{1,0:T(8,128)}, bf16[512,6144]{1,0:T(8,128)(2,1)}, bf16[512,2048]{1,0:T(8,128)(2,1)}) custom-call(bf16[768,1536]{1,0:T(8,128)(2,1)} %get-tuple-element.60.slopes, bf16[2048,1536]{1,0:T(8,128)(2,1)} %get-tuple-element.61.weight, bf16[768,2048]{1,0:T(8,128)(2,1)} %get-tuple-element.62.normed, ...), custom_call_target="tpu_custom_call" | custom-call | flops 10000000000 | bytes 200000000 | tf_op jit(solution)/shard_map/input_back/pallas_call | solution.py:1712
  614.4 9.4 %convert_element_type.88 = f32[512,6144]{1,0:T(8,128)} convert(bf16[512,6144]{1,0:T(8,128)(2,1)} %get-tuple-element.68) | non-fusion elementwise | flops 3145728 | bytes 18874368 | tf_op jit(solution)/shard_map/convert_element_type | solution.py:1992
  624.4 2.7 convert_element_type.89
  627.1 13.0 %convert_element_type.90 = f32[512,11264]{1,0:T(8,128)} convert(bf16[512,11264]{1,0:T(8,128)(2,1)} %get-tuple-element.71) | non-fusion elementwise | flops 5767168 | bytes 34603008 | tf_op jit(solution)/shard_map/convert_element_type | solution.py:1992
  640.0 6.0 convert_element_type.91
  646.6 2.2 add_convert_fusion
  648.8 1.1 copy.24
  (40 shorter events, 2.2 us)
Async XLA Ops:
  7.2 639.5 %reduce-scatter.2.cloned.1.call-start = ((), (), s32[]{:S(2)}) async-start(), calls=%async_computation.1 | async-start | bytes 3932160 | tf_op jit(solution)/shard_map/reduce_scatter | solution.py:1853
  17.5 103.1 %copy-start.2 = (f32[768,128]{1,0:T(8,128)}, f32[768,128]{1,0:T(8,128)S(1)}, u32[]{:S(2)}) copy-start(f32[768,128]{1,0:T(8,128)S(1)} %get-tuple-element.80.plus) | copy-start | bytes 1179652
  17.5 103.1 %copy-start.3 = (f32[768,128]{1,0:T(8,128)}, f32[768,128]{1,0:T(8,128)S(1)}, u32[]{:S(2)}) copy-start(f32[768,128]{1,0:T(8,128)S(1)} %get-tuple-element.81.minus) | copy-start | bytes 1179652
  17.5 103.1 %copy-start.4 = (f32[768,128]{1,0:T(8,128)}, f32[768,128]{1,0:T(8,128)S(1)}, u32[]{:S(2)}) copy-start(f32[768,128]{1,0:T(8,128)S(1)} %get-tuple-element.82.cosine) | copy-start | bytes 1179652
  17.5 2.0 copy-start.6
  19.5 1.1 copy-start.7
  121.4 88.0 %copy-start.1 = (s32[768,128]{1,0:T(8,128)}, s32[768,128]{1,0:T(8,128)S(1)}, u32[]{:S(2)}) copy-start(s32[768,128]{1,0:T(8,128)S(1)} %broadcast_in_dim.45.seg_rows) | copy-start | bytes 1179652
  121.4 1.8 copy-start
  123.2 86.2 %copy-start.5 = (s32[8,768]{1,0:T(8,128)}, s32[8,768]{1,0:T(8,128)S(1)}, u32[]{:S(2)}) copy-start(s32[8,768]{1,0:T(8,128)S(1)} %broadcast_in_dim.46.seg_columns) | copy-start | bytes 73732
  209.4 0.7 copy-start.8
  614.4 9.4 %copy-start.12 = (f32[8,512]{1,0:T(8,128)S(1)}, f32[8,512]{1,0:T(8,128)}, u32[]{:S(2)}) copy-start(f32[8,512]{1,0:T(8,128)} %get-tuple-element.69) | copy-start | bytes 49156
  614.4 10.0 %copy-start.9 = (bf16[512,2048]{1,0:T(8,128)(2,1)S(1)}, bf16[512,2048]{1,0:T(8,128)(2,1)}, u32[]{:S(2)}) copy-start(bf16[512,2048]{1,0:T(8,128)(2,1)} %get-tuple-element.70) | copy-start | bytes 6291460
  624.4 15.6 %slice-start = ((s8[5767168]{0:T(1024)(128)(4,1)}), s8[4194304]{0:T(1024)(128)(4,1)S(1)}, s32[]{:S(2)}) async-start(s8[5767168]{0:T(1024)(128)(4,1)} %bitcast.11), calls=%async_computation.2 | async-start | bytes 8388608
  627.1 13.0 %slice-start.1 = ((s8[5767168]{0:T(1024)(128)(4,1)}), s8[1572864]{0:T(1024)(128)(4,1)S(1)}, s32[]{:S(2)}) async-start(s8[5767168]{0:T(1024)(128)(4,1)} %bitcast.11), calls=%async_computation.3 | async-start | bytes 3145728
  640.0 6.6 %copy-start.10 = (f32[192,2048]{1,0:T(8,128)S(1)}, f32[192,2048]{1,0:T(8,128)}, u32[]{:S(2)}) copy-start(f32[192,2048]{1,0:T(8,128)} %get-tuple-element.48.middle) | copy-start | bytes 4718596
  646.0 2.8 copy-start.11
Sparse Core Ops, SparseCore 0:
  384.3 95.7 reduce-scatter.1

commit v6 on v5

--- a/solution.py
+++ b/solution.py
@@ -419,7 +419,7 @@
         ] + line_sems(shards, 1) + [dma((shards,)), dma((shards,)), dma((7, shards))]
         + spread_sems(shards, 3) + spread_sems(shards, 1),
         compiler_params=pltpu.CompilerParams(
-            collective_id=1, has_side_effects=True, vmem_limit_bytes=48 * 2**20
+            collective_id=1, has_side_effects=True, vmem_limit_bytes=62 * 2**20
         ),
         name="start",
         cost_estimate=pl.CostEstimate(flops=2 * group * D * width, bytes_accessed=150 * 10**6, transcendentals=0),
@@ -1634,9 +1634,9 @@
     sequence += [o_owners.arrive, o_gatherer.start]
     for step in sequence:
         step()
-    line.result(total)
     owners.arrive()
     gatherer.start()
+    line.result(total)
 
     part[...] = jnp.zeros_like(part)
 
@@ -1677,12 +1677,17 @@
             small[...] += part_in[o]
     sums = [remote(small, part_in.at[shards + i], s_send.at[shards + i], s_recv.at[shards + i], device)
             for i, device in enumerate((cube.to_core, cube.to_x, cube.to_y))]
-    for i, copy in enumerate(sums):
-        copy.start()
-        copy.wait()
+
+    def add_small(i):
+        sums[i].start()
+        sums[i].wait()
         small[...] += part_in[shards + i]
+
+    add_small(0)
     o_gatherer.pass_on()
     gatherer.pass_on()
+    add_small(1)
+    add_small(2)
     o_gatherer.pass_last()
     gatherer.pass_last()
     for o in range(shards):
@@ -1849,12 +1854,19 @@
     d_normed_two, down_share, gate_up_rows = hidden_back_call(
         shards, slopes, weight_gate_up, hidden, group_cotangent.reshape(shards * rows, D), normed_two
     )
-    down_part, d_normed_two = lax.optimization_barrier((down_part, d_normed_two))
-    down_own = lax.psum_scatter(down_part, "shard", scatter_dimension=0, tiled=True)
+    down_parts = down_part[:, : D // 2], down_part[:, D // 2 :]
+
+    def sum_half(half):
+        return lax.psum_scatter(half, "shard", scatter_dimension=0, tiled=True)
+
+    first_half, d_normed_two = lax.optimization_barrier((down_parts[0], d_normed_two))
+    first_half = sum_half(first_half)
     d_middle, norm_grads, d_qkv, bias_grad, d_middle_columns, down_grad, gate_up_grad = heads_back_call(
         shards, rows, d_normed_two, middle, cotangent, gain_two, weight_out, qkv, stats, seg_rows, seg_columns,
         cosine, minus, plus, down_share, gate_up_rows,
     )
+    second_half, d_qkv = lax.optimization_barrier((down_parts[1], d_qkv))
+    down_own = jnp.concatenate([first_half, sum_half(second_half)], axis=1)
     input_grad, small, qkv_grad, out_grad = input_back_call(
         shards, d_qkv, weight_qkv, normed, attended, d_middle_columns, tokens, gain_one, d_middle, bias_grad, norm_grads
     )
@@ -1973,13 +1985,13 @@
     minus = jnp.where(lane < ROT_DIM // 2, -sine_value, 0.0)
     plus = jnp.where((lane >= ROT_DIM // 2) & (lane < ROT_DIM), sine_value, 0.0)
 
-    def rows_at(vector, first):
-        block = vector.astype(f32).reshape(-1, width)
-        return jnp.pad(block, ((first, 8 - first - block.shape[0]), (0, 0)))
-
-    vectors = rows_at(qkv_bias, 0)
-    for i, vector in enumerate((norm1_gain, norm1_shift, norm2_gain, norm2_shift)):
-        vectors = vectors + rows_at(vector, 3 + i)
+    vectors = jnp.zeros((8 * width,), f32)
+    at = 0
+    for vector in (qkv_bias, norm1_gain, norm1_shift, norm2_gain, norm2_shift):
+        after = 8 * width - at - vector.shape[0]
+        vectors = vectors + jnp.pad(vector.astype(f32), (at, after))
+        at += vector.shape[0]
+    vectors = vectors.reshape(8, width)
     weights = (qkv_weight, out_weight, gate_up_weight, down_weight)
     tables = (seg_rows, seg_columns, cosine, minus, plus)
     if copies == 8:

time: 663 us -> 682 us (1.029)
  Pallas kernels: 590 us -> 606 us
    pallas_call x1, Pallas kernels: 125 us -> 161 us  [input_back_call(): pl.pallas_call(functools.partial(input_back_kernel, shards), out_shape=[j...]
    pallas_call x1, Pallas kernels: 105 us -> 84.4 us  [heads_back_call(): pl.pallas_call(functools.partial(heads_back_kernel, shards, rows), out_sh...]
  transfers between devices with their start and end apart: 1 -> 2, of which waited for: 0 -> 0; matrix products, arithmetic and copies ran while one was open for 5% -> 5% of each run, Pallas kernels for 35% -> 24%
where the time goes in v6:
time: 682 us; the launch traced here: 674 us
  Pallas kernels  606 us (89%)
  other arithmetic  38.5 us (6%)
  between operations  16.3 us (2%)
  local copies, waits for them, and re-layouts  12.5 us (2%)
    pallas_call x1, Pallas kernels, input_back_call(): pl.pallas_call(functools.partial(input_back_kernel, shards), out_shape=[j...  161 us
    pallas_call x1, Pallas kernels, hidden_back_call(): pl.pallas_call(functools.partial(hidden_back_kernel, shards), out_shape=[...  109 us
    pallas_call x1, Pallas kernels, start_call(): pl.pallas_call(functools.partial(start_kernel, shards), out_shape=[jax.Sh...  101 us
    pallas_call x1, Pallas kernels, attend_spread_call(): pl.pallas_call(functools.partial(attend_spread_kernel, shards, rows), out...  86.2 us
    pallas_call x1, Pallas kernels, heads_back_call(): pl.pallas_call(functools.partial(heads_back_kernel, shards, rows), out_sh...  84.4 us
    pallas_call x1, Pallas kernels, hidden_call(): pl.pallas_call(functools.partial(hidden_kernel, shards), out_shape=[jax.S...  64.7 us
    convert_element_type x4, other arithmetic, on_device(): out_dtype = tuple((grad.astype(f32) for grad in grads))  31 us
  transfers between devices with their start and end apart: 2, of which 0 were waited for; matrix products, arithmetic and copies ran while one was open for 5% of the time, Pallas kernels for 24%

profile of v6, /device:TPU:9, one launch (start us, length us, event | category | flops | bytes accessed | tf_op | source)
XLA Modules:
  0.0 674.4 jit_solution(8244621139362223340)
XLA Ops:
  7.3 0.8 convert_add_fusion
  8.0 0.6 reshape.126.vectors
  8.6 1.4 fusion.11
  11.9 1.9 convert_add_fusion.1
  13.9 2.6 fusion
  16.5 101.3 %start.1 = (bf16[4,192,2048]{2,1,0:T(8,128)(2,1)}, f32[4,8,512]{2,1,0:T(8,128)}, bf16[768,2048]{1,0:T(8,128)(2,1)}, bf16[768,1536]{1,0:T(8,128)(2,1)}, bf16[2048...) custom-call(bf16[192,2048]{1,0:T(8,128)(2,1)} %tokens.3, f32[8,512]{1,0:T(8,128)} %reshape.126.vectors, ...), custom_call_target="tpu_custom_call" | custom-call | flops 4831838208 | bytes 150000000 | tf_op jit(solution)/shard_map/start/pallas_call | solution.py:401
  117.8 1.6 fusion.9
  119.6 1.8 copy-done
  121.4 86.2 %attend_spread.1 = (bf16[768,2048]{1,0:T(8,128)(2,1)}, f32[768,128]{1,0:T(8,128)S(1)}, bf16[2048,2816]{1,0:T(8,128)(2,1)}) custom-call(bf16[768,1536]{1,0:T(8,128)(2,1)S(1)} %copy-done, s32[768,128]{1,0:T(8,128)S(1)} %broadcast_in_dim.45.seg_rows, s32[8,768]{1,0:T(8,128)S(1)} %broadcast_in_dim.46.seg_columns, bf16[512,11264]{1,0:T(8,128)(2,1)} %gate_up.1), custom_call_target="tpu_custom_call" | custom-call | flops 1000000000 | bytes 150000000 | tf_op jit(solution)/shard_map/attend_spread/pallas_call | solution.py:482
  207.6 0.7 copy-done.3
  208.3 64.7 %hidden.1 = (f32[192,2048]{1,0:T(8,128)}, bf16[768,2048]{1,0:T(8,128)(2,1)}, bf16[768,1408]{1,0:T(8,128)(2,1)}, bf16[768,2816]{1,0:T(8,128)(2,1)}, bf16[4,192,20...) custom-call(bf16[768,2048]{1,0:T(8,128)(2,1)} %get-tuple-element.45.attended, ...), custom_call_target="tpu_custom_call" | custom-call | flops 24000000000 | bytes 150000000 | tf_op jit(solution)/shard_map/hidden/pallas_call | solution.py:608
  273.0 3.9 fusion.8
  276.9 109.1 %hidden_back.1 = (f32[192,2048]{1,0:T(8,128)}, bf16[176,2048]{1,0:T(8,128)(2,1)}, bf16[64,11264]{1,0:T(8,128)(2,1)}) custom-call(bf16[768,2816]{1,0:T(8,128)(2,1)} %get-tuple-element.52.slopes, bf16[2048,2816]{1,0:T(8,128)(2,1)} %get-tuple-element.48.gate_up_weight.weight, bf16[768,1408]{1,0:T(8,128)(2,1)} %get-tuple-element.53.hidden, ...), custom_call_target="tpu_custom_call" | custom-call | flops 10000000000 | bytes 200000000 | tf_op jit(solution)/shard_map/hidden_back/pallas_call | solution.py:1415
  386.1 84.4 %heads_back.1 = (f32[192,2048]{1,0:T(8,128)}, f32[16,2048]{1,0:T(8,128)}, bf16[768,1536]{1,0:T(8,128)(2,1)}, f32[8,1536]{1,0:T(8,128)}, bf16[768,512]{1,0:T(8,12...) custom-call(f32[192,2048]{1,0:T(8,128)} %get-tuple-element.58.d_normed_two, ...), custom_call_target="tpu_custom_call" | custom-call | flops 10000000000 | bytes 200000000 | tf_op jit(solution)/shard_map/heads_back/pallas_call | solution.py:1549
  470.5 0.7 reduce-scatter.3.cloned.1.call-update
  471.2 160.6 %input_back.1 = (f32[192,2048]{1,0:T(8,128)}, f32[8,512]{1,0:T(8,128)}, bf16[512,6144]{1,0:T(8,128)(2,1)}, bf16[512,2048]{1,0:T(8,128)(2,1)}) custom-call(bf16[768,1536]{1,0:T(8,128)(2,1)} %get-tuple-element.64.slopes, bf16[2048,1536]{1,0:T(8,128)(2,1)} %get-tuple-element.65.weight, bf16[768,2048]{1,0:T(8,128)(2,1)} %get-tuple-element.66.normed, ...), custom_call_target="tpu_custom_call" | custom-call | flops 10000000000 | bytes 200000000 | tf_op jit(solution)/shard_map/input_back/pallas_call | solution.py:1717
  631.8 9.4 %convert_element_type.88 = f32[512,6144]{1,0:T(8,128)} convert(bf16[512,6144]{1,0:T(8,128)(2,1)} %get-tuple-element.72) | non-fusion elementwise | flops 3145728 | bytes 18874368 | tf_op jit(solution)/shard_map/convert_element_type | solution.py:2004
  641.2 0.6 slice.69
  641.8 2.7 convert_element_type.89
  644.5 13.0 %convert_element_type.90 = f32[512,11264]{1,0:T(8,128)} convert(bf16[512,11264]{1,0:T(8,128)(2,1)} %get-tuple-element.75) | non-fusion elementwise | flops 5767168 | bytes 34603008 | tf_op jit(solution)/shard_map/convert_element_type | solution.py:2004
  657.4 6.0 convert_element_type.91
  663.4 0.6 fusion.10
  664.0 2.2 add_convert_fusion
  666.2 1.1 copy.24
  (30 shorter events, 0.3 us)
Async XLA Ops:
  7.2 656.9 %reduce-scatter.5.cloned.1.call-start = ((), (), s32[]{:S(2)}) async-start(), calls=%async_computation.3 | async-start | bytes 1966080 | tf_op jit(solution)/shard_map/reduce_scatter | solution.py:1860
  119.5 88.0 %copy-start.1 = (s32[768,128]{1,0:T(8,128)}, s32[768,128]{1,0:T(8,128)S(1)}, u32[]{:S(2)}) copy-start(s32[768,128]{1,0:T(8,128)S(1)} %broadcast_in_dim.45.seg_rows) | copy-start | bytes 1179652
  119.5 1.8 copy-start
  121.4 86.2 %copy-start.2 = (s32[8,768]{1,0:T(8,128)}, s32[8,768]{1,0:T(8,128)S(1)}, u32[]{:S(2)}) copy-start(s32[8,768]{1,0:T(8,128)S(1)} %broadcast_in_dim.46.seg_columns) | copy-start | bytes 73732
  207.5 0.7 copy-start.3
  470.5 193.6 %reduce-scatter.3.cloned.1.call-start = ((), (), s32[]{:S(2)}) async-start(), calls=%async_computation.2 | async-start | bytes 1966080 | tf_op jit(solution)/shard_map/reduce_scatter | solution.py:1860
  631.8 9.4 %copy-start.7 = (f32[8,512]{1,0:T(8,128)S(1)}, f32[8,512]{1,0:T(8,128)}, u32[]{:S(2)}) copy-start(f32[8,512]{1,0:T(8,128)} %get-tuple-element.73) | copy-start | bytes 49156
  631.8 10.0 %copy-start.4 = (bf16[512,2048]{1,0:T(8,128)(2,1)S(1)}, bf16[512,2048]{1,0:T(8,128)(2,1)}, u32[]{:S(2)}) copy-start(bf16[512,2048]{1,0:T(8,128)(2,1)} %get-tuple-element.74) | copy-start | bytes 6291460
  641.8 15.6 %slice-start = ((s8[5767168]{0:T(1024)(128)(4,1)}), s8[4194304]{0:T(1024)(128)(4,1)S(1)}, s32[]{:S(2)}) async-start(s8[5767168]{0:T(1024)(128)(4,1)} %bitcast.11), calls=%async_computation.4 | async-start | bytes 8388608
  644.5 13.0 %slice-start.1 = ((s8[5767168]{0:T(1024)(128)(4,1)}), s8[1572864]{0:T(1024)(128)(4,1)S(1)}, s32[]{:S(2)}) async-start(s8[5767168]{0:T(1024)(128)(4,1)} %bitcast.11), calls=%async_computation.5 | async-start | bytes 3145728
  657.4 6.6 copy-start.5
  663.4 2.8 copy-start.6
Sparse Core Ops, SparseCore 0:
  470.6 52.4 reduce-scatter.4
  525.9 63.2 reduce-scatter.2

commit v7 on v6

--- a/solution.py
+++ b/solution.py
@@ -245,6 +245,10 @@
     centered = values - jnp.mean(values, axis=-1, keepdims=True)
     spread = jnp.mean(centered * centered, axis=-1, keepdims=True)
     return (centered * lax.rsqrt(spread + norm_eps) * gain + shift).astype(jnp.bfloat16)
+
+
+def vector_row(vectors, i):
+    return jnp.concatenate([vectors[o, i : i + 1, :] for o in range(vectors.shape[0])], axis=1)
 
 
 def bias_piece(v_buf, z, t, tile, shards, per_part):
@@ -302,8 +306,7 @@
             v_arrival(o).wait_recv()
     keep_v = pltpu.make_async_copy(v_buf, all_vectors, loc.at[2, 0])
     keep_v.start()
-    gain = jnp.concatenate([v_buf[o, 3:4, :] for o in range(shards)], axis=1)
-    shift = jnp.concatenate([v_buf[o, 4:5, :] for o in range(shards)], axis=1)
+    gain, shift = vector_row(v_buf, 3), vector_row(v_buf, 4)
 
     def put(source, target, o, i):
         block = pl.ds(aligned(o, rows), rows)
@@ -498,7 +501,7 @@
     )(qkv, seg_rows, seg_columns, gate_up)
 
 
-def hidden_kernel(shards, attended, tokens, out_weight, gate_up_weight, down_weight, cotangent, gain, shift,
+def hidden_kernel(shards, attended, tokens, out_weight, gate_up_weight, down_weight, cotangent, vectors,
                   middle_own, normed_two, hidden, slopes, all_cotangent, down_part,
                   a_buf, x_buf, o_buf, g_buf, d_buf, c_buf, mid, n_buf, gu, h_buf, s_buf, c_send, c_recv, loc):
     z = lax.axis_index("shard")
@@ -506,6 +509,7 @@
     rows = cotangent.shape[0]
     group = rows * shards
     inner = h_buf.shape[1]
+    gain, shift = vector_row(vectors, 5), vector_row(vectors, 6)
     line = Line(shards, 1, cotangent, c_buf, c_send, c_recv)
     line.start(0)
     load = [pltpu.make_async_copy(source, target, loc.at[i]) for i, (source, target) in enumerate((
@@ -532,7 +536,7 @@
         @pl.loop(0, span // 32)
         def _(i):
             block = pl.ds(aligned(i, 32), 32)
-            n_buf[pl.ds(pl.multiple_of(at + i * 32, 32), 32), :] = layer_norm_rows(mid[block, :], gain[...], shift[...])
+            n_buf[pl.ds(pl.multiple_of(at + i * 32, 32), 32), :] = layer_norm_rows(mid[block, :], gain, shift)
         for k in range(2):
             @pl.when(z == 2 * part + k)
             def _():
@@ -597,7 +601,7 @@
         copy.wait()
 
 
-def hidden_call(shards, attended, tokens, out_weight, gate_up_weight, down_weight, cotangent, gain, shift):
+def hidden_call(shards, attended, tokens, out_weight, gate_up_weight, down_weight, cotangent, vectors):
     rows = cotangent.shape[0]
     group = rows * shards
     inner = down_weight.shape[0]
@@ -615,7 +619,7 @@
             jax.ShapeDtypeStruct((shards, rows, D), low),
             jax.ShapeDtypeStruct((group, D), low),
         ],
-        in_specs=[any_] * 6 + [vm, vm],
+        in_specs=[any_] * 6 + [vm],
         out_specs=[vm] + [any_] * 5,
         scratch_shapes=[
             pltpu.VMEM((group, D), low),
@@ -635,7 +639,7 @@
         ),
         name="hidden",
         cost_estimate=pl.CostEstimate(flops=24 * 10**9, bytes_accessed=150 * 10**6, transcendentals=0),
-    )(attended, tokens, out_weight, gate_up_weight, down_weight, cotangent, gain, shift)
+    )(attended, tokens, out_weight, gate_up_weight, down_weight, cotangent, vectors)
 
 
 def head_mask(even, rows):
@@ -1443,13 +1447,14 @@
     return back, unit
 
 
-def heads_back_kernel(shards, rows, d_normed_two, middle, cotangent, gain, out_weight, qkv, stats, seg_rows, seg_columns,
-                      cosine, minus, plus, down_share, gate_up_rows,
-                      d_middle, norm_grads, d_qkv, bias_grad, m_columns, down_grad, gate_up_grad,
-                      o_buf, m_low, da_own, d_attended, d_keys, d_values, e_send, e_recv, loc, *sems):
+def heads_back_kernel(shards, rows, d_normed_two, middle, cotangent, vectors, out_weight, qkv, stats, seg_rows, seg_columns,
+                      cosine, minus, plus, down_part, down_share, gate_up_rows,
+                      d_middle, norm_grads, d_qkv, bias_grad, mixed, m_columns, down_grad, gate_up_grad,
+                      o_buf, m_low, da_own, d_attended, d_keys, d_values, total, own, got, z_send, z_recv, e_send, e_recv, loc, *sems):
     cube = Cube()
     z = lax.axis_index("shard")
-    loads = load_all(((out_weight, o_buf),), loc)
+    loads = load_all(((out_weight, o_buf), (down_part, own)), loc)
+    gain = vector_row(vectors, 5)
     greet(cube.partners(shards), shards + 2)
     width = D // shards
     half = gate_up_rows.shape[1] // 2
@@ -1457,6 +1462,7 @@
         Gatherer(cube, gate_up_rows.at[:, pl.ds(i * half, half)], gate_up_grad.at[:, pl.ds(i * half, half)], sems[3 * i + 3 : 3 * i + 6])
         for i in (0, 1)
     ]
+    line = LineSum(shards, 3, own, got, z_send, z_recv)
     gatherers[0].start()
     gatherers[1].start()
     arrays = ((da_own, d_attended), (m_low, m_columns))
@@ -1472,7 +1478,7 @@
 
     def here(k, o):
         source, target = arrays[k]
-        return pltpu.make_async_copy(source.at[:, pl.ds(o * width, width)], target.at[pl.ds(o * rows, rows)], loc.at[1 + k])
+        return pltpu.make_async_copy(source.at[:, pl.ds(o * width, width)], target.at[pl.ds(o * rows, rows)], loc.at[2 + k])
 
     def begin(k, o):
         @pl.when(z != o)
@@ -1499,7 +1505,7 @@
     def _(i):
         block = pl.ds(aligned(i, 16), 16)
         slope = d_normed_two[block, :]
-        back, unit = norm_back_rows(slope, middle[block, :], gain[...])
+        back, unit = norm_back_rows(slope, middle[block, :], gain)
         value = cotangent[block, :].astype(jnp.float32) + back
         d_middle[block, :] = value
         m_low[block, :] = value.astype(jnp.bfloat16)
@@ -1511,6 +1517,9 @@
         da_own[:, o * width : (o + 1) * width] = contract_last(
             m_low[...], o_buf[o * width : (o + 1) * width, :]).astype(jnp.bfloat16)
         begin(0, o)
+    loads[1].wait()
+    for t in range(shards // 2):
+        line.ready(line.pair(t))
     for o in range(shards):
         begin(1, o)
     arrive(0)
@@ -1519,8 +1528,9 @@
     def nothing():
         pass
 
-    steps = [nothing, gatherers[1].pass_on, gatherers[2].start] + [nothing] * 4 + [gatherers[0].pass_last] + [nothing] * 3
-    steps += [gatherers[1].pass_last]
+    moves = line.steps()
+    steps = [nothing, gatherers[1].pass_on, gatherers[2].start, nothing, moves[0], nothing, gatherers[0].pass_last]
+    steps += [moves[1], nothing, moves[2], nothing] + [gatherers[1].pass_last] + moves[3:]
     attend_back_body(rows, qkv, d_attended, stats, seg_rows, seg_columns, cosine, minus, plus,
                      d_qkv, bias_grad, d_keys, d_values, steps)
     for step in steps:
@@ -1528,6 +1538,13 @@
     gatherers[2].pass_on()
     arrive(1)
     gatherers[2].pass_last()
+    line.result(total)
+
+    @pl.loop(0, rows // 16)
+    def _(i):
+        block = pl.ds(aligned(i, 16), 16)
+        mixed[block, :] = (middle[block, :] + total[block, :]).astype(mixed.dtype)
+    line.finish()
     for k in (0, 1):
         for o in range(shards):
             @pl.when(z != o)
@@ -1537,8 +1554,8 @@
         gatherer.finish()
 
 
-def heads_back_call(shards, rows, d_normed_two, middle, cotangent, gain, out_weight, qkv, stats, seg_rows, seg_columns,
-                    cosine, minus, plus, down_share, gate_up_rows):
+def heads_back_call(shards, rows, d_normed_two, middle, cotangent, vectors, out_weight, qkv, stats, seg_rows, seg_columns,
+                    cosine, minus, plus, down_part, down_share, gate_up_rows):
     group = qkv.shape[0]
     width = D // shards
     vm = pl.BlockSpec(memory_space=pltpu.VMEM)
@@ -1553,25 +1570,26 @@
             jax.ShapeDtypeStruct((16, D), f32),
             jax.ShapeDtypeStruct((group, 3 * width), low),
             jax.ShapeDtypeStruct((8, 3 * width), f32),
+            jax.ShapeDtypeStruct((rows, D), low),
             jax.ShapeDtypeStruct((group, width), low),
             jax.ShapeDtypeStruct((8 * down_share.shape[0], D), low),
             jax.ShapeDtypeStruct((8 * gate_up_rows.shape[0], gate_up_rows.shape[1]), low),
         ],
-        in_specs=[vm] * 4 + [any_] + [vm] * 7 + [any_] * 2,
-        out_specs=[vm, vm, vm, vm, any_, any_, any_],
+        in_specs=[vm] * 4 + [any_] + [vm] * 7 + [any_] * 3,
+        out_specs=[vm] * 5 + [any_] * 3,
         scratch_shapes=[
             pltpu.VMEM(out_weight.shape, low), pltpu.VMEM((rows, D), low), pltpu.VMEM((rows, D), low),
             pltpu.VMEM((group, width), low),
-            pltpu.VMEM((group, width), f32), pltpu.VMEM((group, width), f32),
-        ] + [dma((2, shards)), dma((2, shards)), dma((3,))] + gatherer_sems() * 3,
-        compiler_params=pltpu.CompilerParams(collective_id=7, has_side_effects=True, vmem_limit_bytes=56 * 2**20),
+            pltpu.VMEM((group, width), f32), pltpu.VMEM((group, width), f32), pltpu.VMEM((rows, D), f32),
+        ] + line_scratch(shards, rows, D, 3) + [dma((2, shards)), dma((2, shards)), dma((4,))] + gatherer_sems() * 3,
+        compiler_params=pltpu.CompilerParams(collective_id=7, has_side_effects=True, vmem_limit_bytes=60 * 2**20),
         name="heads_back",
         cost_estimate=pl.CostEstimate(flops=10**10, bytes_accessed=200 * 10**6, transcendentals=0),
-    )(d_normed_two, middle, cotangent, gain, out_weight, qkv, stats, seg_rows, seg_columns, cosine, minus, plus,
-      down_share, gate_up_rows)
-
-
-def input_back_kernel(shards, slopes, weight, normed, attended, d_middle_columns, tokens, gain, d_middle, bias_grad, norm_grads,
+    )(d_normed_two, middle, cotangent, vectors, out_weight, qkv, stats, seg_rows, seg_columns, cosine, minus, plus,
+      down_part, down_share, gate_up_rows)
+
+
+def input_back_kernel(shards, slopes, weight, normed, attended, d_middle_columns, tokens, vectors, d_middle, bias_grad, norm_grads,
                       input_grad, small, qkv_grad, out_grad,
                       w_buf, n_buf, a_buf, m_buf, total, part, part_in, own, got, z_send, z_recv,
                       term, core, near, last, r_send, r_recv, o_term, o_core, o_near, o_last, o_send, o_recv,
@@ -1580,6 +1598,7 @@
     z = lax.axis_index("shard")
     loads = load_all(((attended, a_buf), (d_middle_columns, m_buf), (weight, w_buf), (normed, n_buf)), loc)
     greet(cube.partners(shards), shards + 2)
+    gain = vector_row(vectors, 3)
     rows = tokens.shape[0]
     width = D // shards
     share = width // 8
@@ -1644,7 +1663,7 @@
     def _(i):
         block = pl.ds(aligned(i, 16), 16)
         slope = total[block, :]
-        back, unit = norm_back_rows(slope, tokens[block, :].astype(jnp.float32), gain[...])
+        back, unit = norm_back_rows(slope, tokens[block, :].astype(jnp.float32), gain)
         input_grad[block, :] = d_middle[block, :] + back
         ones = (slope * unit).reshape(2, 8, D).sum(axis=0).sum(axis=0, keepdims=True)
         twos = slope.reshape(2, 8, D).sum(axis=0).sum(axis=0, keepdims=True)
@@ -1704,7 +1723,7 @@
     o_gatherer.finish()
 
 
-def input_back_call(shards, slopes, weight, normed, attended, d_middle_columns, tokens, gain, d_middle, bias_grad, norm_grads):
+def input_back_call(shards, slopes, weight, normed, attended, d_middle_columns, tokens, vectors, d_middle, bias_grad, norm_grads):
     group = slopes.shape[0]
     rows = group // shards
     width = D // shards
@@ -1734,7 +1753,7 @@
         compiler_params=pltpu.CompilerParams(collective_id=8, has_side_effects=True, vmem_limit_bytes=60 * 2**20),
         name="input_back",
         cost_estimate=pl.CostEstimate(flops=10**10, bytes_accessed=200 * 10**6, transcendentals=0),
-    )(slopes, weight, normed, attended, d_middle_columns, tokens, gain, d_middle, bias_grad, norm_grads)
+    )(slopes, weight, normed, attended, d_middle_columns, tokens, vectors, d_middle, bias_grad, norm_grads)
 
 
 def swap_pieces(pieces):
@@ -1837,40 +1856,25 @@
     qkv_weight, out_weight, gate_up_weight, down_weight = weights
     seg_rows, seg_columns, cosine, minus, plus = tables
     rows = tokens.shape[0]
-    f32 = jnp.float32
-    low = jnp.bfloat16
     all_tokens, all_vectors, normed, qkv, weight_qkv, weight_out = start_call(
         shards, tokens, vectors, qkv_weight, out_weight, cosine, minus, plus
     )
-    gain_one, shift_one, gain_two, shift_two = (
-        all_vectors[:, 3 + i].reshape(1, D) for i in range(4)
-    )
     attended, stats, weight_gate_up = attend_spread_call(
         shards, rows, qkv, seg_rows, seg_columns, gate_up_weight
     )
     middle, normed_two, hidden, slopes, group_cotangent, down_part = hidden_call(
-        shards, attended, all_tokens, weight_out, weight_gate_up, down_weight, cotangent, gain_two, shift_two
+        shards, attended, all_tokens, weight_out, weight_gate_up, down_weight, cotangent, all_vectors
     )
     d_normed_two, down_share, gate_up_rows = hidden_back_call(
         shards, slopes, weight_gate_up, hidden, group_cotangent.reshape(shards * rows, D), normed_two
     )
-    down_parts = down_part[:, : D // 2], down_part[:, D // 2 :]
-
-    def sum_half(half):
-        return lax.psum_scatter(half, "shard", scatter_dimension=0, tiled=True)
-
-    first_half, d_normed_two = lax.optimization_barrier((down_parts[0], d_normed_two))
-    first_half = sum_half(first_half)
-    d_middle, norm_grads, d_qkv, bias_grad, d_middle_columns, down_grad, gate_up_grad = heads_back_call(
-        shards, rows, d_normed_two, middle, cotangent, gain_two, weight_out, qkv, stats, seg_rows, seg_columns,
-        cosine, minus, plus, down_share, gate_up_rows,
-    )
-    second_half, d_qkv = lax.optimization_barrier((down_parts[1], d_qkv))
-    down_own = jnp.concatenate([first_half, sum_half(second_half)], axis=1)
+    d_middle, norm_grads, d_qkv, bias_grad, mixed, d_middle_columns, down_grad, gate_up_grad = heads_back_call(
+        shards, rows, d_normed_two, middle, cotangent, all_vectors, weight_out, qkv, stats, seg_rows, seg_columns,
+        cosine, minus, plus, down_part.reshape(shards, rows, D), down_share, gate_up_rows,
+    )
     input_grad, small, qkv_grad, out_grad = input_back_call(
-        shards, d_qkv, weight_qkv, normed, attended, d_middle_columns, tokens, gain_one, d_middle, bias_grad, norm_grads
-    )
-    mixed = (middle + down_own.astype(f32)).astype(low)
+        shards, d_qkv, weight_qkv, normed, attended, d_middle_columns, tokens, all_vectors, d_middle, bias_grad, norm_grads
+    )
     return mixed, input_grad, small, (qkv_grad, out_grad, gate_up_grad, down_grad)
 
 

time: 682 us -> 624 us (0.915)
  Pallas kernels: 606 us -> 573 us
  between operations: 16.3 us -> 3.2 us
    pallas_call x1, Pallas kernels: 161 us -> 118 us  [input_back_call(): pl.pallas_call(functools.partial(input_back_kernel, shards), out_shape=[j...]
    pallas_call x1, Pallas kernels: 84.4 us -> 93.7 us  [heads_back_call(): pl.pallas_call(functools.partial(heads_back_kernel, shards, rows), out_sh...]
  transfers between devices with their start and end apart: 2 -> 0, of which waited for: 0 -> 0; matrix products, arithmetic and copies ran while one was open for 5% -> 0% of each run, Pallas kernels for 24% -> 0%
where the time goes in v7:
time: 624 us; the launch traced here: 617 us
  Pallas kernels  573 us (92%)
  other arithmetic  33.1 us (5%)
  local copies, waits for them, and re-layouts  7.93 us (1%)
    pallas_call x1, Pallas kernels, input_back_call(): pl.pallas_call(functools.partial(input_back_kernel, shards), out_shape=[j...  118 us
    pallas_call x1, Pallas kernels, hidden_back_call(): pl.pallas_call(functools.partial(hidden_back_kernel, shards), out_shape=[...  109 us
    pallas_call x1, Pallas kernels, start_call(): pl.pallas_call(functools.partial(start_kernel, shards), out_shape=[jax.Sh...  101 us
    pallas_call x1, Pallas kernels, heads_back_call(): pl.pallas_call(functools.partial(heads_back_kernel, shards, rows), out_sh...  93.7 us
    pallas_call x1, Pallas kernels, attend_spread_call(): pl.pallas_call(functools.partial(attend_spread_kernel, shards, rows), out...  86.2 us
    pallas_call x1, Pallas kernels, hidden_call(): pl.pallas_call(functools.partial(hidden_kernel, shards), out_shape=[jax.S...  64.8 us
    convert_element_type x4, other arithmetic, on_device(): out_dtype = tuple((grad.astype(f32) for grad in grads))  27.7 us

profile of v7, /device:TPU:9, one launch (start us, length us, event | category | flops | bytes accessed | tf_op | source)
XLA Modules:
  0.0 617.1 jit_solution(8352105556767285840)
XLA Ops:
  0.6 1.4 fusion.9
  3.9 1.9 convert_add_fusion.1
  5.9 2.6 fusion
  8.6 0.8 convert_add_fusion
  9.3 0.6 reshape.129.vectors
  9.9 101.3 %start.1 = (bf16[4,192,2048]{2,1,0:T(8,128)(2,1)}, f32[4,8,512]{2,1,0:T(8,128)}, bf16[768,2048]{1,0:T(8,128)(2,1)}, bf16[768,1536]{1,0:T(8,128)(2,1)}, bf16[2048...) custom-call(bf16[192,2048]{1,0:T(8,128)(2,1)} %tokens.3, f32[8,512]{1,0:T(8,128)} %reshape.129.vectors, ...), custom_call_target="tpu_custom_call" | custom-call | flops 4831838208 | bytes 150000000 | tf_op jit(solution)/shard_map/start/pallas_call | solution.py:404
  111.2 0.2 broadcast_in_dim.45.seg_rows
  111.4 0.0 copy-start.1
  111.4 1.8 copy-done
  113.2 86.2 %attend_spread.1 = (bf16[768,2048]{1,0:T(8,128)(2,1)}, f32[768,128]{1,0:T(8,128)S(1)}, bf16[2048,2816]{1,0:T(8,128)(2,1)}) custom-call(bf16[768,1536]{1,0:T(8,128)(2,1)S(1)} %copy-done, s32[768,128]{1,0:T(8,128)S(1)} %broadcast_in_dim.45.seg_rows, s32[8,768]{1,0:T(8,128)S(1)} %broadcast_in_dim.46.seg_columns, bf16[512,11264]{1,0:T(8,128)(2,1)} %gate_up.1), custom_call_target="tpu_custom_call" | custom-call | flops 1000000000 | bytes 150000000 | tf_op jit(solution)/shard_map/attend_spread/pallas_call | solution.py:485
  199.4 0.0 copy-start.3
  199.5 0.7 copy-done.3
  200.2 64.8 %hidden.1 = (f32[192,2048]{1,0:T(8,128)}, bf16[768,2048]{1,0:T(8,128)(2,1)}, bf16[768,1408]{1,0:T(8,128)(2,1)}, bf16[768,2816]{1,0:T(8,128)(2,1)}, bf16[4,192,20...) custom-call(bf16[768,2048]{1,0:T(8,128)(2,1)} %get-tuple-element.42.attended, ...), custom_call_target="tpu_custom_call" | custom-call | flops 24000000000 | bytes 150000000 | tf_op jit(solution)/shard_map/hidden/pallas_call | solution.py:612
  265.0 109.3 %hidden_back.1 = (f32[192,2048]{1,0:T(8,128)}, bf16[176,2048]{1,0:T(8,128)(2,1)}, bf16[64,11264]{1,0:T(8,128)(2,1)}) custom-call(bf16[768,2816]{1,0:T(8,128)(2,1)} %get-tuple-element.47.slopes, bf16[2048,2816]{1,0:T(8,128)(2,1)} %get-tuple-element.45.gate_up_weight.weight, bf16[768,1408]{1,0:T(8,128)(2,1)} %get-tuple-element.48.hidden, ...), custom_call_target="tpu_custom_call" | custom-call | flops 10000000000 | bytes 200000000 | tf_op jit(solution)/shard_map/hidden_back/pallas_call | solution.py:1419
  374.3 93.7 %heads_back.1 = (f32[192,2048]{1,0:T(8,128)}, f32[16,2048]{1,0:T(8,128)}, bf16[768,1536]{1,0:T(8,128)(2,1)}, f32[8,1536]{1,0:T(8,128)}, bf16[192,2048]{1,0:T(8,1...) custom-call(f32[192,2048]{1,0:T(8,128)} %get-tuple-element.51.d_normed_two, ...), custom_call_target="tpu_custom_call" | custom-call | flops 10000000000 | bytes 200000000 | tf_op jit(solution)/shard_map/heads_back/pallas_call | solution.py:1566
  468.0 117.7 %input_back.1 = (f32[192,2048]{1,0:T(8,128)}, f32[8,512]{1,0:T(8,128)}, bf16[512,6144]{1,0:T(8,128)(2,1)}, bf16[512,2048]{1,0:T(8,128)(2,1)}) custom-call(bf16[768,1536]{1,0:T(8,128)(2,1)} %get-tuple-element.58.slopes, bf16[2048,1536]{1,0:T(8,128)(2,1)} %get-tuple-element.59.weight, bf16[768,2048]{1,0:T(8,128)(2,1)} %get-tuple-element.60.normed, ...), custom_call_target="tpu_custom_call" | custom-call | flops 10000000000 | bytes 200000000 | tf_op jit(solution)/shard_map/input_back/pallas_call | solution.py:1736
  585.6 9.4 %convert_element_type.80 = f32[512,6144]{1,0:T(8,128)} convert(bf16[512,6144]{1,0:T(8,128)(2,1)} %get-tuple-element.66) | non-fusion elementwise | flops 3145728 | bytes 18874368 | tf_op jit(solution)/shard_map/convert_element_type | solution.py:2008
  595.0 9.8 %convert_element_type.82 = f32[512,11264]{1,0:T(8,128)} convert(bf16[512,11264]{1,0:T(8,128)(2,1)S(1)} %copy-done.4) | non-fusion elementwise | flops 5767168 | bytes 34603008 | tf_op jit(solution)/shard_map/convert_element_type | solution.py:2008
  604.8 2.5 convert_element_type.81
  607.4 6.0 convert_element_type.83
  613.4 0.6 slice.49
  614.0 0.6 fusion.8
  614.6 0.9 copy.25
  615.5 1.1 copy.26
  (24 shorter events, 0.1 us)
Async XLA Ops:
  111.4 88.1 %copy-start.1 = (s32[768,128]{1,0:T(8,128)}, s32[768,128]{1,0:T(8,128)S(1)}, u32[]{:S(2)}) copy-start(s32[768,128]{1,0:T(8,128)S(1)} %broadcast_in_dim.45.seg_rows) | copy-start | bytes 1179652
  111.4 1.8 copy-start
  113.2 86.2 %copy-start.2 = (s32[8,768]{1,0:T(8,128)}, s32[8,768]{1,0:T(8,128)S(1)}, u32[]{:S(2)}) copy-start(s32[8,768]{1,0:T(8,128)S(1)} %broadcast_in_dim.46.seg_columns) | copy-start | bytes 73732
  199.4 0.7 copy-start.3
  585.6 9.4 %copy-start.4 = (bf16[512,11264]{1,0:T(8,128)(2,1)S(1)}, bf16[512,11264]{1,0:T(8,128)(2,1)}, u32[]{:S(2)}) copy-start(bf16[512,11264]{1,0:T(8,128)(2,1)} %get-tuple-element.69) | copy-start | bytes 34603012
  595.0 12.4 %slice-start = ((s8[5767168]{0:T(1024)(128)(4,1)}), s8[4194304]{0:T(1024)(128)(4,1)S(1)}, s32[]{:S(2)}) async-start(s8[5767168]{0:T(1024)(128)(4,1)} %bitcast.9), calls=%async_computation | async-start | bytes 8388608
  595.0 9.8 %copy-start.5 = (bf16[512,2048]{1,0:T(8,128)(2,1)S(1)}, bf16[512,2048]{1,0:T(8,128)(2,1)}, u32[]{:S(2)}) copy-start(bf16[512,2048]{1,0:T(8,128)(2,1)} %get-tuple-element.68) | copy-start | bytes 6291460
  595.0 12.4 %slice-start.1 = ((s8[5767168]{0:T(1024)(128)(4,1)}), s8[1572864]{0:T(1024)(128)(4,1)S(1)}, s32[]{:S(2)}) async-start(s8[5767168]{0:T(1024)(128)(4,1)} %bitcast.9), calls=%async_computation.1 | async-start | bytes 3145728
  607.4 6.0 copy-start.8
  607.4 7.2 %copy-start.7 = (bf16[192,2048]{1,0:T(8,128)(2,1)S(1)}, bf16[192,2048]{1,0:T(8,128)(2,1)}, u32[]{:S(2)}) copy-start(bf16[192,2048]{1,0:T(8,128)(2,1)} %get-tuple-element.96) | copy-start | bytes 2359300
  607.4 8.1 %copy-start.6 = (f32[192,2048]{1,0:T(8,128)S(1)}, f32[192,2048]{1,0:T(8,128)}, u32[]{:S(2)}) copy-start(f32[192,2048]{1,0:T(8,128)} %get-tuple-element.97) | copy-start | bytes 4718596

commit v8 on v7

--- a/solution.py
+++ b/solution.py
@@ -1084,14 +1084,17 @@
             else:
                 self.copy(o, part).start()
 
+    def arrive_from(self, k):
+        o = lax.rem(self.z + k, self.shards)
+        for part in range(self.parts):
+            if k == 0:
+                self.local(o, part).wait()
+            else:
+                self.arrival(o, part).wait_recv()
+
     def arrive(self):
         for k in range(self.shards):
-            o = lax.rem(self.z + k, self.shards)
-            for part in range(self.parts):
-                if k == 0:
-                    self.local(o, part).wait()
-                else:
-                    self.arrival(o, part).wait_recv()
+            self.arrive_from(k)
 
     def finish(self):
         for k in range(1, self.shards):
@@ -1195,9 +1198,9 @@
                     for cut in range(self.cuts):
                         self.copy(way, block, cut, self.own.at[block, self.piece(cut)]).start()
 
-    def nearest(self):
+    def ends(self, i):
         for way in (0, 1):
-            block = 1 if way == 0 else self.shards - 2
+            block = self.shards - 1 - i if way == 0 else i
 
             @pl.when(self.z == (0 if way == 0 else self.shards - 1))
             def _():
@@ -1332,7 +1335,7 @@
                        s_buf, w_buf, h_buf, c_buf, n_buf, own, got, z_send, z_recv,
                        term, core, near, last, r_send, r_recv, g_core, g_near, g_last, g_send, g_recv, loc, *sems):
     cube = Cube()
-    loads = load_all(((slopes, s_buf), (weight, w_buf), (hidden, h_buf), (cotangent, c_buf), (normed_two, n_buf)), loc)
+    loads = load_all(((hidden, h_buf), (cotangent, c_buf), (slopes, s_buf), (weight, w_buf), (normed_two, n_buf)), loc)
     greet(cube.partners(shards), shards + 2)
     line = LineSum(shards, 3, own, got, z_send, z_recv)
     share = hidden.shape[1] // 8
@@ -1342,14 +1345,10 @@
     reducer = Reducer(cube, share, term, core, near, last, r_send, r_recv)
     g_reducer = Reducer(cube, width // 8, g_term, g_core, g_near, g_last, g_send, g_recv)
     owners = Owners(shards, 2, g_reducer.own, gate_up_rows, *sems)
-    for copy in loads[:2]:
-        copy.wait()
-    for t in range(shards // 2):
+    def product(t):
         pair = line.pair(t)
         pair_product(own, pair, s_buf, w_buf)
         line.ready(pair)
-    for copy in loads[2:]:
-        copy.wait()
 
     def down_term(k):
         term_product(term, k, h_buf, c_buf.at[:, pl.ds(k * columns, columns)])
@@ -1388,7 +1387,9 @@
     nears = of(reducer.after_near, chunks) + each(g_reducer.after_near)
     lasts = of(down_ending, chunks) + [functools.partial(g_ending, k, o) for k, o in turn]
     g_terms = each(gate_up_term)
-    sequence = of(down_term, chunks) + cores[:2] + g_terms[:2] + nears[:1] + cores[2:3] + g_terms[2:] + nears[1:2] + lasts[:1]
+    sequence = [copy.wait for copy in loads[:2]] + of(down_term, chunks) + [copy.wait for copy in loads[2:]]
+    sequence += [functools.partial(product, 0)] + cores[:2]
+    sequence += [functools.partial(product, t) for t in range(1, shards // 2)] + g_terms[:2] + nears[:1] + cores[2:3] + g_terms[2:] + nears[1:2] + lasts[:1]
     sequence += cores[3:4] + moves[:5]
     for i in range(2, chunks + shards):
         sequence += nears[i : i + 1] + lasts[i - 1 : i] + cores[i + 2 : i + 3] + moves[i + 3 : i + 4]
@@ -1596,8 +1597,10 @@
                       qkv_rows, out_rows, s_send, s_recv, loc, *sems):
     cube = Cube()
     z = lax.axis_index("shard")
-    loads = load_all(((attended, a_buf), (d_middle_columns, m_buf), (weight, w_buf), (normed, n_buf)), loc)
-    greet(cube.partners(shards), shards + 2)
+    loads = load_all(((normed, n_buf), (weight, w_buf), (attended, a_buf), (d_middle_columns, m_buf)), loc)
+    r = lax.axis_index("replica")
+    others = [lax.rem(r + i, 8) for i in range(1, 8)]
+    greet([((z != o), {"shard": o}) for o in range(shards)] + [(z >= 0, {"replica": o}) for o in others], shards + 6)
     gain = vector_row(vectors, 3)
     rows = tokens.shape[0]
     width = D // shards
@@ -1607,7 +1610,16 @@
     o_reducer = Reducer(cube, share, o_term, o_core, o_near, o_last, o_send, o_recv)
     owners = Owners(shards, 3, reducer.own, qkv_rows, *sems[0:3])
     o_owners = Owners(shards, 1, o_reducer.own, out_rows, *sems[3:6])
-    gatherer = Gatherer(cube, qkv_rows, qkv_grad, sems[6:9])
+    gatherers = [
+        [
+            Gatherer(
+                cube, *(ref.at[:, pl.ds(aligned(p * shards + lax.rem(z + k, shards), width), width)] for ref in (qkv_rows, qkv_grad)),
+                [sem.at[3 * k + p] for sem in sems[6:9]],
+            )
+            for p in range(3)
+        ]
+        for k in range(shards)
+    ]
     o_gatherer = Gatherer(cube, out_rows, out_grad, sems[9:12])
 
     def qkv_term(o):
@@ -1621,8 +1633,7 @@
     def product(t):
         pair = line.pair(t)
         pair_product(own, pair, slopes, w_buf)
-        if t + 1 < shards // 2:
-            line.ready(pair)
+        line.ends(t)
 
     turn = further(shards)
 
@@ -1633,28 +1644,36 @@
         red.after_last(o)
         own_.start(k)
 
-    loads[0].wait()
-    loads[1].wait()
-    for _, o in turn:
-        out_term(o)
-    loads[2].wait()
     moves = line.steps()
     cores, nears = each(reducer.after_core), each(reducer.after_near)
     lasts = [functools.partial(ending, reducer, owners, k, o) for k, o in turn]
     terms = each(qkv_term)
-    sequence = [functools.partial(product, 0)] + each(o_reducer.after_core)
-    sequence += [functools.partial(product, t) for t in range(1, shards // 2)] + [loads[3].wait] + each(o_reducer.after_near)
-    sequence += terms[:2] + cores[:1] + terms[2:3] + cores[1:2] + terms[3:]
+
+    def begin_from(i):
+        owners.arrive_from(i)
+        for g in gatherers[i]:
+            g.start()
+
+    def pass_from(i):
+        for g in gatherers[i]:
+            g.pass_on()
+
+    def pass_last_from(i):
+        for g in gatherers[i]:
+            g.pass_last()
+
+    sequence = [loads[0].wait] + terms + [loads[1].wait, functools.partial(product, 0)] + cores[:2]
+    sequence += [functools.partial(product, t) for t in range(1, shards // 2)] + [loads[2].wait, loads[3].wait] + each(out_term)
+    sequence += moves[:1] + nears[:1] + cores[2:3] + each(o_reducer.after_core) + moves[1:3] + nears[1:2] + lasts[:1] + cores[3:] + moves[3:5]
+    sequence += nears[2:3] + lasts[1:2] + moves[5:6] + nears[3:] + lasts[2:3] + [functools.partial(line.ends, i) for i in range(shards // 2, shards - 1)]
+    sequence += each(o_reducer.after_near) + lasts[3:]
     sequence += [functools.partial(ending, o_reducer, o_owners, k, o) for k, o in turn]
-    sequence += moves[:2] + nears[:1] + cores[2:3] + moves[2:4] + nears[1:2] + lasts[:1] + cores[3:] + moves[4:6]
-    for i in range(2, shards):
-        sequence += nears[i : i + 1] + lasts[i - 1 : i] + moves[i + 4 : i + 5]
-    sequence += lasts[-1:] + [line.nearest] + moves[shards + 4 :]
-    sequence += [o_owners.arrive, o_gatherer.start]
+    order = list(reversed(range(shards)))
+    sequence += [functools.partial(begin_from, i) for i in order] + moves[6:7]
+    sequence += [functools.partial(pass_from, i) for i in order[:2]] + moves[7:8] + [o_owners.arrive, o_gatherer.start]
+    sequence += [functools.partial(pass_from, i) for i in order[2:]] + moves[8:] + [functools.partial(pass_last_from, i) for i in order[:2]]
     for step in sequence:
         step()
-    owners.arrive()
-    gatherer.start()
     line.result(total)
 
     part[...] = jnp.zeros_like(part)
@@ -1694,21 +1713,25 @@
         def _():
             small_arrival(o).wait_recv()
             small[...] += part_in[o]
-    sums = [remote(small, part_in.at[shards + i], s_send.at[shards + i], s_recv.at[shards + i], device)
-            for i, device in enumerate((cube.to_core, cube.to_x, cube.to_y))]
-
-    def add_small(i):
-        sums[i].start()
-        sums[i].wait()
-        small[...] += part_in[shards + i]
-
-    add_small(0)
+
+    def sum_copy(o):
+        return remote(small, part_in.at[shards + r], s_send.at[shards + o], s_recv.at[shards + r], {"replica": o})
+
+    def sum_arrival(o):
+        place = part_in.at[shards + o]
+        return remote(place, place, s_send.at[shards + o], s_recv.at[shards + o], {"replica": o})
+
+    for o in others:
+        sum_copy(o).start()
+    part_in[shards + r] = small[...]
     o_gatherer.pass_on()
-    gatherer.pass_on()
-    add_small(1)
-    add_small(2)
+    for o in others:
+        sum_copy(o).wait_send()
+        sum_arrival(o).wait_recv()
+    small[...] = sum([part_in[shards + i] for i in range(1, 8)], part_in[shards])
     o_gatherer.pass_last()
-    gatherer.pass_last()
+    for i in order[2:]:
+        pass_last_from(i)
     for o in range(shards):
         @pl.when(z != o)
         def _():
@@ -1719,8 +1742,8 @@
         o_reducer.finish(k)
     owners.finish()
     o_owners.finish()
-    gatherer.finish()
-    o_gatherer.finish()
+    for g in sum(gatherers, [o_gatherer]):
+        g.finish()
 
 
 def input_back_call(shards, slopes, weight, normed, attended, d_middle_columns, tokens, vectors, d_middle, bias_grad, norm_grads):
@@ -1746,10 +1769,11 @@
         scratch_shapes=[
             pltpu.VMEM(weight.shape, low), pltpu.VMEM(normed.shape, low), pltpu.VMEM(attended.shape, low),
             pltpu.VMEM(d_middle_columns.shape, low), pltpu.VMEM((rows, D), f32),
-            pltpu.VMEM((shards, 8, width), f32), pltpu.VMEM((shards + 3, 8, width), f32),
+            pltpu.VMEM((shards, 8, width), f32), pltpu.VMEM((shards + 8, 8, width), f32),
         ] + line_scratch(shards, rows, D, 3) + reducer_scratch(shards, share, 3 * width) + reducer_scratch(shards, share, width)
-        + [pltpu.VMEM((share, 3 * D), low), pltpu.VMEM((share, D), low), dma((shards + 3,)), dma((shards + 3,)), dma((4,))]
-        + owner_sems(shards, 3) + owner_sems(shards, 1) + gatherer_sems() * 2,
+        + [pltpu.VMEM((share, 3 * D), low), pltpu.VMEM((share, D), low), dma((shards + 8,)), dma((shards + 8,)), dma((4,))]
+        + owner_sems(shards, 3) + owner_sems(shards, 1)
+        + [dma((3 * shards, 8)), dma((3 * shards, 8)), dma((3 * shards, 1))] + gatherer_sems(),
         compiler_params=pltpu.CompilerParams(collective_id=8, has_side_effects=True, vmem_limit_bytes=60 * 2**20),
         name="input_back",
         cost_estimate=pl.CostEstimate(flops=10**10, bytes_accessed=200 * 10**6, transcendentals=0),

time: 624 us -> 616 us (0.987)
  Pallas kernels: 573 us -> 565 us
    pallas_call x1, Pallas kernels: 118 us -> 111 us  [input_back_call(): pl.pallas_call(functools.partial(input_back_kernel, shards), out_shape=[j...]
where the time goes in v8:
time: 616 us; the launch traced here: 609 us
  Pallas kernels  565 us (92%)
  other arithmetic  33.1 us (5%)
  local copies, waits for them, and re-layouts  7.93 us (1%)
    pallas_call x1, Pallas kernels, input_back_call(): pl.pallas_call(functools.partial(input_back_kernel, shards), out_shape=[j...  111 us
    pallas_call x1, Pallas kernels, hidden_back_call(): pl.pallas_call(functools.partial(hidden_back_kernel, shards), out_shape=[...  106 us
    pallas_call x1, Pallas kernels, start_call(): pl.pallas_call(functools.partial(start_kernel, shards), out_shape=[jax.Sh...  101 us
    pallas_call x1, Pallas kernels, heads_back_call(): pl.pallas_call(functools.partial(heads_back_kernel, shards, rows), out_sh...  95.1 us
    pallas_call x1, Pallas kernels, attend_spread_call(): pl.pallas_call(functools.partial(attend_spread_kernel, shards, rows), out...  86.2 us
    pallas_call x1, Pallas kernels, hidden_call(): pl.pallas_call(functools.partial(hidden_kernel, shards), out_shape=[jax.S...  65 us
    convert_element_type x4, other arithmetic, on_device(): out_dtype = tuple((grad.astype(f32) for grad in grads))  27.7 us

profile of v8, /device:TPU:9, one launch (start us, length us, event | category | flops | bytes accessed | tf_op | source)
XLA Modules:
  0.0 609.0 jit_solution(14157394474483210653)
XLA Ops:
  0.6 1.4 fusion.9
  3.9 1.9 convert_add_fusion.1
  5.9 2.6 fusion
  8.6 0.8 convert_add_fusion
  9.3 0.6 reshape.129.vectors
  9.9 101.3 %start.1 = (bf16[4,192,2048]{2,1,0:T(8,128)(2,1)}, f32[4,8,512]{2,1,0:T(8,128)}, bf16[768,2048]{1,0:T(8,128)(2,1)}, bf16[768,1536]{1,0:T(8,128)(2,1)}, bf16[2048...) custom-call(bf16[192,2048]{1,0:T(8,128)(2,1)} %tokens.3, f32[8,512]{1,0:T(8,128)} %reshape.129.vectors, ...), custom_call_target="tpu_custom_call" | custom-call | flops 4831838208 | bytes 150000000 | tf_op jit(solution)/shard_map/start/pallas_call | solution.py:404
  111.2 0.2 broadcast_in_dim.45.seg_rows
  111.4 0.0 copy-start.1
  111.4 1.8 copy-done
  113.2 86.2 %attend_spread.1 = (bf16[768,2048]{1,0:T(8,128)(2,1)}, f32[768,128]{1,0:T(8,128)S(1)}, bf16[2048,2816]{1,0:T(8,128)(2,1)}) custom-call(bf16[768,1536]{1,0:T(8,128)(2,1)S(1)} %copy-done, s32[768,128]{1,0:T(8,128)S(1)} %broadcast_in_dim.45.seg_rows, s32[8,768]{1,0:T(8,128)S(1)} %broadcast_in_dim.46.seg_columns, bf16[512,11264]{1,0:T(8,128)(2,1)} %gate_up.1), custom_call_target="tpu_custom_call" | custom-call | flops 1000000000 | bytes 150000000 | tf_op jit(solution)/shard_map/attend_spread/pallas_call | solution.py:485
  199.5 0.0 copy-start.3
  199.5 0.7 copy-done.3
  200.2 65.0 %hidden.1 = (f32[192,2048]{1,0:T(8,128)}, bf16[768,2048]{1,0:T(8,128)(2,1)}, bf16[768,1408]{1,0:T(8,128)(2,1)}, bf16[768,2816]{1,0:T(8,128)(2,1)}, bf16[4,192,20...) custom-call(bf16[768,2048]{1,0:T(8,128)(2,1)} %get-tuple-element.42.attended, ...), custom_call_target="tpu_custom_call" | custom-call | flops 24000000000 | bytes 150000000 | tf_op jit(solution)/shard_map/hidden/pallas_call | solution.py:612
  265.2 106.2 %hidden_back.1 = (f32[192,2048]{1,0:T(8,128)}, bf16[176,2048]{1,0:T(8,128)(2,1)}, bf16[64,11264]{1,0:T(8,128)(2,1)}) custom-call(bf16[768,2816]{1,0:T(8,128)(2,1)} %get-tuple-element.47.slopes, bf16[2048,2816]{1,0:T(8,128)(2,1)} %get-tuple-element.45.gate_up_weight.weight, bf16[768,1408]{1,0:T(8,128)(2,1)} %get-tuple-element.48.hidden, ...), custom_call_target="tpu_custom_call" | custom-call | flops 10000000000 | bytes 200000000 | tf_op jit(solution)/shard_map/hidden_back/pallas_call | solution.py:1420
  371.4 95.1 %heads_back.1 = (f32[192,2048]{1,0:T(8,128)}, f32[16,2048]{1,0:T(8,128)}, bf16[768,1536]{1,0:T(8,128)(2,1)}, f32[8,1536]{1,0:T(8,128)}, bf16[192,2048]{1,0:T(8,1...) custom-call(f32[192,2048]{1,0:T(8,128)} %get-tuple-element.51.d_normed_two, ...), custom_call_target="tpu_custom_call" | custom-call | flops 10000000000 | bytes 200000000 | tf_op jit(solution)/shard_map/heads_back/pallas_call | solution.py:1567
  466.5 111.2 %input_back.1 = (f32[192,2048]{1,0:T(8,128)}, f32[8,512]{1,0:T(8,128)}, bf16[512,6144]{1,0:T(8,128)(2,1)}, bf16[512,2048]{1,0:T(8,128)(2,1)}) custom-call(bf16[768,1536]{1,0:T(8,128)(2,1)} %get-tuple-element.58.slopes, bf16[2048,1536]{1,0:T(8,128)(2,1)} %get-tuple-element.59.weight, bf16[768,2048]{1,0:T(8,128)(2,1)} %get-tuple-element.60.normed, ...), custom_call_target="tpu_custom_call" | custom-call | flops 10000000000 | bytes 200000000 | tf_op jit(solution)/shard_map/input_back/pallas_call | solution.py:1759
  577.8 9.4 %convert_element_type.80 = f32[512,6144]{1,0:T(8,128)} convert(bf16[512,6144]{1,0:T(8,128)(2,1)} %get-tuple-element.66) | non-fusion elementwise | flops 3145728 | bytes 18874368 | tf_op jit(solution)/shard_map/convert_element_type | solution.py:2032
  587.1 9.8 %convert_element_type.82 = f32[512,11264]{1,0:T(8,128)} convert(bf16[512,11264]{1,0:T(8,128)(2,1)S(1)} %copy-done.4) | non-fusion elementwise | flops 5767168 | bytes 34603008 | tf_op jit(solution)/shard_map/convert_element_type | solution.py:2032
  597.0 2.5 convert_element_type.81
  599.5 6.0 convert_element_type.83
  605.5 0.6 slice.49
  606.2 0.6 fusion.8
  606.8 0.9 copy.25
  607.6 1.1 copy.26
  (24 shorter events, 0.1 us)
Async XLA Ops:
  111.4 88.1 %copy-start.1 = (s32[768,128]{1,0:T(8,128)}, s32[768,128]{1,0:T(8,128)S(1)}, u32[]{:S(2)}) copy-start(s32[768,128]{1,0:T(8,128)S(1)} %broadcast_in_dim.45.seg_rows) | copy-start | bytes 1179652
  111.4 1.8 copy-start
  113.2 86.2 %copy-start.2 = (s32[8,768]{1,0:T(8,128)}, s32[8,768]{1,0:T(8,128)S(1)}, u32[]{:S(2)}) copy-start(s32[8,768]{1,0:T(8,128)S(1)} %broadcast_in_dim.46.seg_columns) | copy-start | bytes 73732
  199.5 0.7 copy-start.3
  577.8 9.4 %copy-start.4 = (bf16[512,11264]{1,0:T(8,128)(2,1)S(1)}, bf16[512,11264]{1,0:T(8,128)(2,1)}, u32[]{:S(2)}) copy-start(bf16[512,11264]{1,0:T(8,128)(2,1)} %get-tuple-element.69) | copy-start | bytes 34603012
  587.1 12.4 %slice-start = ((s8[5767168]{0:T(1024)(128)(4,1)}), s8[4194304]{0:T(1024)(128)(4,1)S(1)}, s32[]{:S(2)}) async-start(s8[5767168]{0:T(1024)(128)(4,1)} %bitcast.9), calls=%async_computation | async-start | bytes 8388608
  587.1 9.8 %copy-start.5 = (bf16[512,2048]{1,0:T(8,128)(2,1)S(1)}, bf16[512,2048]{1,0:T(8,128)(2,1)}, u32[]{:S(2)}) copy-start(bf16[512,2048]{1,0:T(8,128)(2,1)} %get-tuple-element.68) | copy-start | bytes 6291460
  587.1 12.4 %slice-start.1 = ((s8[5767168]{0:T(1024)(128)(4,1)}), s8[1572864]{0:T(1024)(128)(4,1)S(1)}, s32[]{:S(2)}) async-start(s8[5767168]{0:T(1024)(128)(4,1)} %bitcast.9), calls=%async_computation.1 | async-start | bytes 3145728
  599.5 6.0 copy-start.8
  599.5 7.2 %copy-start.7 = (bf16[192,2048]{1,0:T(8,128)(2,1)S(1)}, bf16[192,2048]{1,0:T(8,128)(2,1)}, u32[]{:S(2)}) copy-start(bf16[192,2048]{1,0:T(8,128)(2,1)} %get-tuple-element.96) | copy-start | bytes 2359300
  599.5 8.1 %copy-start.6 = (f32[192,2048]{1,0:T(8,128)S(1)}, f32[192,2048]{1,0:T(8,128)}, u32[]{:S(2)}) copy-start(f32[192,2048]{1,0:T(8,128)} %get-tuple-element.97) | copy-start | bytes 4718596

commit v9 on v8

--- a/solution.py
+++ b/solution.py
@@ -2,6 +2,7 @@
 
 import jax
 import jax.numpy as jnp
+import numpy as np
 from jax import lax
 from jax.experimental import pallas as pl
 from jax.experimental.pallas import tpu as pltpu
@@ -29,12 +30,6 @@
         segment = segment + passed
         position = position - passed * lengths[i]
     return (segment, position)
-
-
-def rope_tables(position, index):
-    frequency = jnp.exp(-jnp.log(10000.0) * (2.0 * index.astype(jnp.float32) / ROT_DIM))
-    angles = position.astype(jnp.float32)[:, None] * frequency
-    return (jnp.cos(angles), jnp.sin(angles))
 
 
 def contract_last(left, right):
@@ -361,6 +356,12 @@
     for step in range(shards - 1):
         if step > 0:
             line.relay(step, 0)
+        if step == min(1, shards - 2):
+            for o in range(shards):
+                spread_out.pass_on(o)
+        if step == shards - 2:
+            for o in range(shards):
+                spread_out.pass_last(o)
         for way in (0, 1):
             owner = z - step - 1 if way == 0 else z + step + 1
 
@@ -368,11 +369,6 @@
             def _():
                 normalize(owner)
                 project(owner)
-        if step == min(1, shards - 2):
-            for o in range(shards):
-                spread_out.pass_on(o)
-    for o in range(shards):
-        spread_out.pass_last(o)
     spread_out.landed()
     line.finish()
     spread.sent()
@@ -2007,11 +2003,16 @@
     segment, position = group_layout(seq_lengths[0], jnp.arange(group_rows, dtype=jnp.int32))
     seg_rows = jnp.broadcast_to(segment[:, None], (group_rows, 128))
     seg_columns = jnp.broadcast_to(segment[None, :], (8, group_rows))
-    lane = jnp.arange(128, dtype=jnp.int32)[None, :] % HEAD_DIM
-    cosine, sine_value = rope_tables(position, lane % (ROT_DIM // 2))
-    cosine = jnp.where(lane < ROT_DIM, cosine, 1.0)
-    minus = jnp.where(lane < ROT_DIM // 2, -sine_value, 0.0)
-    plus = jnp.where((lane >= ROT_DIM // 2) & (lane < ROT_DIM), sine_value, 0.0)
+    lane = np.arange(128)[None, :] % HEAD_DIM
+    half_rot = ROT_DIM // 2
+    frequency = (10000.0 ** (-2.0 * (lane % half_rot) / ROT_DIM)).astype(np.float32)
+    first = (lane < half_rot).astype(np.float32)
+    second = ((lane >= half_rot) & (lane < ROT_DIM)).astype(np.float32)
+    angles = position.astype(f32)[:, None] * frequency
+    cosine = jnp.cos(angles) * (first + second) + (1.0 - first - second)
+    sine_value = jnp.sin(angles)
+    minus = -sine_value * first
+    plus = sine_value * second
 
     vectors = jnp.zeros((8 * width,), f32)
     at = 0

time: 616 us -> 609 us (0.989)
  Pallas kernels: 565 us -> 558 us
where the time goes in v9:
time: 609 us; the launch traced here: 602 us
  Pallas kernels  558 us (92%)
  other arithmetic  33.8 us (6%)
  local copies, waits for them, and re-layouts  7.93 us (1%)
    pallas_call x1, Pallas kernels, input_back_call(): pl.pallas_call(functools.partial(input_back_kernel, shards), out_shape=[j...  112 us
    pallas_call x1, Pallas kernels, hidden_back_call(): pl.pallas_call(functools.partial(hidden_back_kernel, shards), out_shape=[...  106 us
    pallas_call x1, Pallas kernels, start_call(): pl.pallas_call(functools.partial(start_kernel, shards), out_shape=[jax.Sh...  99.8 us
    pallas_call x1, Pallas kernels, heads_back_call(): pl.pallas_call(functools.partial(heads_back_kernel, shards, rows), out_sh...  97.5 us
    pallas_call x1, Pallas kernels, attend_spread_call(): pl.pallas_call(functools.partial(attend_spread_kernel, shards, rows), out...  83.6 us
    pallas_call x1, Pallas kernels, hidden_call(): pl.pallas_call(functools.partial(hidden_kernel, shards), out_shape=[jax.S...  59.2 us
    convert_element_type x4, other arithmetic, on_device(): out_dtype = tuple((grad.astype(f32) for grad in grads))  27.7 us

profile of v9, /device:TPU:9, one launch (start us, length us, event | category | flops | bytes accessed | tf_op | source)
XLA Modules:
  0.0 602.5 jit_solution(1574514285027813158)
XLA Ops:
  0.6 1.4 fusion.6
  3.9 1.9 convert_add_fusion.1
  5.9 3.4 fusion
  9.2 0.8 convert_add_fusion
  10.0 0.6 reshape.79.vectors
  10.6 99.8 %start.1 = (bf16[4,192,2048]{2,1,0:T(8,128)(2,1)}, f32[4,8,512]{2,1,0:T(8,128)}, bf16[768,2048]{1,0:T(8,128)(2,1)}, bf16[768,1536]{1,0:T(8,128)(2,1)}, bf16[2048...) custom-call(bf16[192,2048]{1,0:T(8,128)(2,1)} %tokens.3, f32[8,512]{1,0:T(8,128)} %reshape.79.vectors, ...), custom_call_target="tpu_custom_call" | custom-call | flops 4831838208 | bytes 150000000 | tf_op jit(solution)/shard_map/start/pallas_call | solution.py:400
  110.4 0.2 broadcast_in_dim.4.seg_rows
  110.5 0.0 copy-start.1
  110.6 1.8 copy-done
  112.4 83.6 %attend_spread.1 = (bf16[768,2048]{1,0:T(8,128)(2,1)}, f32[768,128]{1,0:T(8,128)S(1)}, bf16[2048,2816]{1,0:T(8,128)(2,1)}) custom-call(bf16[768,1536]{1,0:T(8,128)(2,1)S(1)} %copy-done, s32[768,128]{1,0:T(8,128)S(1)} %broadcast_in_dim.4.seg_rows, s32[8,768]{1,0:T(8,128)S(1)} %broadcast_in_dim.5.seg_columns, bf16[512,11264]{1,0:T(8,128)(2,1)} %gate_up.1), custom_call_target="tpu_custom_call" | custom-call | flops 1000000000 | bytes 150000000 | tf_op jit(solution)/shard_map/attend_spread/pallas_call | solution.py:481
  196.0 0.0 copy-start.3
  196.0 0.7 copy-done.3
  196.8 59.2 %hidden.1 = (f32[192,2048]{1,0:T(8,128)}, bf16[768,2048]{1,0:T(8,128)(2,1)}, bf16[768,1408]{1,0:T(8,128)(2,1)}, bf16[768,2816]{1,0:T(8,128)(2,1)}, bf16[4,192,20...) custom-call(bf16[768,2048]{1,0:T(8,128)(2,1)} %get-tuple-element.42.attended, ...), custom_call_target="tpu_custom_call" | custom-call | flops 24000000000 | bytes 150000000 | tf_op jit(solution)/shard_map/hidden/pallas_call | solution.py:608
  256.0 106.1 %hidden_back.1 = (f32[192,2048]{1,0:T(8,128)}, bf16[176,2048]{1,0:T(8,128)(2,1)}, bf16[64,11264]{1,0:T(8,128)(2,1)}) custom-call(bf16[768,2816]{1,0:T(8,128)(2,1)} %get-tuple-element.47.slopes, bf16[2048,2816]{1,0:T(8,128)(2,1)} %get-tuple-element.45.gate_up_weight.weight, bf16[768,1408]{1,0:T(8,128)(2,1)} %get-tuple-element.48.hidden, ...), custom_call_target="tpu_custom_call" | custom-call | flops 10000000000 | bytes 200000000 | tf_op jit(solution)/shard_map/hidden_back/pallas_call | solution.py:1416
  362.1 97.5 %heads_back.1 = (f32[192,2048]{1,0:T(8,128)}, f32[16,2048]{1,0:T(8,128)}, bf16[768,1536]{1,0:T(8,128)(2,1)}, f32[8,1536]{1,0:T(8,128)}, bf16[192,2048]{1,0:T(8,1...) custom-call(f32[192,2048]{1,0:T(8,128)} %get-tuple-element.51.d_normed_two, ...), custom_call_target="tpu_custom_call" | custom-call | flops 10000000000 | bytes 200000000 | tf_op jit(solution)/shard_map/heads_back/pallas_call | solution.py:1563
  459.6 111.6 %input_back.1 = (f32[192,2048]{1,0:T(8,128)}, f32[8,512]{1,0:T(8,128)}, bf16[512,6144]{1,0:T(8,128)(2,1)}, bf16[512,2048]{1,0:T(8,128)(2,1)}) custom-call(bf16[768,1536]{1,0:T(8,128)(2,1)} %get-tuple-element.58.slopes, bf16[2048,1536]{1,0:T(8,128)(2,1)} %get-tuple-element.59.weight, bf16[768,2048]{1,0:T(8,128)(2,1)} %get-tuple-element.60.normed, ...), custom_call_target="tpu_custom_call" | custom-call | flops 10000000000 | bytes 200000000 | tf_op jit(solution)/shard_map/input_back/pallas_call | solution.py:1755
  571.2 9.4 %convert_element_type.71 = f32[512,6144]{1,0:T(8,128)} convert(bf16[512,6144]{1,0:T(8,128)(2,1)} %get-tuple-element.66) | non-fusion elementwise | flops 3145728 | bytes 18874368 | tf_op jit(solution)/shard_map/convert_element_type | solution.py:2033
  580.6 9.8 %convert_element_type.73 = f32[512,11264]{1,0:T(8,128)} convert(bf16[512,11264]{1,0:T(8,128)(2,1)S(1)} %copy-done.4) | non-fusion elementwise | flops 5767168 | bytes 34603008 | tf_op jit(solution)/shard_map/convert_element_type | solution.py:2033
  590.4 2.5 convert_element_type.72
  593.0 6.0 convert_element_type.74
  599.0 0.6 slice.49
  599.6 0.6 fusion.5
  600.2 0.9 copy.30
  601.1 1.1 copy.31
  (21 shorter events, 0.0 us)
Async XLA Ops:
  110.5 85.5 %copy-start.1 = (s32[768,128]{1,0:T(8,128)}, s32[768,128]{1,0:T(8,128)S(1)}, u32[]{:S(2)}) copy-start(s32[768,128]{1,0:T(8,128)S(1)} %broadcast_in_dim.4.seg_rows) | copy-start | bytes 1179652
  110.6 1.8 copy-start
  112.4 83.6 %copy-start.2 = (s32[8,768]{1,0:T(8,128)}, s32[8,768]{1,0:T(8,128)S(1)}, u32[]{:S(2)}) copy-start(s32[8,768]{1,0:T(8,128)S(1)} %broadcast_in_dim.5.seg_columns) | copy-start | bytes 73732
  196.0 0.7 copy-start.3
  571.2 9.4 %copy-start.4 = (bf16[512,11264]{1,0:T(8,128)(2,1)S(1)}, bf16[512,11264]{1,0:T(8,128)(2,1)}, u32[]{:S(2)}) copy-start(bf16[512,11264]{1,0:T(8,128)(2,1)} %get-tuple-element.69) | copy-start | bytes 34603012
  580.6 12.4 %slice-start = ((s8[5767168]{0:T(1024)(128)(4,1)}), s8[4194304]{0:T(1024)(128)(4,1)S(1)}, s32[]{:S(2)}) async-start(s8[5767168]{0:T(1024)(128)(4,1)} %bitcast.9), calls=%async_computation | async-start | bytes 8388608
  580.6 9.8 %copy-start.5 = (bf16[512,2048]{1,0:T(8,128)(2,1)S(1)}, bf16[512,2048]{1,0:T(8,128)(2,1)}, u32[]{:S(2)}) copy-start(bf16[512,2048]{1,0:T(8,128)(2,1)} %get-tuple-element.68) | copy-start | bytes 6291460
  580.6 12.4 %slice-start.1 = ((s8[5767168]{0:T(1024)(128)(4,1)}), s8[1572864]{0:T(1024)(128)(4,1)S(1)}, s32[]{:S(2)}) async-start(s8[5767168]{0:T(1024)(128)(4,1)} %bitcast.9), calls=%async_computation.1 | async-start | bytes 3145728
  593.0 6.0 %copy-start.8 = (f32[8,512]{1,0:T(8,128)S(1)}, f32[8,512]{1,0:T(8,128)}, u32[]{:S(2)}) copy-start(f32[8,512]{1,0:T(8,128)} %get-tuple-element.67) | copy-start | bytes 49156
  593.0 7.2 %copy-start.7 = (bf16[192,2048]{1,0:T(8,128)(2,1)S(1)}, bf16[192,2048]{1,0:T(8,128)(2,1)}, u32[]{:S(2)}) copy-start(bf16[192,2048]{1,0:T(8,128)(2,1)} %get-tuple-element.94) | copy-start | bytes 2359300
  593.0 8.1 %copy-start.6 = (f32[192,2048]{1,0:T(8,128)S(1)}, f32[192,2048]{1,0:T(8,128)}, u32[]{:S(2)}) copy-start(f32[192,2048]{1,0:T(8,128)} %get-tuple-element.95) | copy-start | bytes 4718596
